TPU v7x, 32 devices: a whole 2x2x4 slice. The times are simulated.
32 devices in a mesh: dp: 8 (over z, core), seq: 4 (over y, x).
Axes of the slice: x: 2, y: 2, z: 4, core: 2. Of those that a mesh axis runs over, the one named last changes fastest.
Arguments:
- inputs: float32 [32, 2048, 512], P('dp', 'seq'), may hold values from -6 to 6
- cotangent: float32 [32, 2048, 512], P('dp', 'seq'), may hold values from -6 to 6
- masked: int32 [32, 2048], P('dp', 'seq'), may hold values from 0 to 1, as said below
- proj_seed: int32 [1], replicated, may hold values from 0 to 999999
- gain_attn: float32 [512], P('dp'), may hold values from 0.5 to 1.5
- w_query: float32 [512, 512], P('dp'), may hold values from -0.25 to 0.25
- w_key: float32 [512, 512], P('dp'), may hold values from -0.25 to 0.25
- w_value: float32 [512, 512], P('dp'), may hold values from -0.25 to 0.25
- w_out: float32 [512, 512], P('dp'), may hold values from -6 to 6
- gain_ffn: float32 [512], P('dp'), may hold values from 0.5 to 1.5
- w_up: float32 [512, 2048], P('dp'), may hold values from -0.25 to 0.25
- w_down: float32 [2048, 512], P('dp'), may hold values from -0.125 to 0.125
Outputs:
- outputs: float32 [32, 2048, 512], P('dp', 'seq')
- input_grad: float32 [32, 2048, 512], P('dp', 'seq')
- gain_attn_grad: float32 [512], P('dp')
- w_query_grad: float32 [512, 512], P('dp')
- w_key_grad: float32 [512, 512], P('dp')
- w_value_grad: float32 [512, 512], P('dp')
- w_out_grad: float32 [512, 512], P('dp')
- gain_ffn_grad: float32 [512], P('dp')
- w_up_grad: float32 [512, 2048], P('dp')
- w_down_grad: float32 [2048, 512], P('dp')
Inputs may be any that keep to these rules, and one draw needn't show every extreme that they name: 1 marks a masked residue, whose output gradient counts.
All inputs are finite; a program needn't handle non-finite values.
Results may differ from a plain program's by a relative error of at most 0.025.
Values may be sent and summed in bfloat16 or wider, within the bound.
A program may use at most 256 MiB of HBM per device.

v0:
```python
import math

import jax
import jax.numpy as jnp
from jax import lax
from jax.sharding import PartitionSpec as P

D = 512
HEADS = 8
HEAD_DIM = 64
FEATURES = 256
FF = 2048


epsilon = 1e-05
top_precision = lax.Precision.HIGHEST


def scramble(hashed):
    return jnp.bitwise_xor(hashed, lax.shift_right_logical(hashed, jnp.full_like(hashed, 16)))


def feature_matrix(proj_seed):
    entries = FEATURES * HEAD_DIM
    counter = jnp.arange(2 * entries, dtype=jnp.int32)
    hashed = counter * 1664525 + proj_seed[0] * 22695477 + 1013904223
    hashed = scramble(hashed) * 73244475
    hashed = scramble(hashed) * 73244475
    hashed = scramble(hashed)
    low_bits = jnp.bitwise_and(hashed, 8388607)
    uniform_vals = (low_bits.astype(jnp.float32) + 0.5) * (1.0 / 8388608.0)
    radius = jnp.sqrt(-2.0 * jnp.log(uniform_vals[:entries]))
    normal_vals = radius * jnp.cos(2.0 * math.pi * uniform_vals[entries:])
    return normal_vals.reshape(FEATURES, HEAD_DIM)


def contract(form, left, right):
    return jnp.einsum(form, left, right, preferred_element_type=jnp.float32)


def normalize(values):
    centred = values - jnp.mean(values, axis=-1, keepdims=True)
    scale = lax.rsqrt(jnp.mean(centred * centred, axis=-1, keepdims=True) + epsilon)
    return (centred * scale, scale)


def norm_grad(grad_normed, unit_rows, scale, gain):
    scaled_grad = grad_normed * gain
    first = jnp.mean(scaled_grad, axis=-1, keepdims=True)
    second = jnp.mean(scaled_grad * unit_rows, axis=-1, keepdims=True)
    return scale * (scaled_grad - first - unit_rows * second)


def features(projected, feature_dirs):
    scaled = projected.reshape(projected.shape[0], HEADS, HEAD_DIM) * HEAD_DIM ** (-0.25)
    angles = jnp.einsum("lhd,md->lhm", scaled, feature_dirs, precision=top_precision)
    half_square = 0.5 * jnp.sum(scaled * scaled, axis=-1, keepdims=True)
    return (scaled, jnp.exp(angles - half_square) * FEATURES ** (-0.5))


def feature_grad(grad_feat, feat_vals, scaled, feature_dirs):
    weighted = grad_feat * feat_vals
    grad_scaled = jnp.einsum("lhm,md->lhd", weighted, feature_dirs, precision=top_precision)
    grad_scaled = grad_scaled - jnp.sum(weighted, axis=-1, keepdims=True) * scaled
    return (grad_scaled * HEAD_DIM ** (-0.25)).reshape(scaled.shape[0], HEADS * HEAD_DIM)


def gelu_slope(hidden):
    cumulative = 0.5 * (1.0 + lax.erf(hidden * (1.0 / math.sqrt(2.0))))
    density = jnp.exp(-0.5 * hidden * hidden) * (1.0 / math.sqrt(2.0 * math.pi))
    return cumulative + hidden * density


def micro_step(tokens, upstream, mask_row, gathered, feature_dirs):
    gain_one, w_query, w_key, w_value, w_out, gain_two, w_up, w_down = gathered
    gain_one = gain_one.astype(jnp.float32)
    gain_two = gain_two.astype(jnp.float32)
    row_count = tokens.shape[0]
    unit_one, scale_one = normalize(tokens)
    normed_one = (unit_one * gain_one).astype(jnp.bfloat16)
    queries = contract("ld,de->le", normed_one, w_query)
    key_rows = contract("ld,de->le", normed_one, w_key)
    value_rows = contract("ld,de->le", normed_one, w_value).astype(jnp.bfloat16)
    value_heads = value_rows.reshape(row_count, HEADS, HEAD_DIM)
    query_scaled, query_feat = features(queries, feature_dirs)
    key_scaled, key_feat = features(key_rows, feature_dirs)
    query_low = query_feat.astype(jnp.bfloat16)
    key_low = key_feat.astype(jnp.bfloat16)
    local_summary = contract("lhm,lhe->hme", key_low, value_heads)
    local_totals = jnp.sum(key_low, axis=0, dtype=jnp.float32)
    summary, totals = lax.psum((local_summary, local_totals), "seq")
    summary_low = summary.astype(jnp.bfloat16)
    totals_low = totals.astype(jnp.bfloat16)
    numerator = contract("lhm,hme->lhe", query_low, summary_low)
    denominator = contract("lhm,hm->lh", query_low, totals_low)
    attended = numerator / denominator[:, :, None]
    attended_low = attended.reshape(row_count, D).astype(jnp.bfloat16)
    middle = tokens + contract("ld,de->le", attended_low, w_out)
    unit_two, scale_two = normalize(middle)
    normed_two = (unit_two * gain_two).astype(jnp.bfloat16)
    hidden = contract("ld,df->lf", normed_two, w_up)
    activated = jax.nn.gelu(hidden, approximate=False).astype(jnp.bfloat16)
    output = middle + contract("lf,fd->ld", activated, w_down)
    grad_output = upstream * mask_row[:, None].astype(jnp.float32)
    grad_output_low = grad_output.astype(jnp.bfloat16)
    down_grad = contract("lf,ld->fd", activated, grad_output_low)
    grad_active = contract("ld,fd->lf", grad_output_low, w_down)
    grad_hidden = (grad_active * gelu_slope(hidden)).astype(jnp.bfloat16)
    up_grad = contract("ld,lf->df", normed_two, grad_hidden)
    grad_normed_two = contract("lf,df->ld", grad_hidden, w_up)
    gain_two_grad = jnp.sum(grad_normed_two * unit_two, axis=0)
    grad_middle = grad_output + norm_grad(grad_normed_two, unit_two, scale_two, gain_two)
    grad_middle_low = grad_middle.astype(jnp.bfloat16)
    outproj_grad = contract("ld,le->de", attended_low, grad_middle_low)
    grad_attended = contract("le,de->ld", grad_middle_low, w_out).reshape(
        row_count, HEADS, HEAD_DIM
    )
    grad_numerator = (grad_attended / denominator[:, :, None]).astype(jnp.bfloat16)
    grad_denominator = (-jnp.sum(grad_attended * attended, axis=-1) / denominator).astype(
        jnp.bfloat16
    )
    local_grad_summary = contract("lhm,lhe->hme", query_low, grad_numerator)
    local_grad_totals = contract("lhm,lh->hm", query_low, grad_denominator)
    grad_summary, grad_totals = (
        lax.psum(local_grad_summary.astype(jnp.bfloat16), "seq").astype(jnp.float32),
        lax.psum(local_grad_totals.astype(jnp.bfloat16), "seq").astype(jnp.float32),
    )
    grad_summary_low = grad_summary.astype(jnp.bfloat16)
    grad_totals_low = grad_totals.astype(jnp.bfloat16)
    grad_query_feat = contract("lhe,hme->lhm", grad_numerator, summary_low) + contract(
        "lh,hm->lhm", grad_denominator, totals_low
    )
    grad_key_feat = (
        contract("lhe,hme->lhm", value_heads, grad_summary_low)
        + grad_totals_low.astype(jnp.float32)[None]
    )
    grad_values = (
        contract("lhm,hme->lhe", key_low, grad_summary_low)
        .reshape(row_count, D)
        .astype(jnp.bfloat16)
    )
    grad_queries = feature_grad(grad_query_feat, query_feat, query_scaled, feature_dirs).astype(
        jnp.bfloat16
    )
    grad_keys = feature_grad(grad_key_feat, key_feat, key_scaled, feature_dirs).astype(jnp.bfloat16)
    query_grad = contract("ld,le->de", normed_one, grad_queries)
    key_grad = contract("ld,le->de", normed_one, grad_keys)
    value_grad = contract("ld,le->de", normed_one, grad_values)
    grad_normed_one = contract("le,de->ld", grad_queries, w_query)
    grad_normed_one = grad_normed_one + contract("le,de->ld", grad_keys, w_key)
    grad_normed_one = grad_normed_one + contract("le,de->ld", grad_values, w_value)
    gain_one_grad = jnp.sum(grad_normed_one * unit_one, axis=0)
    grad_tokens = grad_middle + norm_grad(grad_normed_one, unit_one, scale_one, gain_one)
    weight_grads = (
        gain_one_grad,
        query_grad,
        key_grad,
        value_grad,
        outproj_grad,
        gain_two_grad,
        up_grad,
        down_grad,
    )
    return (output, grad_tokens, weight_grads)


def on_device(
    inputs,
    cotangent,
    masked,
    proj_seed,
    gain_attn,
    w_query,
    w_key,
    w_value,
    w_out,
    gain_ffn,
    w_up,
    w_down,
):
    feature_dirs = feature_matrix(proj_seed)
    low_gain_attn = gain_attn.astype(jnp.bfloat16)
    low_query = w_query.astype(jnp.bfloat16)
    low_key = w_key.astype(jnp.bfloat16)
    low_value = w_value.astype(jnp.bfloat16)
    low_out = w_out.astype(jnp.bfloat16)
    low_gain_ffn = gain_ffn.astype(jnp.bfloat16)
    low_up = w_up.astype(jnp.bfloat16)
    low_down = w_down.astype(jnp.bfloat16)
    running = (
        jnp.zeros((D,), jnp.float32),
        jnp.zeros((D, D), jnp.float32),
        jnp.zeros((D, D), jnp.float32),
        jnp.zeros((D, D), jnp.float32),
        jnp.zeros((D, D), jnp.float32),
        jnp.zeros((D,), jnp.float32),
        jnp.zeros((D, FF), jnp.float32),
        jnp.zeros((FF, D), jnp.float32),
    )
    output_rows = []
    grad_rows_list = []
    for micro_index in range(inputs.shape[0]):
        gathered = (
            lax.all_gather(low_gain_attn, "dp", axis=0, tiled=True),
            lax.all_gather(low_query, "dp", axis=0, tiled=True),
            lax.all_gather(low_key, "dp", axis=0, tiled=True),
            lax.all_gather(low_value, "dp", axis=0, tiled=True),
            lax.all_gather(low_out, "dp", axis=0, tiled=True),
            lax.all_gather(low_gain_ffn, "dp", axis=0, tiled=True),
            lax.all_gather(low_up, "dp", axis=0, tiled=True),
            lax.all_gather(low_down, "dp", axis=0, tiled=True),
        )
        output, grad_tokens, weight_grads = micro_step(
            inputs[micro_index], cotangent[micro_index], masked[micro_index], gathered, feature_dirs
        )
        output_rows.append(output)
        grad_rows_list.append(grad_tokens)
        running = tuple(
            (running_sum + addend for running_sum, addend in zip(running, weight_grads))
        )
    summed_rows = (
        lax.psum_scatter(
            running[0].astype(jnp.bfloat16), "dp", scatter_dimension=0, tiled=True
        ).astype(jnp.float32),
        lax.psum_scatter(
            running[1].astype(jnp.bfloat16), "dp", scatter_dimension=0, tiled=True
        ).astype(jnp.float32),
        lax.psum_scatter(
            running[2].astype(jnp.bfloat16), "dp", scatter_dimension=0, tiled=True
        ).astype(jnp.float32),
        lax.psum_scatter(
            running[3].astype(jnp.bfloat16), "dp", scatter_dimension=0, tiled=True
        ).astype(jnp.float32),
        lax.psum_scatter(
            running[4].astype(jnp.bfloat16), "dp", scatter_dimension=0, tiled=True
        ).astype(jnp.float32),
        lax.psum_scatter(
            running[5].astype(jnp.bfloat16), "dp", scatter_dimension=0, tiled=True
        ).astype(jnp.float32),
        lax.psum_scatter(
            running[6].astype(jnp.bfloat16), "dp", scatter_dimension=0, tiled=True
        ).astype(jnp.float32),
        lax.psum_scatter(
            running[7].astype(jnp.bfloat16), "dp", scatter_dimension=0, tiled=True
        ).astype(jnp.float32),
    )
    owned = (
        lax.psum(summed_rows[0].astype(jnp.bfloat16), "seq").astype(jnp.float32),
        lax.psum(summed_rows[1].astype(jnp.bfloat16), "seq").astype(jnp.float32),
        lax.psum(summed_rows[2].astype(jnp.bfloat16), "seq").astype(jnp.float32),
        lax.psum(summed_rows[3].astype(jnp.bfloat16), "seq").astype(jnp.float32),
        lax.psum(summed_rows[4].astype(jnp.bfloat16), "seq").astype(jnp.float32),
        lax.psum(summed_rows[5].astype(jnp.bfloat16), "seq").astype(jnp.float32),
        lax.psum(summed_rows[6].astype(jnp.bfloat16), "seq").astype(jnp.float32),
        lax.psum(summed_rows[7].astype(jnp.bfloat16), "seq").astype(jnp.float32),
    )
    outputs = jnp.stack(output_rows, axis=0)
    input_grad = jnp.stack(grad_rows_list, axis=0)
    return (
        outputs,
        input_grad,
        owned[0],
        owned[1],
        owned[2],
        owned[3],
        owned[4],
        owned[5],
        owned[6],
        owned[7],
    )


def solution(mesh):
    in_specs = (
        P("dp", "seq", None),
        P("dp", "seq", None),
        P("dp", "seq"),
        P(),
        P("dp"),
        P("dp", None),
        P("dp", None),
        P("dp", None),
        P("dp", None),
        P("dp"),
        P("dp", None),
        P("dp", None),
    )
    out_specs = (
        P("dp", "seq", None),
        P("dp", "seq", None),
        P("dp"),
        P("dp", None),
        P("dp", None),
        P("dp", None),
        P("dp", None),
        P("dp"),
        P("dp", None),
        P("dp", None),
    )
    return jax.shard_map(
        on_device, mesh=mesh, in_specs=in_specs, out_specs=out_specs, check_vma=False
    )
```

profile of v0, /device:TPU:0, one launch (start us, length us, event | category | flops | bytes accessed | tf_op | source)
XLA Modules:
  0.0 736.6 jit_solution(413041198162742323)
XLA Ops:
  10.9 3.8 slice_reduce_fusion.3
  17.0 18.8 %all-reduce.6 = (bf16[512]{0:T(512)(128)(2,1)S(1)}, bf16[512]{0:T(512)(128)(2,1)S(1)}) all-reduce(bf16[512]{0:T(512)(128)(2,1)S(1)} %dynamic-update-slice, bf16[512]{0:T(512)(128)(2,1)S(1)} %dynamic-update-slice.1), channel_id=1, replica_groups=mesh['dp'=8,'seq'=4] {'dp'}, use_global_device_ids=true, to_apply=%add | all-reduce | flops 1024 | bytes 4096
  38.5 2.7 copy.143
  42.8 15.7 %all_gather.18 = bf16[512,512]{1,0:T(8,128)(2,1)S(1)} all-gather(bf16[64,512]{1,0:T(8,128)(2,1)S(1)} %convert_element_type.537), channel_id=1, replica_groups=mesh['dp'=8,'seq'=4] {'dp'}, dimensions={0}, use_global_device_ids=true | all-gather | bytes 589824 | tf_op jit(solution)/shard_map/all_gather | solution.py:207
  66.0 17.1 %all_gather.19 = bf16[512,512]{1,0:T(8,128)(2,1)} all-gather(bf16[64,512]{1,0:T(8,128)(2,1)S(1)} %convert_element_type.540), channel_id=1, replica_groups=mesh['dp'=8,'seq'=4] {'dp'}, dimensions={0}, use_global_device_ids=true | all-gather | bytes 589824 | tf_op jit(solution)/shard_map/all_gather | solution.py:205
  85.1 15.8 %all_gather.17 = bf16[512,512]{1,0:T(8,128)(2,1)} all-gather(bf16[64,512]{1,0:T(8,128)(2,1)S(1)} %convert_element_type.533), channel_id=1, replica_groups=mesh['dp'=8,'seq'=4] {'dp'}, dimensions={0}, use_global_device_ids=true | all-gather | bytes 589824 | tf_op jit(solution)/shard_map/all_gather | solution.py:206
  103.0 2.8 multiply_reduce_fusion.21
  114.3 6.0 convert_reduce_fusion
  121.9 5.9 convert_reduce_fusion.1
  129.3 5.9 convert_reduce_fusion.2
  136.7 5.9 convert_reduce_fusion.3
  145.3 79.1 %all-reduce.18 = (bf16[8,256]{1,0:T(8,128)(2,1)S(1)}, bf16[8,256,64]{1,2,0:T(8,128)(2,1)}, bf16[8,256]{1,0:T(8,128)(2,1)S(1)}, bf16[8,256,64]{1,2,0:T(8,128)(2,1...) all-reduce(f32[8,256]{1,0:T(8,128)S(1)} %get-tuple-element.100, ...), channel_id=1, replica_groups=mesh['dp'=8,'seq'=4] {'seq'}, use_global_device_ids=true, to_apply=%region_33.0 | all-reduce | flops 532480 | bytes 3194880 | tf_op jit(solution)/shard_map/psum | solution.py:91
  224.9 7.6 %fusion.71 = (bf16[512,8,256]{2,0,1:T(8,128)(2,1)S(1)}, f32[512,8,256]{2,0,1:T(8,128)}) fusion(f32[512,8]{0,1:T(8,128)S(1)} %broadcast_multiply_fusion.8, f32[256,64,1]{0,1,2:T(8,128)S(1)} %fusion.215, f32[512,8,64]{0,2,1:T(8,128)} %get-tuple-element.140), kind=kOutput, calls=%fused_computation.135 | convolution fusion | flops 808714240 | bytes 7421952 | tf_op jit(solution)/shard_map/lhd,md->lhm/dot_general | solution.py:56
  233.2 14.8 %all_gather.20 = bf16[512,512]{1,0:T(8,128)(2,1)S(1)} all-gather(bf16[64,512]{1,0:T(8,128)(2,1)S(1)} %convert_element_type.546), channel_id=1, replica_groups=mesh['dp'=8,'seq'=4] {'dp'}, dimensions={0}, use_global_device_ids=true | all-gather | bytes 589824 | tf_op jit(solution)/shard_map/all_gather | solution.py:208
  251.6 6.0 fusion.69
  261.5 5.8 fusion.67
  271.3 6.1 fusion.65
  282.4 2.6 copy.148
  285.1 2.6 copy.147
  291.0 13.1 %fusion.8 = (bf16[512,2048]{1,0:T(8,128)(2,1)}, f32[512,2048]{1,0:T(8,128)}) fusion(bf16[512,2048]{1,0:T(8,128)(2,1)} %all-gather.3.cloned.1.call-done, f32[512,512]{0,1:T(8,128)S(1)} %get-tuple-element.168, f32[512]{0:T(512)S(1)} %add_rsqrt_fusion.2, f32[512]{0:T(512)S(1)} %broadcast_multiply_fusion.34, f32[512]{0:T(512)S(1)} %convert_element_type.548), kind=kOutput, calls=%fused_computation.16 | convolution fusion | flops 1142947840 | bytes 9443328 | tf_op jit(solution)/shard_map/ld,df->lf/dot_general | solution.py:38
  304.1 12.3 %fusion.5 = (bf16[512,2048]{1,0:T(8,128)(2,1)}, f32[512,2048]{1,0:T(8,128)}) fusion(bf16[512,2048]{1,0:T(8,128)(2,1)S(1)} %copy-done.150, f32[512,512]{0,1:T(8,128)S(1)} %copy-done.54, f32[512]{0:T(512)S(1)} %add_rsqrt_fusion.4, f32[512]{0:T(512)S(1)} %broadcast_multiply_fusion.36, f32[512]{0:T(512)S(1)} %convert_element_type.548), kind=kOutput, calls=%fused_computation.13 | convolution fusion | flops 1142947840 | bytes 9443328 | tf_op jit(solution)/shard_map/ld,df->lf/dot_general | solution.py:38
  316.4 11.7 %fusion.2 = (bf16[512,2048]{1,0:T(8,128)(2,1)}, f32[512,2048]{1,0:T(8,128)}) fusion(bf16[512,2048]{1,0:T(8,128)(2,1)S(1)} %copy-done.150, f32[512,512]{0,1:T(8,128)S(1)} %copy-done.57, f32[512]{0:T(512)S(1)} %convert_element_type.548, f32[512]{0:T(512)S(1)} %add_rsqrt_fusion.6, f32[512]{0:T(512)S(1)} %broadcast_multiply_fusion.38), kind=kOutput, calls=%fused_computation.10 | convolution fusion | flops 1142947840 | bytes 9443328 | tf_op jit(solution)/shard_map/ld,df->lf/dot_general | solution.py:38
  328.1 5.0 fusion.29
  346.5 2.6 multiply_reduce_fusion.3
  352.9 3.8 fusion.263
  356.7 11.3 %fusion.11 = (bf16[512,2048]{1,0:T(8,128)(2,1)}, f32[512,2048]{1,0:T(8,128)S(1)}) fusion(bf16[512,2048]{1,0:T(8,128)(2,1)S(1)} %copy-done.151, f32[512,512]{0,1:T(8,128)S(1)} %copy-done.14, f32[512]{0:T(512)S(1)} %add_rsqrt_fusion, f32[512]{0:T(512)S(1)} %broadcast_multiply_fusion.32, f32[512]{0:T(512)S(1)} %convert_element_type.548), kind=kOutput, calls=%fused_computation.19 | convolution fusion | flops 1142947840 | bytes 9443328 | tf_op jit(solution)/shard_map/ld,df->lf/dot_general | solution.py:38
  368.1 2.8 fusion.35
  383.3 4.4 fusion.267
  387.9 3.4 fusion.265
  391.4 3.6 fusion.269
  395.0 4.2 fusion.95
  400.0 4.2 fusion.91
  404.3 4.2 fusion.93
  408.5 5.2 fusion.89
  416.1 14.5 %all-reduce.8 = (bf16[8,256]{1,0:T(8,128)(2,1)S(1)}, bf16[8,256]{1,0:T(8,128)(2,1)S(1)}, bf16[8,256]{1,0:T(8,128)(2,1)S(1)}, bf16[8,256]{1,0:T(8,128)(2,1)S(1)}) all-reduce(bf16[8,256]{1,0:T(8,128)(2,1)S(1)} %bitcast.591, bf16[8,256]{1,0:T(8,128)(2,1)S(1)} %bitcast.592, ...), channel_id=1, replica_groups=mesh['dp'=8,'seq'=4] {'seq'}, use_global_device_ids=true, to_apply=%region_68.0 | all-reduce | flops 8192 | bytes 32768 | tf_op jit(solution)/shard_map/psum | solution.py:126
  430.7 2.8 fusion.96
  435.7 2.5 convolution_add_fusion.9
  438.3 2.7 fusion.99
  441.1 5.1 fusion.246
  446.1 4.7 fusion.242
  450.9 15.2 %all-reduce.17.cloned.1.call-done = (bf16[8,256,64]{1,2,0:T(8,128)(2,1)}, bf16[8,256,64]{1,2,0:T(8,128)(2,1)}, bf16[8,256,64]{1,2,0:T(8,128)(2,1)}, bf16[8,256,64]{1,2,0:T(8,128)(2,1)}) async-done(((bf16[8,256,64]{1,2,0:T(8,128)(2,1)}, bf16[8,256,64]{1,2,0:T(8,128)(2,1)}, bf16[8,256,64]{1,2,0:T(8,128)(2,1)}, bf16[8,256,64]{1,2,0:T(8,128)(2,1)}), (bf16[8,256,64]{1,2,0:T(8,128)(2,1)}, ...) | async-done | bytes 1048592 | tf_op jit(solution)/shard_map/psum | solution.py:125
  466.1 2.5 convolution_convert_fusion.5
  468.6 4.2 fusion.264
  477.7 2.6 fusion.270
  480.4 4.2 fusion.94
  485.1 4.2 fusion.90
  489.3 4.2 fusion.92
  493.5 4.4 fusion.88
  500.4 3.2 convolution_convert_fusion.6
  503.7 3.2 convolution_convert_fusion.7
  514.0 3.1 fusion.244
  517.5 5.1 add_convert_fusion.1
  522.8 3.7 fusion.84
  531.4 2.5 pad_maximum_fusion
  534.0 5.5 copy.92
  551.1 3.2 add_convert_fusion
  565.0 28.9 %reduce-scatter.11.cloned.1.call-done = bf16[64,512]{1,0:T(8,128)(2,1)} async-done(((bf16[512,512]{1,0:T(8,128)(2,1)}), bf16[64,512]{1,0:T(8,128)(2,1)}) %reduce-scatter.11.cloned.1.call-update) | async-done | bytes 65552 | tf_op jit(solution)/shard_map/reduce_scatter | solution.py:231
  593.9 36.3 %reduce-scatter.15.cloned.1.call-done = bf16[64,2048]{1,0:T(8,128)(2,1)} async-done(((bf16[512,2048]{1,0:T(8,128)(2,1)}), bf16[64,2048]{1,0:T(8,128)(2,1)}) %reduce-scatter.15.cloned.1.call-update) | async-done | bytes 262160 | tf_op jit(solution)/shard_map/reduce_scatter | solution.py:240
  630.2 37.3 %reduce-scatter.17.cloned.1.call-done = bf16[256,512]{1,0:T(8,128)(2,1)} async-done(((bf16[2048,512]{1,0:T(8,128)(2,1)}), bf16[256,512]{1,0:T(8,128)(2,1)}) %reduce-scatter.17.cloned.1.call-update) | async-done | bytes 262160 | tf_op jit(solution)/shard_map/reduce_scatter | solution.py:243
  667.6 2.6 add_bitcast_fusion.1
  672.7 5.3 copy.93
  678.0 14.7 %all-reduce.5 = (bf16[512]{0:T(512)(128)(2,1)S(1)}, bf16[512]{0:T(512)(128)(2,1)S(1)}) all-reduce(bf16[512]{0:T(512)(128)(2,1)S(1)} %add_convert_fusion.3, bf16[512]{0:T(512)(128)(2,1)S(1)} %add_convert_fusion.2), channel_id=2, replica_groups=mesh['dp'=8,'seq'=4] {'dp'}, use_global_device_ids=true, to_apply=%region_76.0.clone | all-reduce | flops 1024 | bytes 4096
  692.9 9.7 %all-reduce.7 = (bf16[64]{0:T(256)(128)(2,1)S(1)}, bf16[64]{0:T(256)(128)(2,1)S(1)}) all-reduce(bf16[64]{0:T(256)(128)(2,1)S(1)} %dynamic-slice.3, bf16[64]{0:T(256)(128)(2,1)S(1)} %dynamic-slice.5), channel_id=1, replica_groups=mesh['dp'=8,'seq'=4] {'seq'}, use_global_device_ids=true, to_apply=%region_77.0 | all-reduce | flops 128 | bytes 512 | tf_op jit(solution)/shard_map/psum | solution.py:248
  703.6 16.1 %all-reduce.15.cloned.1.call-done = (bf16[64,512]{1,0:T(8,128)(2,1)}, bf16[64,512]{1,0:T(8,128)(2,1)}, bf16[64,512]{1,0:T(8,128)(2,1)}, bf16[64,512]{1,0:T(8,128...) async-done(((bf16[64,512]{1,0:T(8,128)(2,1)}, bf16[64,512]{1,0:T(8,128)(2,1)}, bf16[64,512]{1,0:T(8,128)(2,1)}, bf16[64,512]{1,0:T(8,128)(2,1)}, ...) | async-done | bytes 786448 | tf_op jit(solution)/shard_map/psum | solution.py:249
  (688 shorter events, 145.9 us)
Async XLA Ops:
  7.2 283.8 %all-gather.3.cloned.1.call-start = ((), (), s32[]{:S(2)}) async-start(), calls=%async_computation.6 | async-start | bytes 2359296 | tf_op jit(solution)/shard_map/all_gather | solution.py:210
  9.0 319.1 %all-gather.5.cloned.1.call-start = ((), (), s32[]{:S(2)}) async-start(), calls=%async_computation.7 | async-start | bytes 2359296 | tf_op jit(solution)/shard_map/all_gather | solution.py:211
  10.8 455.3 %all-reduce.17.cloned.1.call-start = ((), (), s32[]{:S(2)}) async-start(), calls=%async_computation.15 | async-start | bytes 2097152 | tf_op jit(solution)/shard_map/psum | solution.py:125
  15.1 264.7 %copy-start.4 = (f32[1,512,512]{1,2,0:T(8,128)}, f32[1,512,512]{1,2,0:T(8,128)S(1)}, u32[]{:S(2)}) copy-start(f32[1,512,512]{1,2,0:T(8,128)S(1)} %copy.142) | copy-start | bytes 3145732
  35.7 28.8 %copy-start.165 = (f32[512]{0:T(512)}, f32[512]{0:T(512)S(1)}, u32[]{:S(2)}) copy-start(f32[512]{0:T(512)S(1)} %convert_element_type.530) | copy-start | bytes 6148
  35.8 26.8 %copy-start.189 = (f32[512]{0:T(512)}, f32[512]{0:T(512)S(1)}, u32[]{:S(2)}) copy-start(f32[512]{0:T(512)S(1)} %get-tuple-element.220) | copy-start | bytes 6148
  35.8 28.8 %copy-start.191 = (f32[512]{0:T(512)}, f32[512]{0:T(512)S(1)}, u32[]{:S(2)}) copy-start(f32[512]{0:T(512)S(1)} %get-tuple-element.221) | copy-start | bytes 6148
  36.0 28.6 %copy-start.203 = (f32[512]{0:T(512)}, f32[512]{0:T(512)S(1)}, u32[]{:S(2)}) copy-start(f32[512]{0:T(512)S(1)} %add_rsqrt_fusion.7) | copy-start | bytes 6148
  36.3 213.5 %copy-start = (f32[1,512,512]{1,2,0:T(8,128)}, f32[1,512,512]{1,2,0:T(8,128)S(1)}, u32[]{:S(2)}) copy-start(f32[1,512,512]{1,2,0:T(8,128)S(1)} %copy.145) | copy-start | bytes 3145732
  36.3 26.2 %copy-start.185 = (f32[512]{0:T(512)}, f32[512]{0:T(512)S(1)}, u32[]{:S(2)}) copy-start(f32[512]{0:T(512)S(1)} %get-tuple-element.218) | copy-start | bytes 6148
  36.4 26.2 %copy-start.187 = (f32[512]{0:T(512)}, f32[512]{0:T(512)S(1)}, u32[]{:S(2)}) copy-start(f32[512]{0:T(512)S(1)} %get-tuple-element.219) | copy-start | bytes 6148
  36.6 26.0 %copy-start.199 = (f32[512]{0:T(512)}, f32[512]{0:T(512)S(1)}, u32[]{:S(2)}) copy-start(f32[512]{0:T(512)S(1)} %add_rsqrt_fusion.1) | copy-start | bytes 6148
  38.3 221.7 %copy-start.2 = (f32[1,512,512]{1,2,0:T(8,128)}, f32[1,512,512]{1,2,0:T(8,128)S(1)}, u32[]{:S(2)}) copy-start(f32[1,512,512]{1,2,0:T(8,128)S(1)} %copy.144) | copy-start | bytes 3145732
  38.5 24.0 %copy-start.201 = (f32[512]{0:T(512)}, f32[512]{0:T(512)S(1)}, u32[]{:S(2)}) copy-start(f32[512]{0:T(512)S(1)} %add_rsqrt_fusion.3) | copy-start | bytes 6148
  41.3 19.9 %copy-start.6 = (f32[1,512,512]{1,2,0:T(8,128)S(1)}, f32[1,512,512]{1,2,0:T(8,128)}, u32[]{:S(2)}) copy-start(f32[1,512,512]{1,2,0:T(8,128)} %copy.143) | copy-start | bytes 3145732
  42.8 21.8 %copy-start.205 = (f32[512]{0:T(512)}, f32[512]{0:T(512)S(1)}, u32[]{:S(2)}) copy-start(f32[512]{0:T(512)S(1)} %add_rsqrt_fusion.5) | copy-start | bytes 6148
  62.6 22.5 %copy-start.183 = (f32[64,512]{1,0:T(8,128)S(1)}, f32[64,512]{1,0:T(8,128)}, u32[]{:S(2)}) copy-start(f32[64,512]{1,0:T(8,128)} %param.18) | copy-start | bytes 393220
  107.4 6.9 copy-start.81
  107.9 13.9 %copy-start.83 = (f32[512,8,64]{0,2,1:T(8,128)}, f32[512,8,64]{0,2,1:T(8,128)S(1)}, u32[]{:S(2)}) copy-start(f32[512,8,64]{0,2,1:T(8,128)S(1)} %get-tuple-element.147) | copy-start | bytes 3145732
  109.8 19.4 %copy-start.85 = (f32[512,8,64]{0,2,1:T(8,128)}, f32[512,8,64]{0,2,1:T(8,128)S(1)}, u32[]{:S(2)}) copy-start(f32[512,8,64]{0,2,1:T(8,128)S(1)} %get-tuple-element.150) | copy-start | bytes 3145732
  111.8 24.9 %copy-start.87 = (f32[512,8,64]{0,2,1:T(8,128)}, f32[512,8,64]{0,2,1:T(8,128)S(1)}, u32[]{:S(2)}) copy-start(f32[512,8,64]{0,2,1:T(8,128)S(1)} %get-tuple-element.153) | copy-start | bytes 3145732
  113.2 7.1 copy-start.117
  113.2 111.7 %copy-start.193 = (f32[512,8]{0,1:T(8,128)}, f32[512,8]{0,1:T(8,128)S(1)}, u32[]{:S(2)}) copy-start(f32[512,8]{0,1:T(8,128)S(1)} %broadcast_multiply_fusion.8) | copy-start | bytes 49156
  114.3 157.0 %copy-start.15 = (f32[256,64,1]{0,1,2:T(8,128)}, f32[256,64,1]{0,1,2:T(8,128)S(1)}, u32[]{:S(2)}) copy-start(f32[256,64,1]{0,1,2:T(8,128)S(1)} %fusion.215) | copy-start | bytes 196612
  114.3 7.5 %copy-start.167 = (f32[512,8]{0,1:T(8,128)}, f32[512,8]{0,1:T(8,128)S(1)}, u32[]{:S(2)}) copy-start(f32[512,8]{0,1:T(8,128)S(1)} %broadcast_multiply_fusion.9) | copy-start | bytes 49156
  120.4 7.4 %copy-start.17 = (bf16[512,8,256]{2,0,1:T(8,128)(2,1)}, bf16[512,8,256]{2,0,1:T(8,128)(2,1)S(1)}, u32[]{:S(2)}) copy-start(bf16[512,8,256]{2,0,1:T(8,128)(2,1)S(1)} %get-tuple-element.101) | copy-start | bytes 6291460
  121.9 7.4 %copy-start.173 = (f32[512,8]{0,1:T(8,128)}, f32[512,8]{0,1:T(8,128)S(1)}, u32[]{:S(2)}) copy-start(f32[512,8]{0,1:T(8,128)S(1)} %broadcast_multiply_fusion.11) | copy-start | bytes 49156
  127.7 7.4 %copy-start.21 = (bf16[512,8,256]{2,0,1:T(8,128)(2,1)}, bf16[512,8,256]{2,0,1:T(8,128)(2,1)S(1)}, u32[]{:S(2)}) copy-start(bf16[512,8,256]{2,0,1:T(8,128)(2,1)S(1)} %get-tuple-element.99) | copy-start | bytes 6291460
  129.2 7.4 %copy-start.171 = (f32[512,8]{0,1:T(8,128)}, f32[512,8]{0,1:T(8,128)S(1)}, u32[]{:S(2)}) copy-start(f32[512,8]{0,1:T(8,128)S(1)} %broadcast_multiply_fusion.13) | copy-start | bytes 49156
  135.2 7.4 %copy-start.19 = (bf16[512,8,256]{2,0,1:T(8,128)(2,1)}, bf16[512,8,256]{2,0,1:T(8,128)(2,1)S(1)}, u32[]{:S(2)}) copy-start(bf16[512,8,256]{2,0,1:T(8,128)(2,1)S(1)} %get-tuple-element.97) | copy-start | bytes 6291460
  136.7 7.3 copy-start.119
  224.9 8.3 %copy-start.184 = (f32[64,512]{1,0:T(8,128)S(1)}, f32[64,512]{1,0:T(8,128)}, u32[]{:S(2)}) copy-start(f32[64,512]{1,0:T(8,128)} %param.20) | copy-start | bytes 393220
  224.9 23.2 %copy-start.223 = (bf16[8,256,64]{1,2,0:T(8,128)(2,1)S(1)}, bf16[8,256,64]{1,2,0:T(8,128)(2,1)}, u32[]{:S(2)}) copy-start(bf16[8,256,64]{1,2,0:T(8,128)(2,1)} %get-tuple-element.59) | copy-start | bytes 786436
  232.6 17.8 %copy-start.25 = (bf16[512,8,256]{2,0,1:T(8,128)(2,1)}, bf16[512,8,256]{2,0,1:T(8,128)(2,1)S(1)}, u32[]{:S(2)}) copy-start(bf16[512,8,256]{2,0,1:T(8,128)(2,1)S(1)} %get-tuple-element.141) | copy-start | bytes 6291460
  233.2 14.9 %copy-start.175 = (f32[8,1,512]{2,1,0:T(1,128)}, f32[8,1,512]{2,1,0:T(1,128)S(1)}, u32[]{:S(2)}) copy-start(f32[8,1,512]{2,1,0:T(1,128)S(1)} %fusion.226) | copy-start | bytes 49156
  233.2 17.1 %copy-start.207 = (f32[8,1,512]{2,0,1:T(8,128)}, f32[8,1,512]{2,0,1:T(8,128)S(1)}, u32[]{:S(2)}) copy-start(f32[8,1,512]{2,0,1:T(8,128)S(1)} %copy.190) | copy-start | bytes 49156
  248.1 31.7 %copy-start.11 = (bf16[512,512]{1,0:T(8,128)(2,1)}, bf16[512,512]{1,0:T(8,128)(2,1)S(1)}, u32[]{:S(2)}) copy-start(bf16[512,512]{1,0:T(8,128)(2,1)S(1)} %all_gather.20) | copy-start | bytes 1572868
  251.6 6.6 copy-start.228
  260.5 88.6 %copy-start.50 = (f32[512,512]{0,1:T(8,128)}, f32[512,512]{0,1:T(8,128)S(1)}, u32[]{:S(2)}) copy-start(f32[512,512]{0,1:T(8,128)S(1)} %get-tuple-element.168) | copy-start | bytes 3145732
  260.7 6.6 copy-start.195
  261.5 6.5 copy-start.227
  270.5 6.9 copy-start.197
  271.3 6.8 copy-start.225
  290.9 13.1 %copy-start.54 = (f32[512,512]{0,1:T(8,128)S(1)}, f32[512,512]{0,1:T(8,128)}, u32[]{:S(2)}) copy-start(f32[512,512]{0,1:T(8,128)} %copy-done.53) | copy-start | bytes 3145732
  291.0 13.1 %copy-start.150 = (bf16[512,2048]{1,0:T(8,128)(2,1)S(1)}, bf16[512,2048]{1,0:T(8,128)(2,1)}, u32[]{:S(2)}) copy-start(bf16[512,2048]{1,0:T(8,128)(2,1)} %all-gather.3.cloned.1.call-done) | copy-start | bytes 6291460
  304.1 12.3 %copy-start.57 = (f32[512,512]{0,1:T(8,128)S(1)}, f32[512,512]{0,1:T(8,128)}, u32[]{:S(2)}) copy-start(f32[512,512]{0,1:T(8,128)} %copy-done.56) | copy-start | bytes 3145732
  356.7 11.3 %copy-start.70 = (f32[1,512,512]{1,2,0:T(8,128)S(1)}, f32[1,512,512]{1,2,0:T(8,128)}, u32[]{:S(2)}) copy-start(f32[1,512,512]{1,2,0:T(8,128)} %copy.149) | copy-start | bytes 3145732
  372.8 6.5 copy-start.66
  404.2 9.9 %copy-start.102 = (bf16[512,8,64]{0,2,1:T(8,128)(2,1)}, bf16[512,8,64]{0,2,1:T(8,128)(2,1)S(1)}, u32[]{:S(2)}) copy-start(bf16[512,8,64]{0,2,1:T(8,128)(2,1)S(1)} %fusion.91) | copy-start | bytes 1572868
  415.7 149.3 %reduce-scatter.7.cloned.1.call-start = ((), (), s32[]{:S(2)}) async-start(), calls=%async_computation.8 | async-start | bytes 589824 | tf_op jit(solution)/shard_map/reduce_scatter | solution.py:225
  416.1 19.6 %copy-start.46 = (f32[512,512]{0,1:T(8,128)S(1)}, f32[512,512]{0,1:T(8,128)}, u32[]{:S(2)}) copy-start(f32[512,512]{0,1:T(8,128)} %copy-done.45) | copy-start | bytes 3145732
  438.3 126.7 %reduce-scatter.13.cloned.1.call-start = ((), (), s32[]{:S(2)}) async-start(), calls=%async_computation.11 | async-start | bytes 589824 | tf_op jit(solution)/shard_map/reduce_scatter | solution.py:234
  446.1 20.0 %copy-start.22 = (bf16[512,8,256]{2,0,1:T(8,128)(2,1)S(1)}, bf16[512,8,256]{2,0,1:T(8,128)(2,1)}, u32[]{:S(2)}) copy-start(bf16[512,8,256]{2,0,1:T(8,128)(2,1)} %copy-done.21) | copy-start | bytes 6291460
  446.1 22.5 %copy-start.174 = (f32[512,8]{0,1:T(8,128)S(1)}, f32[512,8]{0,1:T(8,128)}, u32[]{:S(2)}) copy-start(f32[512,8]{0,1:T(8,128)} %copy-done.173) | copy-start | bytes 49156
  450.8 114.1 %reduce-scatter.9.cloned.1.call-start = ((), (), s32[]{:S(2)}) async-start(), calls=%async_computation.9 | async-start | bytes 589824 | tf_op jit(solution)/shard_map/reduce_scatter | solution.py:228
  484.6 8.9 %copy-start.106 = (bf16[512,8,64]{0,2,1:T(8,128)(2,1)}, bf16[512,8,64]{0,2,1:T(8,128)(2,1)S(1)}, u32[]{:S(2)}) copy-start(bf16[512,8,64]{0,2,1:T(8,128)(2,1)S(1)} %fusion.94) | copy-start | bytes 1572868
  489.3 9.1 %copy-start.111 = (bf16[512,8,64]{0,2,1:T(8,128)(2,1)}, bf16[512,8,64]{0,2,1:T(8,128)(2,1)S(1)}, u32[]{:S(2)}) copy-start(bf16[512,8,64]{0,2,1:T(8,128)(2,1)S(1)} %fusion.90) | copy-start | bytes 1572868
  499.1 7.8 %copy-start.18 = (bf16[512,8,256]{2,0,1:T(8,128)(2,1)S(1)}, bf16[512,8,256]{2,0,1:T(8,128)(2,1)}, u32[]{:S(2)}) copy-start(bf16[512,8,256]{2,0,1:T(8,128)(2,1)} %copy-done.17) | copy-start | bytes 6291460
  508.5 85.4 %reduce-scatter.11.cloned.1.call-start = ((), (), s32[]{:S(2)}) async-start(), calls=%async_computation.10 | async-start | bytes 589824 | tf_op jit(solution)/shard_map/reduce_scatter | solution.py:231
  514.0 116.3 %reduce-scatter.15.cloned.1.call-start = ((), (), s32[]{:S(2)}) async-start(), calls=%async_computation.12 | async-start | bytes 2359296 | tf_op jit(solution)/shard_map/reduce_scatter | solution.py:240
  522.7 144.9 %reduce-scatter.17.cloned.1.call-start = ((), (), s32[]{:S(2)}) async-start(), calls=%async_computation.13 | async-start | bytes 2359296 | tf_op jit(solution)/shard_map/reduce_scatter | solution.py:243
  534.0 7.0 copy-start.105
  554.3 165.4 %all-reduce.15.cloned.1.call-start = ((), (), s32[]{:S(2)}) async-start(), calls=%async_computation.14 | async-start | bytes 1572864 | tf_op jit(solution)/shard_map/psum | solution.py:249
  562.6 105.0 %copy-start.47 = (f32[512,512]{0,1:T(8,128)S(1)}, f32[512,512]{0,1:T(8,128)}, u32[]{:S(2)}) copy-start(f32[512,512]{0,1:T(8,128)} %copy-done.45) | copy-start | bytes 3145732
  (180 other events, 580.2 us)
Sparse Core Ops, SparseCore 0:
  9.6 31.9 all-gather.2
  43.2 30.5 all-gather.4
  415.8 50.2 all-reduce.16
  468.2 30.9 reduce-scatter.6
  501.4 29.1 reduce-scatter.12
  532.7 29.0 reduce-scatter.8
  564.7 29.1 reduce-scatter.10
  596.2 33.9 reduce-scatter.14
  633.1 34.4 reduce-scatter.16
  671.1 48.5 all-reduce.14
where the time goes:
time: 746 us; the launch traced here: 737 us
  matrix products  296 us (40%)
  blocking collectives  200 us (27%)
  waiting for transfers between devices  134 us (18%)
  local copies, waits for them, and re-layouts  49.2 us (7%)
  other arithmetic  36.3 us (5%)
  between operations  19.6 us (3%)
    dot_general x104, matrix products, contract(): return jnp.einsum(form, left, right, preferred_element_type=jnp.float32)  212 us
    psum x1, blocking collectives, micro_step(): summary, totals = lax.psum((local_summary, local_totals), 'seq')  79.1 us
    dot_general x8, matrix products, features(): jnp.einsum('lhd,md->lhm', scaled, feature_dirs, precision=top_precision)  49.2 us
    unnamed x485, local copies, waits for them, and re-layouts  43.3 us
    reduce_scatter x1, waiting for transfers between devices, on_device(): lax.psum_scatter(running[7].astype(jnp.bfloat16), 'dp', scatter_dimension...  37.3 us
    reduce_scatter x1, waiting for transfers between devices, on_device(): lax.psum_scatter(running[6].astype(jnp.bfloat16), 'dp', scatter_dimension...  36.3 us
    dot_general x8, matrix products, feature_grad(): jnp.einsum('lhm,md->lhd', weighted, feature_dirs, precision=top_precision)  34.7 us
    unnamed x2, blocking collectives  33.5 us
  transfers between devices with their start and end apart: 10, of which 5 were waited for; matrix products, arithmetic and copies ran while one was open for 37% of the time, Pallas kernels for 0%

commit v1 on v0

v1 whole, which is shorter than its diff:
```python
import functools
import math

import jax
import jax.numpy as jnp
from jax import lax
from jax.experimental import pallas as pl
from jax.experimental.pallas import tpu as pltpu
from jax.sharding import PartitionSpec as P

D = 512
HEADS = 8
PAIRS = 4
HEAD_DIM = 64
FEATURES = 256
FF = 2048
CHUNK = 512

epsilon = 1e-05
LOG2E = math.log2(math.e)
LOW = jnp.bfloat16
F32 = jnp.float32


def scramble(hashed):
    return jnp.bitwise_xor(hashed, lax.shift_right_logical(hashed, jnp.full_like(hashed, 16)))


def uniform_entries(counter, seed):
    hashed = counter * 1664525 + seed * 22695477 + 1013904223
    hashed = scramble(hashed) * 73244475
    hashed = scramble(hashed) * 73244475
    hashed = scramble(hashed)
    low_bits = jnp.bitwise_and(hashed, 8388607)
    return (low_bits.astype(F32) + 0.5) * (1.0 / 8388608.0)


def direction_entries(index, seed):
    radius = jnp.sqrt(-2.0 * jnp.log(uniform_entries(index, seed)))
    turn = uniform_entries(index + FEATURES * HEAD_DIM, seed)
    return radius * jnp.cos(2.0 * math.pi * turn)


def dot(left, right):
    return jnp.dot(left, right, preferred_element_type=F32)


def dot_nt(left, right):
    return lax.dot_general(left, right, (((1,), (1,)), ((), ())), preferred_element_type=F32)


def normalize(values):
    centred = values - jnp.mean(values, axis=-1, keepdims=True)
    scale = lax.rsqrt(jnp.mean(centred * centred, axis=-1, keepdims=True) + epsilon)
    return centred * scale, scale


def norm_grad(grad_normed, unit_rows, scale, gain):
    scaled_grad = grad_normed * gain
    first = jnp.mean(scaled_grad, axis=-1, keepdims=True)
    second = jnp.mean(scaled_grad * unit_rows, axis=-1, keepdims=True)
    return scale * (scaled_grad - first - unit_rows * second)


def feature_pair(rows, forms_ref):
    high = rows.astype(LOW)
    rest = (rows - high.astype(F32)).astype(LOW)
    square = (rows * rows * (LOG2E / 16.0) + 1.0 / 16.0).astype(LOW)
    h0, h1 = high[:, :64], high[:, 64:]
    r0, r1 = rest[:, :64], rest[:, 64:]
    s0, s1 = square[:, :64], square[:, 64:]
    left0 = jnp.concatenate([r0, h0, h0, s0], axis=1)
    left1 = jnp.concatenate([h1, r1, s1, h1], axis=1)
    return jnp.exp2(dot(left0, forms_ref[0])), jnp.exp2(dot(left1, forms_ref[1]))


def keys_phase(x, gain_ref, w_kv_ref, forms_ref, n1_ref, k_ref, v_ref, pk_ref, sums_ref):
    unit, _ = normalize(x)
    normed = (unit * gain_ref[...]).astype(LOW)
    n1_ref[...] = normed
    values = dot(normed, w_kv_ref[:, D:]).astype(LOW)
    v_ref[...] = values
    keys = dot(normed, w_kv_ref[:, :D])
    k_ref[...] = keys.astype(LOW)
    ones = jnp.ones((16, x.shape[0]), LOW)
    for pair in range(PAIRS):
        lanes = slice(pair * 128, pair * 128 + 128)
        phi = feature_pair(keys[:, lanes], forms_ref)
        values_t = values[:, lanes].T
        for half in range(2):
            head = 2 * pair + half
            low = phi[half].astype(LOW)
            pk_ref[:, head * 256 : head * 256 + 256] = low
            left = jnp.concatenate([values_t[half * 64 : half * 64 + 64], ones], axis=0)
            got = dot(left, low)
            sums_ref[head * 64 : head * 64 + 64] = got[:64]
            sums_ref[512 + head : 513 + head] = got[64:65]


def spread_sums(sums_ref, spread_ref):
    for head in range(HEADS):
        own, other = (head % 2) * 64, 64 - (head % 2) * 64
        spread_ref[head, own : own + 64] = sums_ref[head * 64 : head * 64 + 64].astype(LOW)
        spread_ref[head, 128 + own : 192 + own] = jnp.broadcast_to(
            sums_ref[512 + head : 513 + head], (64, 256)
        ).astype(LOW)
        spread_ref[head, other : other + 64] = jnp.zeros((64, 256), LOW)
        spread_ref[head, 128 + other : 192 + other] = jnp.zeros((64, 256), LOW)


def middle_phase(
    x, upstream, mask, sums_ref, n1_ref, gain_ref, w_query_ref, w_out_ref, w_up_ref, w_down_ref, forms_ref, back_ref,
    out_ref, dmid_ref, dq_ref, grad_sums_ref, gain_grad_ref, w_out_grad_ref, w_up_grad_ref, w_down_grad_ref,
    spread_ref, pq_ref, q_ref, att_ref, rden_ref, n2_ref, mid_ref, dy_ref, dn2_ref,
):
    spread_sums(sums_ref, spread_ref)
    queries = dot(n1_ref[...], w_query_ref[...])
    q_ref[...] = queries
    for pair in range(PAIRS):
        lanes = slice(pair * 128, pair * 128 + 128)
        phi0, phi1 = feature_pair(queries[:, lanes], forms_ref)
        low0, low1 = phi0.astype(LOW), phi1.astype(LOW)
        pq_ref[:, pair * 512 : pair * 512 + 256] = low0
        pq_ref[:, pair * 512 + 256 : pair * 512 + 512] = low1
        both = dot_nt(low0, spread_ref[2 * pair]) + dot_nt(low1, spread_ref[2 * pair + 1])
        reciprocal = 1.0 / both[:, 128:]
        rden_ref[:, lanes] = reciprocal
        att_ref[:, lanes] = (both[:, :128] * reciprocal).astype(LOW)
    mid = x + dot(att_ref[...], w_out_ref[...])
    unit, scale = normalize(mid)
    gain = gain_ref[...]
    n2 = (unit * gain).astype(LOW)
    n2_ref[...] = n2
    mid_ref[...] = mid
    dy = upstream * mask
    dy_low = dy.astype(LOW)
    dy_ref[...] = dy_low
    n2_t = n2.T
    dy_t = dy_low.T
    out_ref[...] = mid
    for chunk in range(FF // CHUNK):
        cols = slice(chunk * CHUNK, chunk * CHUNK + CHUNK)
        hidden = dot(n2, w_up_ref[:, cols])
        cumulative = 0.5 * (1.0 + lax.erf(hidden * (1.0 / math.sqrt(2.0))))
        density = jnp.exp2(hidden * hidden * (-0.5 * LOG2E)) * (1.0 / math.sqrt(2.0 * math.pi))
        act = (hidden * cumulative).astype(LOW)
        dg = dot_nt(dy_low, w_down_ref[cols])
        du = (dg * (cumulative + hidden * density)).astype(LOW)
        out_ref[...] += dot(act, w_down_ref[cols])
        if chunk == 0:
            dn2_ref[...] = dot_nt(du, w_up_ref[:, cols])
        else:
            dn2_ref[...] += dot_nt(du, w_up_ref[:, cols])
        w_up_grad_ref[:, cols] += dot(n2_t, du)
        w_down_grad_ref[:, cols] += dot(dy_t, act)
    dn2 = dn2_ref[...]
    gain_grad_ref[...] += jnp.sum(dn2 * unit, axis=0, keepdims=True)
    dmid = dy + norm_grad(dn2, unit, scale, gain)
    dmid_ref[...] = dmid
    da = dmid.astype(LOW)
    w_out_grad_ref[...] += dot(att_ref[...].T, da)
    datt = dot_nt(da, w_out_ref[...])
    for pair in range(PAIRS):
        lanes = slice(pair * 128, pair * 128 + 128)
        dnumer = datt[:, lanes] * rden_ref[:, lanes]
        weighted = -dnumer * att_ref[:, lanes].astype(F32)
        left = jnp.concatenate([dnumer.astype(LOW), weighted.astype(LOW)], axis=1)
        left_t = left.T
        parts = []
        for half in range(2):
            head = 2 * pair + half
            own = half * 64
            pq = pq_ref[:, head * 256 : head * 256 + 256]
            dden = jnp.sum(left_t[128 + own : 192 + own].astype(F32), axis=0, keepdims=True)
            rows = jnp.concatenate(
                [left_t[own : own + 64], jnp.broadcast_to(dden, (16, dden.shape[1])).astype(LOW)], axis=0
            )
            got = dot(rows, pq)
            grad_sums_ref[head * 64 : head * 64 + 64] = got[:64]
            grad_sums_ref[512 + head : 513 + head] = got[64:65]
            dpq = dot(left, spread_ref[head])
            parts.append((dpq * pq.astype(F32)).astype(LOW))
        grads = dot(parts[0], back_ref[:256]) + dot(parts[1], back_ref[256:])
        dq_ref[:, lanes] = (grads[:, :128] - grads[:, 128:] * q_ref[:, lanes] * 0.125).astype(LOW)


def spread_grads(sums_ref, spread_ref):
    for head in range(HEADS):
        own, other = (head % 2) * 64, 64 - (head % 2) * 64
        spread_ref[head, own : own + 64] = sums_ref[head * 64 : head * 64 + 64].astype(LOW)
        spread_ref[head, other : other + 64] = jnp.zeros((64, 256), LOW)
        row = lax.broadcasted_iota(jnp.int32, (128, 256), 0)
        totals = jnp.broadcast_to(sums_ref[512 + head : 513 + head], (128, 256)).astype(F32)
        spread_ref[head, 128:] = jnp.where(row == 0, totals, 0.0).astype(LOW)


def last_phase(
    x, dmid, sums_ref, n1_ref, k_ref, v_ref, pk_ref, gain_ref, w_qkv_ref, back_ref,
    input_grad_ref, gain_grad_ref, w_grad_ref, spread_ref, dqkv_ref,
):
    spread_grads(sums_ref, spread_ref)
    ones = jnp.ones((x.shape[0], 128), LOW)
    for pair in range(PAIRS):
        lanes = slice(pair * 128, pair * 128 + 128)
        left = jnp.concatenate([v_ref[:, lanes], ones], axis=1)
        parts = []
        dv = None
        for half in range(2):
            head = 2 * pair + half
            pk = pk_ref[:, head * 256 : head * 256 + 256]
            dpk = dot(left, spread_ref[head])
            parts.append((dpk * pk.astype(F32)).astype(LOW))
            piece = dot_nt(pk, spread_ref[head, :128])
            dv = piece if dv is None else dv + piece
        dqkv_ref[:, D + D + pair * 128 : D + D + pair * 128 + 128] = dv.astype(LOW)
        grads = dot(parts[0], back_ref[:256]) + dot(parts[1], back_ref[256:])
        dqkv_ref[:, D + pair * 128 : D + pair * 128 + 128] = (
            grads[:, :128] - grads[:, 128:] * k_ref[:, lanes].astype(F32) * 0.125
        ).astype(LOW)
    dqkv = dqkv_ref[...]
    n1_t = n1_ref[...].T
    for part in range(3):
        cols = slice(part * D, part * D + D)
        w_grad_ref[:, cols] += dot(n1_t, dqkv_ref[:, cols])
    dn1 = dot_nt(dqkv, w_qkv_ref[...])
    unit, scale = normalize(x)
    gain_grad_ref[...] += jnp.sum(dn1 * unit, axis=0, keepdims=True)
    input_grad_ref[...] = dmid + norm_grad(dn1, unit, scale, gain_ref[...])


def feature_forms(seed):
    col = lax.broadcasted_iota(jnp.int32, (HEAD_DIM, FEATURES), 1)
    row = lax.broadcasted_iota(jnp.int32, (HEAD_DIM, FEATURES), 0)
    dirs_t = direction_entries(col * HEAD_DIM + row, seed) * HEAD_DIM ** (-0.25)
    scaled = dirs_t * LOG2E
    high = scaled.astype(LOW)
    rest = (scaled - high.astype(F32)).astype(LOW)
    minus = jnp.full((HEAD_DIM, FEATURES), -1.0, LOW)
    forms = jnp.stack(
        [jnp.concatenate([high, high, rest, minus], axis=0), jnp.concatenate([high, high, minus, rest], axis=0)]
    )
    back = dirs_t.T.astype(LOW)
    one, zero = jnp.ones_like(back), jnp.zeros_like(back)
    back = jnp.concatenate(
        [jnp.concatenate([back, zero, one, zero], axis=1), jnp.concatenate([zero, back, zero, one], axis=1)], axis=0
    )
    return forms, back


def whole(shape):
    return pl.BlockSpec(shape, lambda i: (0,) * len(shape))


def each(shape):
    return pl.BlockSpec((None,) + shape, lambda i: (i,) + (0,) * len(shape))


def on_device(inputs, cotangent, masked, proj_seed, gain_attn, w_query, w_key, w_value, w_out, gain_ffn, w_up, w_down):
    count, length = inputs.shape[0], inputs.shape[1]
    params = pltpu.CompilerParams(vmem_limit_bytes=60 * 2**20)
    forms, back = feature_forms(proj_seed[0])
    own_rows = gain_attn.shape[0]
    packed = jnp.concatenate(
        [w_query, w_key, w_value, w_out, w_up, w_down.reshape(own_rows, -1)], axis=1
    ).astype(LOW)
    gains = jnp.stack([gain_attn, gain_ffn], axis=1).astype(LOW)
    packed = lax.all_gather(packed, "dp", axis=0, tiled=True)
    gains = lax.all_gather(gains, "dp", axis=0, tiled=True).astype(F32)
    w_qkv, w_o, w_u = packed[:, :1536], packed[:, 1536:2048], packed[:, 2048:4096]
    w_d = packed[:, 4096:].reshape(FF, D)
    w_q = w_qkv[:, :512]
    w_kv = w_qkv[:, 512:]
    gain_one, gain_two = gains[:, 0].reshape(1, D), gains[:, 1].reshape(1, D)
    sd = jax.ShapeDtypeStruct

    def keys_kernel(x_ref, *refs):
        keys_phase(x_ref[...], *refs)

    n1, keys, values, pk, sums = pl.pallas_call(
        keys_kernel,
        grid=(count,),
        in_specs=[each((length, D)), whole((1, D)), whole((D, 2 * D)), whole((2, 256, 256))],
        out_specs=[each((length, D)), each((length, D)), each((length, D)), each((length, 2048)), each((528, 256))],
        out_shape=[
            sd((count, length, D), LOW), sd((count, length, D), LOW), sd((count, length, D), LOW),
            sd((count, length, 2048), LOW), sd((count, 528, 256), F32),
        ],
        compiler_params=params,
        name="keys_phase",
    )(inputs, gain_one, w_kv, forms)
    sums = lax.psum(sums[:, :520].astype(LOW), "seq")

    def middle_kernel(x_ref, up_ref, mask_ref, *refs):
        @pl.when(pl.program_id(0) == 0)
        def _():
            for ref in refs[13:17]:
                ref[...] = jnp.zeros_like(ref)

        middle_phase(x_ref[...], up_ref[...], mask_ref[...].astype(F32), *refs)

    outputs, dmid, dq, grad_sums, gain_two_grad, w_out_grad, w_up_grad, w_down_grad = pl.pallas_call(
        middle_kernel,
        grid=(count,),
        in_specs=[
            each((length, D)), each((length, D)), each((length, 1)), each((520, 256)), each((length, D)), whole((1, D)),
            whole((D, D)), whole((D, D)), whole((D, FF)), whole((FF, D)), whole((2, 256, 256)), whole((512, 256)),
        ],
        out_specs=[
            each((length, D)), each((length, D)), each((length, D)), each((528, 256)),
            whole((1, D)), whole((D, D)), whole((D, FF)), whole((D, FF)),
        ],
        out_shape=[
            sd((count, length, D), F32), sd((count, length, D), F32), sd((count, length, D), LOW), sd((count, 528, 256), F32),
            sd((1, D), F32), sd((D, D), F32), sd((D, FF), F32), sd((D, FF), F32),
        ],
        scratch_shapes=[
            pltpu.VMEM((HEADS, 256, 256), LOW), pltpu.VMEM((length, 2048), LOW), pltpu.VMEM((length, D), F32),
            pltpu.VMEM((length, D), LOW), pltpu.VMEM((length, D), F32), pltpu.VMEM((length, D), LOW),
            pltpu.VMEM((length, D), F32), pltpu.VMEM((length, D), LOW), pltpu.VMEM((length, D), F32),
        ],
        compiler_params=params,
        name="middle_phase",
    )(inputs, cotangent, masked[:, :, None], sums, n1, gain_two, w_q, w_o, w_u, w_d, forms, back)
    grad_sums = lax.psum(grad_sums[:, :520].astype(LOW), "seq")

    def last_kernel(x_ref, dmid_ref, dq_ref, *refs):
        @pl.when(pl.program_id(0) == 0)
        def _():
            for ref in refs[9:11]:
                ref[...] = jnp.zeros_like(ref)

        refs[-1][:, :D] = dq_ref[...]
        last_phase(x_ref[...], dmid_ref[...], *refs)

    input_grad, gain_one_grad, w_qkv_grad = pl.pallas_call(
        last_kernel,
        grid=(count,),
        in_specs=[
            each((length, D)), each((length, D)), each((length, D)), each((520, 256)), each((length, D)), each((length, D)),
            each((length, D)), each((length, 2048)), whole((1, D)), whole((D, 3 * D)), whole((512, 256)),
        ],
        out_specs=[each((length, D)), whole((1, D)), whole((D, 3 * D))],
        out_shape=[sd((count, length, D), F32), sd((1, D), F32), sd((D, 3 * D), F32)],
        scratch_shapes=[pltpu.VMEM((HEADS, 256, 256), LOW), pltpu.VMEM((length, 3 * D), LOW)],
        compiler_params=params,
        name="last_phase",
    )(inputs, dmid, dq, grad_sums, n1, keys, values, pk, gain_one, w_qkv, back)

    n_dp = D // own_rows
    down = w_down_grad.astype(LOW).reshape(D, n_dp, FF // n_dp).transpose(1, 0, 2).reshape(n_dp, -1)
    total = jnp.concatenate(
        [
            w_qkv_grad.astype(LOW).reshape(n_dp, -1),
            w_out_grad.astype(LOW).reshape(n_dp, -1),
            w_up_grad.astype(LOW).reshape(n_dp, -1),
            down,
            jnp.stack([gain_one_grad[0], gain_two_grad[0]], axis=1).astype(LOW).reshape(n_dp, -1),
        ],
        axis=1,
    )
    mine = lax.psum_scatter(total, "dp", scatter_dimension=0, tiled=True)
    mine = lax.psum(mine, "seq").astype(F32).reshape(-1)
    sizes = [own_rows * 1536, own_rows * 512, own_rows * 2048, own_rows * 2048, own_rows * 2]
    pieces, at = [], 0
    for size in sizes:
        pieces.append(mine[at : at + size])
        at += size
    qkv = pieces[0].reshape(own_rows, 1536)
    gains_grad = pieces[4].reshape(own_rows, 2)
    return (
        outputs,
        input_grad,
        gains_grad[:, 0],
        qkv[:, :512],
        qkv[:, 512:1024],
        qkv[:, 1024:],
        pieces[1].reshape(own_rows, 512),
        gains_grad[:, 1],
        pieces[2].reshape(own_rows, 2048),
        pieces[3].reshape(D, FF // n_dp).T,
    )


def solution(mesh):
    in_specs = (
        P("dp", "seq", None),
        P("dp", "seq", None),
        P("dp", "seq"),
        P(),
        P("dp"),
        P("dp", None),
        P("dp", None),
        P("dp", None),
        P("dp", None),
        P("dp"),
        P("dp", None),
        P("dp", None),
    )
    out_specs = (
        P("dp", "seq", None),
        P("dp", "seq", None),
        P("dp"),
        P("dp", None),
        P("dp", None),
        P("dp", None),
        P("dp", None),
        P("dp"),
        P("dp", None),
        P("dp", None),
    )
    return jax.shard_map(on_device, mesh=mesh, in_specs=in_specs, out_specs=out_specs, check_vma=False)
```

time: 746 us -> 522 us (0.70); the launches traced: 737 us -> 521 us
  matrix products: 296 us -> 0 us
  waiting for transfers between devices: 134 us -> 330 us
  blocking collectives: 200 us -> 13.4 us
  Pallas kernels: 0 us -> 90.5 us
  other arithmetic: 36.3 us -> 19.8 us
    dot_general x120 -> x0, matrix products: 296 us -> none  [the longest x104 212 us: contract(): return jnp.einsum(form, left, right, preferred_element_type=jnp.float32)]
    unnamed x10 -> x6, waiting for transfers between devices: 0.16 us -> 136 us
    psum x2 -> x3, waiting for transfers between devices: 31.3 us -> 142 us  [the longest x1 61.1 us: on_device(): mine = lax.psum(mine, 'seq').astype(F32).reshape(-1)]
    psum x3 -> x0, blocking collectives: 103 us -> none  [the longest x1 79.1 us: micro_step(): summary, totals = lax.psum((local_summary, local_totals), 'seq')]
    reduce_scatter x6 -> x0, waiting for transfers between devices: 103 us -> none  [the longest x1 37.3 us: on_device(): lax.psum_scatter(running[7].astype(jnp.bfloat16), 'dp', scatter_dimension...]
    pallas_call x0 -> x3, Pallas kernels: none -> 90.5 us  [the longest x1 57 us: on_device(): pl.pallas_call(middle_kernel, grid=(count,), in_specs=[each((length, D)),...]
    all_gather x2 -> x1, waiting for transfers between devices: 0.02 us -> 51.7 us  [on_device(): packed = lax.all_gather(packed, 'dp', axis=0, tiled=True)]
    all_gather x4 -> x1, blocking collectives: 63.5 us -> 13.4 us  [on_device(): gains = lax.all_gather(gains, 'dp', axis=0, tiled=True).astype(F32)]
  transfers between devices with their start and end apart: 10 -> 5, of which waited for: 5 -> 5; matrix products, arithmetic and copies ran while one was open for 37% -> 5% of each run, Pallas kernels for 0% -> 0%
where the time goes in v1:
time: 522 us; the launch traced here: 521 us
  waiting for transfers between devices  330 us (63%)
  Pallas kernels  90.5 us (17%)
  local copies, waits for them, and re-layouts  51.8 us (10%)
  other arithmetic  19.8 us (4%)
  between operations  14.7 us (3%)
  blocking collectives  13.4 us (3%)
    unnamed x6, waiting for transfers between devices  136 us
    psum x1, waiting for transfers between devices, on_device(): mine = lax.psum(mine, 'seq').astype(F32).reshape(-1)  61.1 us
    pallas_call x1, Pallas kernels, on_device(): pl.pallas_call(middle_kernel, grid=(count,), in_specs=[each((length, D)),...  57 us
    all_gather x1, waiting for transfers between devices, on_device(): packed = lax.all_gather(packed, 'dp', axis=0, tiled=True)  51.7 us
    psum x1, waiting for transfers between devices, on_device(): grad_sums = lax.psum(grad_sums[:, :520].astype(LOW), 'seq')  42 us
    psum x1, waiting for transfers between devices, on_device(): sums = lax.psum(sums[:, :520].astype(LOW), 'seq')  39.4 us
    pallas_call x1, Pallas kernels, on_device(): pl.pallas_call(last_kernel, grid=(count,), in_specs=[each((length, D)), e...  20.7 us
    unnamed x26, local copies, waits for them, and re-layouts  16 us
  transfers between devices with their start and end apart: 5, of which 5 were waited for; matrix products, arithmetic and copies ran while one was open for 5% of the time, Pallas kernels for 0%

profile of v1, /device:TPU:0, one launch (start us, length us, event | category | flops | bytes accessed | tf_op | source)
XLA Modules:
  0.0 521.3 jit_solution(14006614807631198219)
XLA Ops:
  7.3 1.1 convert.48
  8.4 0.2 reshape.73
  8.5 0.9 convert_dynamic-update-slice_fusion.4
  9.5 0.9 convert_dynamic-update-slice_fusion.3
  10.4 0.9 convert_dynamic-update-slice_fusion.2
  11.3 0.9 convert_dynamic-update-slice_fusion.1
  12.3 0.9 copy-done.2
  13.2 0.0 all-reduce.6.cloned.1.call-start
  14.0 13.4 %all-gather = bf16[8,64,2]{1,2,0:T(2,128)(2,1)S(1)} all-gather(bf16[1,64,2]{1,2,0:T(2,128)(2,1)S(1)} %maximum_bitcast_fusion.1), channel_id=1, replica_groups=mesh['dp'=8,'seq'=4] {'dp'}, dimensions={0}, use_global_device_ids=true | all-gather | bytes 2304 | tf_op jit(solution)/shard_map/all_gather | solution.py:268
  27.3 0.1 reshape.87
  27.4 0.3 subtract_convert_fusion
  27.8 0.7 pad_maximum_fusion.refs_2_.refs_7_
  28.5 0.6 slice_bitcast_fusion
  29.1 51.7 %all-gather.3.cloned.1.call-done = bf16[512,6144]{1,0:T(8,128)(2,1)} async-done(((bf16[64,6144]{1,0:T(8,128)(2,1)}), bf16[512,6144]{1,0:T(8,128)(2,1)}) %all-gather.3.cloned.1.call-update) | async-done | bytes 6291472 | tf_op jit(solution)/shard_map/all_gather | solution.py:267
  80.8 2.3 slice.90.refs_1_
  83.1 12.8 %keys_phase.1 = (bf16[4,512,512]{2,1,0:T(8,128)(2,1)}, bf16[4,512,512]{2,1,0:T(8,128)(2,1)}, bf16[4,512,512]{2,1,0:T(8,128)(2,1)}, bf16[4,512,2048]{2,1,0:T(8,128)(2,1)}, f32[4,528,256]{2,1,0:T(8,128)}) custom-call(f32[4,512,512]{2,1,0:T(8,128)} %x_ref.5, f32[1,512]{1,0:T(1,128)} %get-tuple-element.86.refs_0_.refs_5_, bf16[512,1024]{1,0:T(8,128)(2,1)} %slice.90.refs_1_, ...), custom_call_target="tpu_custom_call" | custom-call | tf_op jit(solution)/shard_map/keys_phase/pallas_call | solution.py:279
  95.9 2.7 slice.121
  98.7 0.7 fusion.21
  99.4 1.4 copy.32.mask_ref
  100.8 0.9 maximum_maximum_fusion.refs_8_.refs_7_
  101.7 4.4 fusion.41
  106.1 2.6 reshape.74.refs_6_
  108.6 2.3 fusion.42
  110.9 39.4 %all-reduce.6.cloned.1.call-done.refs_0_ = bf16[4,520,256]{2,1,0:T(8,128)(2,1)} async-done(((bf16[4,520,256]{2,1,0:T(8,128)(2,1)}), bf16[4,520,256]{2,1,0:T(8,128)(2,1)}) %all-reduce.6.cloned.1.call-update) | async-done | bytes 1064976 | tf_op jit(solution)/shard_map/psum | solution.py:291
  150.3 57.0 %middle_phase.1 = (f32[4,512,512]{2,1,0:T(8,128)}, f32[4,512,512]{2,1,0:T(8,128)}, bf16[4,512,512]{2,1,0:T(8,128)(2,1)}, f32[4,528,256]{2,1,0:T(8,128)}, f32[1,5...) custom-call(f32[4,512,512]{2,1,0:T(8,128)} %x_ref.5, f32[4,512,512]{2,1,0:T(8,128)} %up_ref.1, ...), custom_call_target="tpu_custom_call" | custom-call | tf_op jit(solution)/shard_map/middle_phase/pallas_call | solution.py:301
  207.4 2.7 slice.120
  210.1 0.3 all-reduce.12.cloned.1.call-start
  210.3 2.7 slice.98.refs_6_
  213.0 0.1 convert_element_type.61
  213.1 0.2 reshape.76
  213.4 2.5 convert_element_type.62
  215.9 2.3 reshape.77
  218.2 2.5 convert_element_type.63
  220.7 0.7 copy.35
  221.4 42.0 %all-reduce.8.cloned.1.call-done.refs_0_ = bf16[4,520,256]{2,1,0:T(8,128)(2,1)} async-done(((bf16[4,520,256]{2,1,0:T(8,128)(2,1)}), bf16[4,520,256]{2,1,0:T(8,128)(2,1)}) %all-reduce.8.cloned.1.call-update) | async-done | bytes 1064976 | tf_op jit(solution)/shard_map/psum | solution.py:324
  263.3 20.7 %last_phase.1 = (f32[4,512,512]{2,1,0:T(8,128)}, f32[1,512]{1,0:T(1,128)}, f32[512,1536]{1,0:T(8,128)}) custom-call(f32[4,512,512]{2,1,0:T(8,128)} %x_ref.5, f32[4,512,512]{2,1,0:T(8,128)} %get-tuple-element.29.dmid_ref, bf16[4,512,512]{2,1,0:T(8,128)(2,1)} %get-tuple-element.30.dq_ref, bf16[4,520,256]{2,1,0:T(8,128)(2,1)} %all-reduce.8.cloned.1.call-done.refs_0_, ...), custom_call_target="tpu_custom_call" | custom-call | tf_op jit(solution)/shard_map/last_phase/pallas_call | solution.py:335
  284.0 0.7 convert_bitcast_fusion.1
  284.7 0.2 copy.33
  284.9 0.2 convert_element_type.64
  285.1 3.2 convert_element_type.60
  288.3 3.3 reshape.75
  291.6 2.8 constant_dynamic-update-slice_fusion.5
  294.4 0.9 constant_dynamic-update-slice_fusion.4
  295.3 1.5 constant_dynamic-update-slice_fusion.3
  296.7 1.4 constant_dynamic-update-slice_fusion.2
  298.2 0.5 constant_dynamic-update-slice_fusion.1
  298.8 0.3 all-reduce.10.cloned.1.call-start
  299.1 0.3 copy-done.8
  299.4 0.6 dynamic-slice
  300.0 136.1 %all-reduce.12.cloned.1.call-done = bf16[8,393344]{1,0:T(8,128)(2,1)} async-done(((bf16[8,393344]{1,0:T(8,128)(2,1)}), bf16[8,393344]{1,0:T(8,128)(2,1)}) %all-reduce.12.cloned.1.call-update) | async-done | bytes 6293520
  436.0 5.9 %constant_dynamic-slice_fusion = bf16[1,393344]{1,0:T(2,128)(2,1)} fusion(bf16[8,393344]{1,0:T(8,128)(2,1)} %all-reduce.12.cloned.1.call-done, u32[]{:T(128)} %bitcast.13), kind=kLoop, calls=%fused_computation.86 | loop fusion | bytes 1573380
  442.0 61.1 %all-reduce.10.cloned.1.call-done = bf16[1,393344]{1,0:T(2,128)(2,1)} async-done(((bf16[1,393344]{1,0:T(2,128)(2,1)}), bf16[1,393344]{1,0:T(2,128)(2,1)}) %all-reduce.10.cloned.1.call-update) | async-done | bytes 786704 | tf_op jit(solution)/shard_map/psum | solution.py:362
  503.0 3.3 convert_element_type.65
  506.4 0.3 slice_reduce_fusion.3
  506.7 1.0 slice_reduce_fusion.2
  507.7 2.7 slice_reduce_fusion
  510.4 0.1 reshape.80
  510.5 0.7 slice_reduce_fusion.4
  511.2 0.7 reshape.82
  511.9 0.1 reshape.84
  512.1 1.0 copy.34
  513.0 0.1 reshape.81
  513.1 0.8 fusion.43
  513.9 0.9 reshape.83
  (36 shorter events, 0.4 us)
Async XLA Ops:
  7.2 5.1 copy-start.3
  7.2 6.7 %copy-start.6 = (f32[64]{0:T(128)S(1)}, f32[64]{0:T(128)}, u32[]{:S(2)}) copy-start(f32[64]{0:T(128)} %param.21) | copy-start | bytes 772
  7.2 6.7 %copy-start.7 = (f32[64]{0:T(128)S(1)}, f32[64]{0:T(128)}, u32[]{:S(2)}) copy-start(f32[64]{0:T(128)} %param.16) | copy-start | bytes 772
  7.2 73.6 %all-gather.3.cloned.1.call-start = ((), (), s32[]{:S(2)}) async-start(), calls=%async_computation | async-start | bytes 7077888 | tf_op jit(solution)/shard_map/all_gather | solution.py:267
  12.3 0.9 copy-start.2
  13.2 137.1 %all-reduce.6.cloned.1.call-start = ((), (), s32[]{:S(2)}) async-start(), calls=%async_computation.1 | async-start | bytes 2129920 | tf_op jit(solution)/shard_map/psum | solution.py:291
  95.9 3.5 copy-start.4
  98.6 164.7 %all-reduce.8.cloned.1.call-start = ((), (), s32[]{:S(2)}) async-start(), calls=%async_computation.2 | async-start | bytes 2129920 | tf_op jit(solution)/shard_map/psum | solution.py:324
  210.0 3.0 copy-start.1
  210.1 226.0 %all-reduce.12.cloned.1.call-start = ((), (), s32[]{:S(2)}) async-start(), calls=%async_computation.4 | async-start | bytes 12587008
  220.7 0.7 copy-start.5
  291.6 3.7 copy-start
  298.7 0.7 copy-start.8
  298.8 204.3 %all-reduce.10.cloned.1.call-start = ((), (), s32[]{:S(2)}) async-start(), calls=%async_computation.3 | async-start | bytes 3146752 | tf_op jit(solution)/shard_map/psum | solution.py:362
Sparse Core Ops, SparseCore 0:
  13.3 67.4 all-gather.2
  98.7 51.5 all-reduce.5
  210.2 53.0 all-reduce.7
  298.9 137.1 all-reduce.11
  442.1 60.9 all-reduce.9

commit v2 on v1

--- a/solution.py
+++ b/solution.py
@@ -78,7 +78,7 @@
     unit, _ = normalize(x)
     normed = (unit * gain_ref[...]).astype(LOW)
     n1_ref[...] = normed
-    values = dot(normed, w_kv_ref[:, D:]).astype(LOW)
+    values = dot(normed, w_kv_ref[:, D : 2 * D]).astype(LOW)
     v_ref[...] = values
     keys = dot(normed, w_kv_ref[:, :D])
     k_ref[...] = keys.astype(LOW)
@@ -93,17 +93,41 @@
             pk_ref[:, head * 256 : head * 256 + 256] = low
             left = jnp.concatenate([values_t[half * 64 : half * 64 + 64], ones], axis=0)
             got = dot(left, low)
-            sums_ref[head * 64 : head * 64 + 64] = got[:64]
-            sums_ref[512 + head : 513 + head] = got[64:65]
+            put_sums(sums_ref, head, got[:64], got[64:65])
+
+
+def put_sums(sums_ref, head, rows, totals):
+    parts = sums_ref.shape[0]
+    step = HEADS * HEAD_DIM // parts
+    block = min(step, HEAD_DIM)
+    for at in range(0, HEAD_DIM, block):
+        part, row = divmod(head * HEAD_DIM + at, step)
+        sums_ref[part, row : row + block] = rows[at : at + block].astype(LOW)
+    part = head * HEAD_DIM // step
+    row = step + head - -(-part * step // HEAD_DIM)
+    sums_ref[part, row : row + 1] = totals.astype(LOW)
+
+
+def get_sums(sums_ref, head):
+    parts = sums_ref.shape[0]
+    step = HEADS * HEAD_DIM // parts
+    block = min(step, HEAD_DIM)
+    rows = []
+    for at in range(0, HEAD_DIM, block):
+        part, row = divmod(head * HEAD_DIM + at, step)
+        rows.append(sums_ref[part, row : row + block])
+    part = head * HEAD_DIM // step
+    row = step + head - -(-part * step // HEAD_DIM)
+    rows = rows[0] if len(rows) == 1 else jnp.concatenate(rows, axis=0)
+    return rows, sums_ref[part, row : row + 1]
 
 
 def spread_sums(sums_ref, spread_ref):
     for head in range(HEADS):
         own, other = (head % 2) * 64, 64 - (head % 2) * 64
-        spread_ref[head, own : own + 64] = sums_ref[head * 64 : head * 64 + 64].astype(LOW)
-        spread_ref[head, 128 + own : 192 + own] = jnp.broadcast_to(
-            sums_ref[512 + head : 513 + head], (64, 256)
-        ).astype(LOW)
+        rows, totals = get_sums(sums_ref, head)
+        spread_ref[head, own : own + 64] = rows
+        spread_ref[head, 128 + own : 192 + own] = jnp.broadcast_to(totals.astype(F32), (64, 256)).astype(LOW)
         spread_ref[head, other : other + 64] = jnp.zeros((64, 256), LOW)
         spread_ref[head, 128 + other : 192 + other] = jnp.zeros((64, 256), LOW)
 
@@ -152,7 +176,10 @@
         else:
             dn2_ref[...] += dot_nt(du, w_up_ref[:, cols])
         w_up_grad_ref[:, cols] += dot(n2_t, du)
-        w_down_grad_ref[:, cols] += dot(dy_t, act)
+        owners, _, own_cols = w_down_grad_ref.shape
+        for owner in range(chunk * CHUNK // own_cols, (chunk + 1) * CHUNK // own_cols):
+            at = owner * own_cols - chunk * CHUNK
+            w_down_grad_ref[owner] += dot(dy_t, act[:, at : at + own_cols])
     dn2 = dn2_ref[...]
     gain_grad_ref[...] += jnp.sum(dn2 * unit, axis=0, keepdims=True)
     dmid = dy + norm_grad(dn2, unit, scale, gain)
@@ -176,8 +203,7 @@
                 [left_t[own : own + 64], jnp.broadcast_to(dden, (16, dden.shape[1])).astype(LOW)], axis=0
             )
             got = dot(rows, pq)
-            grad_sums_ref[head * 64 : head * 64 + 64] = got[:64]
-            grad_sums_ref[512 + head : 513 + head] = got[64:65]
+            put_sums(grad_sums_ref, head, got[:64], got[64:65])
             dpq = dot(left, spread_ref[head])
             parts.append((dpq * pq.astype(F32)).astype(LOW))
         grads = dot(parts[0], back_ref[:256]) + dot(parts[1], back_ref[256:])
@@ -187,10 +213,11 @@
 def spread_grads(sums_ref, spread_ref):
     for head in range(HEADS):
         own, other = (head % 2) * 64, 64 - (head % 2) * 64
-        spread_ref[head, own : own + 64] = sums_ref[head * 64 : head * 64 + 64].astype(LOW)
+        rows, totals = get_sums(sums_ref, head)
+        spread_ref[head, own : own + 64] = rows
         spread_ref[head, other : other + 64] = jnp.zeros((64, 256), LOW)
         row = lax.broadcasted_iota(jnp.int32, (128, 256), 0)
-        totals = jnp.broadcast_to(sums_ref[512 + head : 513 + head], (128, 256)).astype(F32)
+        totals = jnp.broadcast_to(totals.astype(F32), (128, 256))
         spread_ref[head, 128:] = jnp.where(row == 0, totals, 0.0).astype(LOW)
 
 
@@ -222,10 +249,267 @@
     for part in range(3):
         cols = slice(part * D, part * D + D)
         w_grad_ref[:, cols] += dot(n1_t, dqkv_ref[:, cols])
-    dn1 = dot_nt(dqkv, w_qkv_ref[...])
+    dn1 = dot_nt(dqkv[:, :D], w_qkv_ref[:, 2 * D : 3 * D]) + dot_nt(dqkv[:, D:], w_qkv_ref[:, : 2 * D])
     unit, scale = normalize(x)
     gain_grad_ref[...] += jnp.sum(dn1 * unit, axis=0, keepdims=True)
     input_grad_ref[...] = dmid + norm_grad(dn1, unit, scale, gain_ref[...])
+
+
+MESH = pl.DeviceIdType.MESH
+
+
+class Place:
+    def __init__(self, n_dp, n_seq):
+        self.n_dp, self.n_seq, self.n_z = n_dp, n_seq, n_dp // 2
+        self.dp, self.seq = lax.axis_index("dp"), lax.axis_index("seq")
+        self.z, self.core = self.dp // 2, lax.rem(self.dp, 2)
+
+    def up_z(self, step):
+        return lax.rem(self.z + step, self.n_z)
+
+    def up_seq(self, step):
+        return lax.rem(self.seq + step, self.n_seq)
+
+    def down_z(self, step):
+        return lax.rem(self.z + (self.n_z - step), self.n_z)
+
+    def owner(self, z):
+        return z * 2 + self.core
+
+    def meet(self):
+        barrier = pltpu.get_barrier_semaphore()
+        for step in range(1, self.n_dp):
+            other = lax.rem(self.dp + step, self.n_dp)
+            pl.semaphore_signal(barrier, inc=1, device_id=(other, self.seq), device_id_type=MESH)
+        for step in range(1, self.n_seq):
+            pl.semaphore_signal(barrier, inc=1, device_id=(self.dp, self.up_seq(step)), device_id_type=MESH)
+        pl.semaphore_wait(barrier, self.n_dp - 1 + self.n_seq - 1)
+
+
+def remote(source, target, sems, at, device):
+    return pltpu.make_async_remote_copy(
+        src_ref=source, dst_ref=target, send_sem=sems[0].at[at], recv_sem=sems[1].at[at],
+        device_id=device, device_id_type=MESH,
+    )
+
+
+def semaphores(*shape):
+    return [pltpu.SemaphoreType.DMA(shape), pltpu.SemaphoreType.DMA(shape)]
+
+
+class Gather:
+    def __init__(self, place, ref, first, width, index, z_sems, plane_sems, core_sems):
+        self.place, self.ref, self.first, self.width, self.index = place, ref, first, width, index
+        self.rows = ref.shape[0] // place.n_dp
+        self.across = min(place.n_seq, width // 128)
+        self.along = place.n_seq // self.across
+        self.z_sems, self.plane_sems, self.core_sems = z_sems, plane_sems, core_sems
+
+    def piece(self, owner, part):
+        rows, columns = self.rows // self.along, self.width // self.across
+        top = pl.multiple_of(owner * self.rows + (part // self.across) * rows, rows)
+        left = pl.multiple_of(self.first + lax.rem(part, self.across) * columns, 128)
+        return self.ref.at[pl.ds(top, rows), pl.ds(left, columns)]
+
+    def shard(self, owner):
+        return self.ref.at[
+            pl.ds(pl.multiple_of(owner * self.rows, self.rows), self.rows), pl.ds(self.first, self.width)
+        ]
+
+    def z_copy(self, step):
+        place = self.place
+        piece = self.piece(place.dp, place.seq)
+        return remote(piece, piece, self.z_sems, (self.index, step - 1), (place.owner(place.up_z(step)), place.seq))
+
+    def plane_copy(self, step, to):
+        place = self.place
+        piece = self.piece(place.owner(place.down_z(step)), place.seq)
+        return remote(
+            piece, piece, self.plane_sems, (self.index, step - 1, to - 1), (place.dp, place.up_seq(to))
+        )
+
+    def core_copy(self, step):
+        place = self.place
+        shard = self.shard(place.owner(place.down_z(step)))
+        return remote(shard, shard, self.core_sems, (self.index, step), (place.z * 2 + 1 - place.core, place.seq))
+
+    def start(self):
+        for step in range(1, self.place.n_z):
+            self.z_copy(step).start()
+        self.core_copy(0).start()
+
+    def to_plane(self):
+        for step in range(1, self.place.n_z):
+            self.z_copy(step).wait_recv()
+            for to in range(1, self.place.n_seq):
+                self.plane_copy(step, to).start()
+
+    def to_core(self):
+        for step in range(1, self.place.n_z):
+            for to in range(1, self.place.n_seq):
+                self.plane_copy(step, to).wait_recv()
+            self.core_copy(step).start()
+
+    def finish(self):
+        for step in range(self.place.n_z):
+            self.core_copy(step).wait_recv()
+
+    def drain(self):
+        for step in range(1, self.place.n_z):
+            self.z_copy(step).wait_send()
+            for to in range(1, self.place.n_seq):
+                self.plane_copy(step, to).wait_send()
+        for step in range(self.place.n_z):
+            self.core_copy(step).wait_send()
+
+
+class Sums:
+    def __init__(self, place, local, arrived, full, add_sems, full_sems):
+        self.place, self.local, self.arrived, self.full = place, local, arrived, full
+        self.add_sems, self.full_sems = add_sems, full_sems
+
+    def add_copy(self, slot, index, to):
+        place = self.place
+        other = place.up_seq(to)
+        return remote(
+            self.local.at[slot, other], self.arrived.at[index, to - 1], self.add_sems, (index, to - 1), (place.dp, other)
+        )
+
+    def full_copy(self, index, to):
+        place = self.place
+        mine = self.full.at[index, place.seq]
+        return remote(mine, mine, self.full_sems, (index, to - 1), (place.dp, place.up_seq(to)))
+
+    def start(self, slot, index):
+        for to in range(1, self.place.n_seq):
+            self.add_copy(slot, index, to).start()
+
+    def add(self, slot, index):
+        place = self.place
+        total = self.local[slot, place.seq].astype(F32)
+        for to in range(1, place.n_seq):
+            self.add_copy(slot, index, to).wait_recv()
+            total = total + self.arrived[index, to - 1].astype(F32)
+        self.full[index, place.seq] = total.astype(LOW)
+        for to in range(1, place.n_seq):
+            self.full_copy(index, to).start()
+        for to in range(1, place.n_seq):
+            self.add_copy(slot, index, to).wait_send()
+
+    def finish(self, index):
+        for to in range(1, self.place.n_seq):
+            self.full_copy(index, to).wait_recv()
+
+    def drain(self, index):
+        for to in range(1, self.place.n_seq):
+            self.full_copy(index, to).wait_send()
+
+
+class Scatter:
+    def __init__(self, place, grads, first, width, by_rows, out, arrived, plane, column, final, sems):
+        self.place, self.grads, self.first, self.width, self.by_rows = place, grads, first, width, by_rows
+        self.out, self.arrived, self.plane, self.column, self.final = out, arrived, plane, column, final
+        self.core_sems, self.plane_sems, self.z_sems, self.full_sems = sems
+
+    @staticmethod
+    def shapes(n_dp, n_seq, rows, width, by_rows):
+        part = (rows // n_seq, width) if by_rows else (rows, width // n_seq)
+        n_z = n_dp // 2
+        return [
+            pltpu.VMEM((n_seq, n_z) + part, LOW), pltpu.VMEM((n_seq, n_z) + part, LOW),
+            pltpu.VMEM((n_seq - 1, n_z) + part, LOW), pltpu.VMEM((2 * n_z - 1,) + part, LOW),
+            pltpu.VMEM((n_seq,) + part, LOW),
+            *semaphores(1), *semaphores(n_seq - 1), *semaphores(n_z - 1), *semaphores(n_seq - 1),
+        ]
+
+    @classmethod
+    def of(cls, place, grads, first, width, by_rows, refs):
+        out, arrived, plane, column, final = refs[:5]
+        sems = [refs[at : at + 2] for at in (5, 7, 9, 11)]
+        return cls(place, grads, first, width, by_rows, out, arrived, plane, column, final, sems)
+
+    N_REFS = 13
+
+    def block(self, owner, part):
+        rows, columns = self.out.shape[2:]
+        if self.by_rows:
+            return self.grads[owner, part * rows : part * rows + rows, self.first : self.first + columns]
+        left = self.first + part * columns
+        return self.grads[owner, :, left : left + columns]
+
+    def core_copy(self):
+        place = self.place
+        return remote(self.out, self.arrived, self.core_sems, 0, (place.z * 2 + 1 - place.core, place.seq))
+
+    def plane_copy(self, to):
+        place = self.place
+        other = place.up_seq(to)
+        return remote(self.arrived.at[other], self.plane.at[to - 1], self.plane_sems, to - 1, (place.dp, other))
+
+    def z_copy(self, step):
+        place = self.place
+        other = place.up_z(step)
+        return remote(
+            self.column.at[other], self.column.at[place.n_z + step - 1], self.z_sems, step - 1,
+            (place.owner(other), place.seq),
+        )
+
+    def full_copy(self, to):
+        place = self.place
+        mine = self.final.at[place.seq]
+        return remote(mine, mine, self.full_sems, to - 1, (place.dp, place.up_seq(to)))
+
+    def start(self):
+        place = self.place
+        for part in range(place.n_seq):
+            for z in range(place.n_z):
+                self.out[part, z] = self.block(z * 2 + 1 - place.core, part).astype(LOW)
+        self.core_copy().start()
+
+    def to_plane(self):
+        place = self.place
+        self.core_copy().wait_recv()
+        for part in range(place.n_seq):
+            for z in range(place.n_z):
+                mine = self.block(z * 2 + place.core, part)
+                self.arrived[part, z] = (mine + self.arrived[part, z].astype(F32)).astype(LOW)
+        for to in range(1, place.n_seq):
+            self.plane_copy(to).start()
+
+    def to_z(self):
+        place = self.place
+        for to in range(1, place.n_seq):
+            self.plane_copy(to).wait_recv()
+        for z in range(place.n_z):
+            total = self.arrived[place.seq, z].astype(F32)
+            for to in range(1, place.n_seq):
+                total = total + self.plane[to - 1, z].astype(F32)
+            self.column[z] = total.astype(LOW)
+        for step in range(1, place.n_z):
+            self.z_copy(step).start()
+
+    def to_copies(self):
+        place = self.place
+        total = self.column[place.z].astype(F32)
+        for step in range(1, place.n_z):
+            self.z_copy(step).wait_recv()
+            total = total + self.column[place.n_z + step - 1].astype(F32)
+        self.final[place.seq] = total.astype(LOW)
+        for to in range(1, place.n_seq):
+            self.full_copy(to).start()
+
+    def finish(self):
+        for to in range(1, self.place.n_seq):
+            self.full_copy(to).wait_recv()
+
+    def drain(self):
+        place = self.place
+        self.core_copy().wait_send()
+        for to in range(1, place.n_seq):
+            self.plane_copy(to).wait_send()
+            self.full_copy(to).wait_send()
+        for step in range(1, place.n_z):
+            self.z_copy(step).wait_send()
 
 
 def feature_forms(seed):
@@ -255,129 +539,320 @@
     return pl.BlockSpec((None,) + shape, lambda i: (i,) + (0,) * len(shape))
 
 
-def on_device(inputs, cotangent, masked, proj_seed, gain_attn, w_query, w_key, w_value, w_out, gain_ffn, w_up, w_down):
+def column_cuts(n_seq):
+    width = 2 * D if (2 * D) % (n_seq * 128) == 0 else 4 * D
+    return [(first, width) for first in range(0, 4 * D, width)]
+
+
+def on_device(sizes, inputs, cotangent, masked, proj_seed, gain_attn, w_query, w_key, w_value, w_out, gain_ffn, w_up, w_down):
+    n_dp, n_seq = sizes
     count, length = inputs.shape[0], inputs.shape[1]
-    params = pltpu.CompilerParams(vmem_limit_bytes=60 * 2**20)
+    own = D // n_dp
+    own_ff = FF // n_dp
+    cuts = column_cuts(n_seq)
+    n_items = len(cuts) + 2
+    part_rows = HEADS * HEAD_DIM // n_seq + 16
     forms, back = feature_forms(proj_seed[0])
-    own_rows = gain_attn.shape[0]
-    packed = jnp.concatenate(
-        [w_query, w_key, w_value, w_out, w_up, w_down.reshape(own_rows, -1)], axis=1
-    ).astype(LOW)
-    gains = jnp.stack([gain_attn, gain_ffn], axis=1).astype(LOW)
-    packed = lax.all_gather(packed, "dp", axis=0, tiled=True)
-    gains = lax.all_gather(gains, "dp", axis=0, tiled=True).astype(F32)
-    w_qkv, w_o, w_u = packed[:, :1536], packed[:, 1536:2048], packed[:, 2048:4096]
-    w_d = packed[:, 4096:].reshape(FF, D)
-    w_q = w_qkv[:, :512]
-    w_kv = w_qkv[:, 512:]
-    gain_one, gain_two = gains[:, 0].reshape(1, D), gains[:, 1].reshape(1, D)
+    gains = jnp.pad(jnp.stack([gain_attn, gain_ffn], axis=1).astype(LOW), ((0, 0), (0, 126)))
     sd = jax.ShapeDtypeStruct
-
-    def keys_kernel(x_ref, *refs):
-        keys_phase(x_ref[...], *refs)
-
-    n1, keys, values, pk, sums = pl.pallas_call(
+    vmem = pl.BlockSpec(memory_space=pltpu.VMEM)
+    anywhere = pl.BlockSpec(memory_space=pl.ANY)
+
+    def params(collective_id):
+        return pltpu.CompilerParams(
+            vmem_limit_bytes=60 * 2**20, collective_id=collective_id, has_side_effects=True
+        )
+
+    def keys_kernel(
+        x_hbm, gains_own, wq, wk, wv, wo, wu, wd, forms_ref,
+        w_att, w_up_full, w_down_full, gain_out, k_ref, v_ref, pk_ref, full,
+        x_buf, gain_buf, gain_rows, n1_buf, local, arrived,
+        x_sems, gain_send, gain_recv, z_send, z_recv, plane_send, plane_recv, core_send, core_recv,
+        add_send, add_recv, full_send, full_recv,
+    ):
+        place = Place(n_dp, n_seq)
+        rows = pl.ds(pl.multiple_of(place.dp * own, own), own)
+        for at, ref in enumerate((wk, wv, wq, wo)):
+            w_att[rows, at * D : at * D + D] = ref[...].astype(LOW)
+        w_up_full[rows] = wu[...].astype(LOW)
+        w_down_full[pl.ds(pl.multiple_of(place.dp * own_ff, own_ff), own_ff)] = wd[...].astype(LOW)
+        gain_buf[rows] = gains_own[...]
+
+        def x_copy(index):
+            return pltpu.make_async_copy(x_hbm.at[index], x_buf.at[lax.rem(index, 2)], x_sems.at[lax.rem(index, 2)])
+
+        x_copy(0).start()
+        place.meet()
+        sems = ((z_send, z_recv), (plane_send, plane_recv), (core_send, core_recv))
+        items = [Gather(place, w_att, first, width, at, *sems) for at, (first, width) in enumerate(cuts)]
+        items.append(Gather(place, w_up_full, 0, FF, len(cuts), *sems))
+        items.append(Gather(place, w_down_full, 0, D, len(cuts) + 1, *sems))
+        sums = Sums(place, local, arrived, full, (add_send, add_recv), (full_send, full_recv))
+
+        def gain_copy(step):
+            mine = gain_buf.at[rows]
+            other = lax.rem(place.dp + step, n_dp)
+            return remote(mine, mine, (gain_send, gain_recv), step - 1, (other, place.seq))
+
+        for step in range(1, n_dp):
+            gain_copy(step).start()
+        for item in items:
+            item.start()
+        items[0].to_plane()
+        items[0].to_core()
+        for step in range(1, n_dp):
+            gain_copy(step).wait_recv()
+        gain_rows[...] = gain_buf[...].astype(F32).T[:8]
+        gain_out[...] = gain_rows[...]
+        items[0].finish()
+        for item in items[1:]:
+            item.to_plane()
+
+        def step(index, carry):
+            slot = lax.rem(index, 2)
+
+            @pl.when(index + 1 < count)
+            def _():
+                x_copy(index + 1).start()
+
+            x_copy(index).wait()
+            keys_phase(
+                x_buf[slot], gain_rows.at[0:1], w_att, forms_ref, n1_buf,
+                k_ref.at[index], v_ref.at[index], pk_ref.at[index], local.at[slot],
+            )
+            sums.start(slot, index)
+
+            @pl.when(index > 0)
+            def _():
+                sums.add(1 - slot, index - 1)
+
+            return carry
+
+        lax.fori_loop(0, count, step, 0)
+        sums.add((count - 1) % 2, count - 1)
+        for item in items[1:]:
+            item.to_core()
+        for item in items[1:]:
+            item.finish()
+        for index in range(count):
+            sums.finish(index)
+        for step in range(1, n_dp):
+            gain_copy(step).wait_send()
+        for item in items:
+            item.drain()
+        for index in range(count):
+            sums.drain(index)
+
+    w_att, w_u, w_d, gain_rows, keys, values, pk, sums = pl.pallas_call(
         keys_kernel,
-        grid=(count,),
-        in_specs=[each((length, D)), whole((1, D)), whole((D, 2 * D)), whole((2, 256, 256))],
-        out_specs=[each((length, D)), each((length, D)), each((length, D)), each((length, 2048)), each((528, 256))],
+        in_specs=[anywhere] + [vmem] * 8,
+        out_specs=[vmem] * 8,
         out_shape=[
-            sd((count, length, D), LOW), sd((count, length, D), LOW), sd((count, length, D), LOW),
-            sd((count, length, 2048), LOW), sd((count, 528, 256), F32),
-        ],
-        compiler_params=params,
+            sd((D, 4 * D), LOW), sd((D, FF), LOW), sd((FF, D), LOW), sd((8, D), F32),
+            sd((count, length, D), LOW), sd((count, length, D), LOW), sd((count, length, 2048), LOW),
+            sd((count, n_seq, part_rows, 256), LOW),
+        ],
+        scratch_shapes=[
+            pltpu.VMEM((2, length, D), F32), pltpu.VMEM((D, 128), LOW), pltpu.VMEM((8, D), F32),
+            pltpu.VMEM((length, D), LOW),
+            pltpu.VMEM((2, n_seq, part_rows, 256), LOW), pltpu.VMEM((count, n_seq - 1, part_rows, 256), LOW),
+            pltpu.SemaphoreType.DMA((2,)),
+            *semaphores(n_dp - 1),
+            *semaphores(n_items, n_dp // 2 - 1), *semaphores(n_items, n_dp // 2 - 1, n_seq - 1),
+            *semaphores(n_items, n_dp // 2),
+            *semaphores(count, n_seq - 1), *semaphores(count, n_seq - 1),
+        ],
+        compiler_params=params(0),
         name="keys_phase",
-    )(inputs, gain_one, w_kv, forms)
-    sums = lax.psum(sums[:, :520].astype(LOW), "seq")
-
-    def middle_kernel(x_ref, up_ref, mask_ref, *refs):
+    )(inputs, gains, w_query, w_key, w_value, w_out, w_up, w_down, forms)
+    gain_one, gain_two = gain_rows[0:1], gain_rows[1:2]
+
+    def middle_kernel(x_ref, up_ref, mask_ref, sums_ref, gain_one_ref, *refs):
         @pl.when(pl.program_id(0) == 0)
         def _():
-            for ref in refs[13:17]:
+            for ref in refs[11:15]:
                 ref[...] = jnp.zeros_like(ref)
 
-        middle_phase(x_ref[...], up_ref[...], mask_ref[...].astype(F32), *refs)
+        x = x_ref[...]
+        n1_ref = refs[-1]
+        unit, _ = normalize(x)
+        n1_ref[...] = (unit * gain_one_ref[...]).astype(LOW)
+        middle_phase(x, up_ref[...], mask_ref[...].astype(F32), sums_ref, n1_ref, *refs[:-1])
 
     outputs, dmid, dq, grad_sums, gain_two_grad, w_out_grad, w_up_grad, w_down_grad = pl.pallas_call(
         middle_kernel,
         grid=(count,),
         in_specs=[
-            each((length, D)), each((length, D)), each((length, 1)), each((520, 256)), each((length, D)), whole((1, D)),
-            whole((D, D)), whole((D, D)), whole((D, FF)), whole((FF, D)), whole((2, 256, 256)), whole((512, 256)),
+            each((length, D)), each((length, D)), each((length, 1)), each((n_seq, part_rows, 256)), whole((1, D)),
+            whole((1, D)),
+            pl.BlockSpec((D, D), lambda i: (0, 2)), pl.BlockSpec((D, D), lambda i: (0, 3)), whole((D, FF)),
+            whole((FF, D)), whole((2, 256, 256)), whole((512, 256)),
         ],
         out_specs=[
-            each((length, D)), each((length, D)), each((length, D)), each((528, 256)),
-            whole((1, D)), whole((D, D)), whole((D, FF)), whole((D, FF)),
+            each((length, D)), each((length, D)), each((length, D)), each((n_seq, part_rows, 256)),
+            whole((1, D)), whole((D, D)), whole((D, FF)), whole((n_dp, D, own_ff)),
         ],
         out_shape=[
-            sd((count, length, D), F32), sd((count, length, D), F32), sd((count, length, D), LOW), sd((count, 528, 256), F32),
-            sd((1, D), F32), sd((D, D), F32), sd((D, FF), F32), sd((D, FF), F32),
+            sd((count, length, D), F32), sd((count, length, D), F32), sd((count, length, D), LOW),
+            sd((count, n_seq, part_rows, 256), LOW),
+            sd((1, D), F32), sd((D, D), F32), sd((D, FF), F32), sd((n_dp, D, own_ff), F32),
         ],
         scratch_shapes=[
             pltpu.VMEM((HEADS, 256, 256), LOW), pltpu.VMEM((length, 2048), LOW), pltpu.VMEM((length, D), F32),
             pltpu.VMEM((length, D), LOW), pltpu.VMEM((length, D), F32), pltpu.VMEM((length, D), LOW),
             pltpu.VMEM((length, D), F32), pltpu.VMEM((length, D), LOW), pltpu.VMEM((length, D), F32),
-        ],
-        compiler_params=params,
+            pltpu.VMEM((length, D), LOW),
+        ],
+        compiler_params=pltpu.CompilerParams(vmem_limit_bytes=60 * 2**20),
         name="middle_phase",
-    )(inputs, cotangent, masked[:, :, None], sums, n1, gain_two, w_q, w_o, w_u, w_d, forms, back)
-    grad_sums = lax.psum(grad_sums[:, :520].astype(LOW), "seq")
-
-    def last_kernel(x_ref, dmid_ref, dq_ref, *refs):
+    )(inputs, cotangent, masked[:, :, None], sums, gain_one, gain_two, w_att, w_att, w_u, w_d, forms, back)
+
+    def sums_kernel(local, full, arrived, add_send, add_recv, full_send, full_recv):
+        place = Place(n_dp, n_seq)
+        place.meet()
+        sums = Sums(place, local, arrived, full, (add_send, add_recv), (full_send, full_recv))
+        for index in range(count):
+            sums.start(index, index)
+        for index in range(count):
+            sums.add(index, index)
+        for index in range(count):
+            sums.finish(index)
+        for index in range(count):
+            sums.drain(index)
+
+    grad_sums = pl.pallas_call(
+        sums_kernel,
+        in_specs=[vmem],
+        out_specs=vmem,
+        out_shape=sd((count, n_seq, part_rows, 256), LOW),
+        scratch_shapes=[
+            pltpu.VMEM((count, n_seq - 1, part_rows, 256), LOW),
+            *semaphores(count, n_seq - 1), *semaphores(count, n_seq - 1),
+        ],
+        compiler_params=params(1),
+        name="grad_sums",
+    )(grad_sums)
+
+    def last_kernel(x_ref, dmid_ref, dq_ref, sums_ref, *refs):
         @pl.when(pl.program_id(0) == 0)
         def _():
-            for ref in refs[9:11]:
+            for ref in refs[7:9]:
                 ref[...] = jnp.zeros_like(ref)
 
-        refs[-1][:, :D] = dq_ref[...]
-        last_phase(x_ref[...], dmid_ref[...], *refs)
+        n1_ref = refs[-1]
+        x = x_ref[...]
+        unit, _ = normalize(x)
+        n1_ref[...] = (unit * refs[3][...]).astype(LOW)
+        refs[-2][:, :D] = dq_ref[...]
+        last_phase(x, dmid_ref[...], sums_ref, n1_ref, *refs[:-1])
 
     input_grad, gain_one_grad, w_qkv_grad = pl.pallas_call(
         last_kernel,
         grid=(count,),
         in_specs=[
-            each((length, D)), each((length, D)), each((length, D)), each((520, 256)), each((length, D)), each((length, D)),
-            each((length, D)), each((length, 2048)), whole((1, D)), whole((D, 3 * D)), whole((512, 256)),
+            each((length, D)), each((length, D)), each((length, D)), each((n_seq, part_rows, 256)), each((length, D)),
+            each((length, D)), each((length, 2048)), whole((1, D)), whole((D, 4 * D)), whole((512, 256)),
         ],
         out_specs=[each((length, D)), whole((1, D)), whole((D, 3 * D))],
         out_shape=[sd((count, length, D), F32), sd((1, D), F32), sd((D, 3 * D), F32)],
-        scratch_shapes=[pltpu.VMEM((HEADS, 256, 256), LOW), pltpu.VMEM((length, 3 * D), LOW)],
-        compiler_params=params,
+        scratch_shapes=[
+            pltpu.VMEM((HEADS, 256, 256), LOW), pltpu.VMEM((length, 3 * D), LOW), pltpu.VMEM((length, D), LOW),
+        ],
+        compiler_params=pltpu.CompilerParams(vmem_limit_bytes=60 * 2**20),
         name="last_phase",
-    )(inputs, dmid, dq, grad_sums, n1, keys, values, pk, gain_one, w_qkv, back)
-
-    n_dp = D // own_rows
-    down = w_down_grad.astype(LOW).reshape(D, n_dp, FF // n_dp).transpose(1, 0, 2).reshape(n_dp, -1)
-    total = jnp.concatenate(
-        [
-            w_qkv_grad.astype(LOW).reshape(n_dp, -1),
-            w_out_grad.astype(LOW).reshape(n_dp, -1),
-            w_up_grad.astype(LOW).reshape(n_dp, -1),
-            down,
-            jnp.stack([gain_one_grad[0], gain_two_grad[0]], axis=1).astype(LOW).reshape(n_dp, -1),
-        ],
-        axis=1,
-    )
-    mine = lax.psum_scatter(total, "dp", scatter_dimension=0, tiled=True)
-    mine = lax.psum(mine, "seq").astype(F32).reshape(-1)
-    sizes = [own_rows * 1536, own_rows * 512, own_rows * 2048, own_rows * 2048, own_rows * 2]
-    pieces, at = [], 0
-    for size in sizes:
-        pieces.append(mine[at : at + size])
-        at += size
-    qkv = pieces[0].reshape(own_rows, 1536)
-    gains_grad = pieces[4].reshape(own_rows, 2)
+    )(inputs, dmid, dq, grad_sums, keys, values, pk, gain_one, w_att, back)
+
+    def scatter_kernel(gains_grad, att_grad, up_grad, down_grad, gain_ref, att_ref, up_ref, down_ref, gain_buf, gain_send, gain_recv, *refs):
+        place = Place(n_dp, n_seq)
+        place.meet()
+
+        def gain_plane(step):
+            mine = gain_buf.at[place.seq]
+            return remote(mine, mine, (gain_send, gain_recv), step - 1, (place.dp, place.up_seq(step)))
+
+        def gain_dp(step):
+            mine = gain_buf.at[n_seq + place.dp]
+            other = lax.rem(place.dp + step, n_dp)
+            return remote(mine, mine, (gain_send, gain_recv), n_seq - 2 + step, (other, place.seq))
+
+        gain_buf[place.seq] = gains_grad[...]
+        for step in range(1, n_seq):
+            gain_plane(step).start()
+        specs = [(up_grad, 0, FF, False, up_ref), (down_grad, 0, own_ff, True, down_ref)]
+        specs += [(att_grad, first, width, False, att_ref) for first, width in cuts]
+        items = []
+        for at, spec in enumerate(specs):
+            items.append(Scatter.of(place, *spec[:4], refs[at * Scatter.N_REFS : (at + 1) * Scatter.N_REFS]))
+        for item in items:
+            item.start()
+        for step in range(1, n_seq):
+            gain_plane(step).wait_recv()
+        total = gain_buf[0]
+        for at in range(1, n_seq):
+            total = total + gain_buf[at]
+        gain_buf[n_seq + place.dp] = total
+        for step in range(1, n_dp):
+            gain_dp(step).start()
+        for item in items:
+            item.to_plane()
+        for item in items:
+            item.to_z()
+        for step in range(1, n_dp):
+            gain_dp(step).wait_recv()
+        total = gain_buf[n_seq]
+        for at in range(1, n_dp):
+            total = total + gain_buf[n_seq + at]
+        gain_ref[...] = total
+        for item in items:
+            item.to_copies()
+        for item, spec in zip(items, specs):
+            item.finish()
+            for part in range(n_seq):
+                got = item.final[part].astype(F32)
+                if item.by_rows:
+                    rows = got.shape[0]
+                    spec[4][:, part * rows : part * rows + rows] = got.T
+                else:
+                    left = item.first + part * got.shape[1]
+                    spec[4][:, left : left + got.shape[1]] = got
+        for item in items:
+            item.drain()
+        for step in range(1, n_seq):
+            gain_plane(step).wait_send()
+        for step in range(1, n_dp):
+            gain_dp(step).wait_send()
+
+    att_grad = jnp.concatenate(
+        [w_qkv_grad[:, D : 2 * D], w_qkv_grad[:, 2 * D :], w_qkv_grad[:, :D], w_out_grad], axis=1
+    ).reshape(n_dp, own, 4 * D)
+    gains_grad = jnp.pad(jnp.concatenate([gain_one_grad, gain_two_grad], axis=0), ((0, 6), (0, 0)))
+    scatter_shapes = Scatter.shapes(n_dp, n_seq, own, FF, False) + Scatter.shapes(n_dp, n_seq, D, own_ff, True)
+    for _, width in cuts:
+        scatter_shapes += Scatter.shapes(n_dp, n_seq, own, width, False)
+    gains_grad, att, up, down = pl.pallas_call(
+        scatter_kernel,
+        in_specs=[vmem] * 4,
+        out_specs=[vmem] * 4,
+        out_shape=[sd((8, D), F32), sd((own, 4 * D), F32), sd((own, FF), F32), sd((own_ff, D), F32)],
+        scratch_shapes=[
+            pltpu.VMEM((n_seq + n_dp, 8, D), F32), *semaphores(n_seq + n_dp - 2),
+            *scatter_shapes,
+        ],
+        compiler_params=params(2),
+        name="weight_grads",
+    )(gains_grad, att_grad, w_up_grad.reshape(n_dp, own, FF), w_down_grad)
+    gains_grad = lax.dynamic_slice(gains_grad, (0, lax.axis_index("dp") * own), (2, own))
     return (
         outputs,
         input_grad,
-        gains_grad[:, 0],
-        qkv[:, :512],
-        qkv[:, 512:1024],
-        qkv[:, 1024:],
-        pieces[1].reshape(own_rows, 512),
-        gains_grad[:, 1],
-        pieces[2].reshape(own_rows, 2048),
-        pieces[3].reshape(D, FF // n_dp).T,
+        gains_grad[0],
+        att[:, 2 * D : 3 * D],
+        att[:, :D],
+        att[:, D : 2 * D],
+        att[:, 3 * D :],
+        gains_grad[1],
+        up,
+        down,
     )
 
 
@@ -408,4 +883,5 @@
         P("dp", None),
         P("dp", None),
     )
-    return jax.shard_map(on_device, mesh=mesh, in_specs=in_specs, out_specs=out_specs, check_vma=False)
+    sizes = (mesh.shape["dp"], mesh.shape["seq"])
+    return jax.shard_map(functools.partial(on_device, sizes), mesh=mesh, in_specs=in_specs, out_specs=out_specs, check_vma=False)

time: 522 us -> 270 us (0.52)
  waiting for transfers between devices: 330 us -> 0 us
  Pallas kernels: 90.5 us -> 248 us
  local copies, waits for them, and re-layouts: 51.8 us -> 13.5 us
  other arithmetic: 19.8 us -> 6.23 us
  blocking collectives: 13.4 us -> 0 us
  between operations: 14.7 us -> 1.42 us
    pallas_call x1 -> x3, Pallas kernels: 12.8 us -> 170 us  [the longest x1 79 us: on_device(): pl.pallas_call(keys_kernel, in_specs=[anywhere] + [vmem] * 8, out_specs=[...]
    psum x3 -> x0, waiting for transfers between devices: 142 us -> none  [the longest x1 61.1 us: on_device(): mine = lax.psum(mine, 'seq').astype(F32).reshape(-1)]
    unnamed x6 -> x0, waiting for transfers between devices: 136 us -> none
    all_gather x1 -> x0, waiting for transfers between devices: 51.7 us -> none  [on_device(): packed = lax.all_gather(packed, 'dp', axis=0, tiled=True)]
    slice x12 -> x4, local copies, waits for them, and re-layouts: 22.4 us -> 6.38 us  [the longest x1 1.89 us: on_device(): att[:, 3 * D:]]
    all_gather x1 -> x0, blocking collectives: 13.4 us -> none  [on_device(): gains = lax.all_gather(gains, 'dp', axis=0, tiled=True).astype(F32)]
    unnamed x26 -> x10, local copies, waits for them, and re-layouts: 16 us -> 3.76 us
    convert_element_type x6 -> x0, other arithmetic: 11.6 us -> none  [the longest x1 3.28 us: on_device(): mine = lax.psum(mine, 'seq').astype(F32).reshape(-1)]
  transfers between devices with their start and end apart: 5 -> 0, of which waited for: 5 -> 0; matrix products, arithmetic and copies ran while one was open for 5% -> 0% of each run, Pallas kernels for 0% -> 0%
where the time goes in v2:
time: 270 us
  Pallas kernels  248 us (92%)
  local copies, waits for them, and re-layouts  13.5 us (5%)
  other arithmetic  6.23 us (2%)
    pallas_call x1, Pallas kernels, on_device(): pl.pallas_call(keys_kernel, in_specs=[anywhere] + [vmem] * 8, out_specs=[...  79 us
    pallas_call x1, Pallas kernels, on_device(): pl.pallas_call(middle_kernel, grid=(count,), in_specs=[each((length, D)),...  58.5 us
    pallas_call x1, Pallas kernels, on_device(): pl.pallas_call(scatter_kernel, in_specs=[vmem] * 4, out_specs=[vmem] * 4,...  57.9 us
    pallas_call x1, Pallas kernels, on_device(): pl.pallas_call(sums_kernel, in_specs=[vmem], out_specs=vmem, out_shape=sd...  32.7 us
    pallas_call x1, Pallas kernels, on_device(): pl.pallas_call(last_kernel, grid=(count,), in_specs=[each((length, D)), e...  20.3 us

profile of v2, /device:TPU:0, one launch (start us, length us, event | category | flops | bytes accessed | tf_op | source)
XLA Modules:
  0.0 269.5 jit_solution(17732785937025677726)
XLA Ops:
  0.6 0.0 copy-start.1
  1.3 0.3 subtract_convert_fusion
  1.7 0.7 pad_maximum_fusion.1.forms_ref.refs_5_
  2.4 0.7 convert_bitcast_fusion
  3.1 0.1 copy.29
  3.2 0.6 pad.8.gains_own
  3.8 79.0 %keys_phase.1 = (bf16[512,2048]{1,0:T(8,128)(2,1)}, bf16[512,2048]{1,0:T(8,128)(2,1)}, bf16[2048,512]{1,0:T(8,128)(2,1)}, f32[8,512]{1,0:T(8,128)}, bf16[4,512,5...) custom-call(f32[4,512,512]{2,1,0:T(8,128)} %x_ref.3, ...), custom_call_target="tpu_custom_call" | custom-call | tf_op jit(solution)/shard_map/keys_phase/pallas_call | solution.py:646
  82.8 1.4 fusion.42
  84.2 0.7 fusion.21
  84.9 0.9 maximum_maximum_fusion.refs_6_.refs_5_
  85.8 0.0 copy-done.1
  85.8 1.4 copy.31.mask_ref
  87.2 58.5 %middle_phase.1 = (f32[4,512,512]{2,1,0:T(8,128)}, f32[4,512,512]{2,1,0:T(8,128)}, bf16[4,512,512]{2,1,0:T(8,128)(2,1)}, bf16[4,4,144,256]{3,2,1,0:T(8,128)(2,1)...) custom-call(f32[4,512,512]{2,1,0:T(8,128)} %x_ref.3, ...), custom_call_target="tpu_custom_call" | custom-call | tf_op jit(solution)/shard_map/middle_phase/pallas_call | solution.py:682
  145.7 32.7 %grad_sums.1.sums_ref = bf16[4,4,144,256]{3,2,1,0:T(8,128)(2,1)} custom-call(bf16[4,4,144,256]{3,2,1,0:T(8,128)(2,1)} %get-tuple-element.41.local), custom_call_target="tpu_custom_call" | custom-call | tf_op jit(solution)/shard_map/grad_sums/pallas_call | solution.py:723
  178.4 20.3 %last_phase.1 = (f32[4,512,512]{2,1,0:T(8,128)}, f32[1,512]{1,0:T(1,128)}, f32[512,1536]{1,0:T(8,128)}) custom-call(f32[4,512,512]{2,1,0:T(8,128)} %x_ref.3, f32[4,512,512]{2,1,0:T(8,128)} %get-tuple-element.39.dmid_ref, bf16[4,512,512]{2,1,0:T(8,128)(2,1)} %get-tuple-element.40.dq_ref, bf16[4,4,144,256]{3,2,1,0:T(8,128)(2,1)} %grad_sums.1.sums_ref, ...), custom_call_target="tpu_custom_call" | custom-call | tf_op jit(solution)/shard_map/last_phase/pallas_call | solution.py:749
  198.7 0.0 copy-start
  198.7 1.8 slice.34
  200.5 1.3 slice.35
  201.8 0.0 copy-done
  201.8 0.0 copy-start.2
  201.8 0.0 copy-start.3
  201.8 2.3 pad_maximum_fusion
  204.1 0.0 copy-done.2
  204.1 0.0 copy-done.3
  204.1 0.6 select_maximum_fusion.gains_grad
  204.7 57.9 %weight_grads.1 = (f32[8,512]{1,0:T(8,128)}, f32[64,2048]{1,0:T(8,128)}, f32[64,2048]{1,0:T(8,128)}, f32[256,512]{1,0:T(8,128)}) custom-call(f32[8,512]{1,0:T(8,128)} %select_maximum_fusion.gains_grad, f32[8,64,2048]{2,1,0:T(8,128)} %bitcast.16, f32[8,64,2048]{2,1,0:T(8,128)} %bitcast.17, f32[8,512,256]{2,1,0:T(8,128)} %get-tuple-element.51.down_grad), custom_call_target="tpu_custom_call" | custom-call | tf_op jit(solution)/shard_map/weight_grads/pallas_call | solution.py:832
  262.6 1.9 fusion.41
  264.5 0.8 constant_dynamic-slice_fusion
  265.2 0.5 slice_bitcast_fusion
  265.8 1.9 copy.35
  267.6 1.9 copy.36
  (6 shorter events, 0.1 us)
Async XLA Ops:
  0.6 85.2 %copy-start.1 = (s32[4,512]{1,0:T(4,128)S(1)}, s32[4,512]{1,0:T(4,128)}, u32[]{:S(2)}) copy-start(s32[4,512]{1,0:T(4,128)} %param.14) | copy-start | bytes 24580
  198.7 3.1 %copy-start = (f32[512,512]{1,0:T(8,128)S(1)}, f32[512,512]{1,0:T(8,128)}, u32[]{:S(2)}) copy-start(f32[512,512]{1,0:T(8,128)} %get-tuple-element.49) | copy-start | bytes 3145732
  201.8 2.3 copy-start.2
  201.8 2.3 copy-start.3

commit v3 on v0

v3 whole, which is shorter than its diff:
```python
import functools
import math

import jax
import jax.numpy as jnp
from jax import lax
from jax.experimental import pallas as pl
from jax.experimental.pallas import tpu as pltpu
from jax.sharding import PartitionSpec as P

D = 512
HEADS = 8
PAIRS = 4
HEAD_DIM = 64
FEATURES = 256
FF = 2048
CHUNKS = 4
KEY, VALUE, QUERY, OUT, UP, DOWN, UNITS = 0, 1, 2, 3, 4, 8, 12

epsilon = 1e-05
LOG2E = math.log2(math.e)
LOW = jnp.bfloat16
F32 = jnp.float32
MESH = pl.DeviceIdType.MESH


def scramble(hashed):
    return jnp.bitwise_xor(hashed, lax.shift_right_logical(hashed, jnp.full_like(hashed, 16)))


def uniform_entries(counter, seed):
    hashed = counter * 1664525 + seed * 22695477 + 1013904223
    hashed = scramble(hashed) * 73244475
    hashed = scramble(hashed) * 73244475
    hashed = scramble(hashed)
    low_bits = jnp.bitwise_and(hashed, 8388607)
    return (low_bits.astype(F32) + 0.5) * (1.0 / 8388608.0)


def direction_entries(index, seed):
    radius = jnp.sqrt(-2.0 * jnp.log(uniform_entries(index, seed)))
    turn = uniform_entries(index + FEATURES * HEAD_DIM, seed)
    return radius * jnp.cos(2.0 * math.pi * turn)


def feature_forms(seed):
    col = lax.broadcasted_iota(jnp.int32, (HEAD_DIM, FEATURES), 1)
    row = lax.broadcasted_iota(jnp.int32, (HEAD_DIM, FEATURES), 0)
    dirs_t = direction_entries(col * HEAD_DIM + row, seed) * HEAD_DIM ** (-0.25)
    scaled = dirs_t * LOG2E
    high = scaled.astype(LOW)
    rest = (scaled - high.astype(F32)).astype(LOW)
    minus = jnp.full((HEAD_DIM, FEATURES), -1.0, LOW)
    forms = jnp.stack(
        [jnp.concatenate([high, high, rest, minus], axis=0), jnp.concatenate([high, high, minus, rest], axis=0)]
    )
    back = dirs_t.T.astype(LOW)
    one, zero = jnp.ones_like(back), jnp.zeros_like(back)
    back = jnp.concatenate(
        [jnp.concatenate([back, zero, one, zero], axis=1), jnp.concatenate([zero, back, zero, one], axis=1)], axis=0
    )
    return forms, back


def dot(left, right):
    return jnp.dot(left, right, preferred_element_type=F32)


def dot_nt(left, right):
    return lax.dot_general(left, right, (((1,), (1,)), ((), ())), preferred_element_type=F32)


def dot_tn(left, right):
    return lax.dot_general(left, right, (((0,), (0,)), ((), ())), preferred_element_type=F32)


def normalize(values):
    centred = values - jnp.mean(values, axis=-1, keepdims=True)
    scale = lax.rsqrt(jnp.mean(centred * centred, axis=-1, keepdims=True) + epsilon)
    return centred * scale, scale


def norm_grad(grad_normed, unit_rows, scale, gain):
    scaled_grad = grad_normed * gain
    first = jnp.mean(scaled_grad, axis=-1, keepdims=True)
    second = jnp.mean(scaled_grad * unit_rows, axis=-1, keepdims=True)
    return scale * (scaled_grad - first - unit_rows * second)


def pair_lanes(pair, base=0):
    return slice(base + pair * 128, base + pair * 128 + 128)


def head_lanes(head):
    return slice(head * 256, head * 256 + 256)


def feature_pair(rows, forms_ref):
    high = rows.astype(LOW)
    rest = (rows - high.astype(F32)).astype(LOW)
    square = (rows * rows * (LOG2E / 16.0) + 1.0 / 16.0).astype(LOW)
    h0, h1 = high[:, :64], high[:, 64:]
    r0, r1 = rest[:, :64], rest[:, 64:]
    s0, s1 = square[:, :64], square[:, 64:]
    left0 = jnp.concatenate([r0, h0, h0, s0], axis=1)
    left1 = jnp.concatenate([h1, r1, s1, h1], axis=1)
    return jnp.exp2(dot(left0, forms_ref[0])), jnp.exp2(dot(left1, forms_ref[1]))


def sums_place(parts, head):
    step = HEADS * HEAD_DIM // parts
    block = min(step, HEAD_DIM)
    runs = [divmod(head * HEAD_DIM + at, step) + (at, block) for at in range(0, HEAD_DIM, block)]
    part = head * HEAD_DIM // step
    return runs, part, step + head - -(-part * step // HEAD_DIM)


def put_sums(sums_ref, head, rows, totals):
    runs, part, row = sums_place(sums_ref.shape[0], head)
    for run_part, run_row, at, block in runs:
        sums_ref[run_part, run_row : run_row + block] = rows[at : at + block].astype(LOW)
    sums_ref[part, row : row + 1] = totals.astype(LOW)


def get_sums(sums_ref, head):
    runs, part, row = sums_place(sums_ref.shape[0], head)
    rows = [sums_ref[run_part, run_row : run_row + block] for run_part, run_row, _, block in runs]
    rows = rows[0] if len(rows) == 1 else jnp.concatenate(rows, axis=0)
    return rows, sums_ref[part, row : row + 1].astype(F32)


def spread_sums(sums_ref, spread_ref):
    for head in range(HEADS):
        own, other = (head % 2) * 64, 64 - (head % 2) * 64
        rows, totals = get_sums(sums_ref, head)
        spread_ref[head, own : own + 64] = rows
        spread_ref[head, 128 + own : 192 + own] = jnp.broadcast_to(totals, (64, 256)).astype(LOW)
        spread_ref[head, other : other + 64] = jnp.zeros((64, 256), LOW)
        spread_ref[head, 128 + other : 192 + other] = jnp.zeros((64, 256), LOW)


def spread_grads(sums_ref, spread_ref):
    for head in range(HEADS):
        own, other = (head % 2) * 64, 64 - (head % 2) * 64
        rows, totals = get_sums(sums_ref, head)
        spread_ref[head, own : own + 64] = rows
        spread_ref[head, other : other + 64] = jnp.zeros((64, 256), LOW)
        row = lax.broadcasted_iota(jnp.int32, (128, 256), 0)
        spread_ref[head, 128:] = jnp.where(row == 0, jnp.broadcast_to(totals, (128, 256)), 0.0).astype(LOW)


def keys_phase(x, gain, weights, forms_ref, state_ref, sums_ref):
    unit, _ = normalize(x)
    normed = (unit * gain).astype(LOW)
    state_ref[:, 3072:3584] = normed
    values = dot(normed, weights[VALUE]).astype(LOW)
    state_ref[:, 2560:3072] = values
    keys = dot(normed, weights[KEY])
    state_ref[:, 2048:2560] = keys.astype(LOW)
    ones = jnp.ones((16, x.shape[0]), LOW)
    for pair in range(PAIRS):
        phi = feature_pair(keys[:, pair_lanes(pair)], forms_ref)
        values_t = values[:, pair_lanes(pair)].T
        for half in range(2):
            head = 2 * pair + half
            low = phi[half].astype(LOW)
            state_ref[:, head_lanes(head)] = low
            left = jnp.concatenate([values_t[half * 64 : half * 64 + 64], ones], axis=0)
            got = dot(left, low)
            put_sums(sums_ref, head, got[:64], got[64:65])


def front_phase(x, upstream, mask, gain_one, gain_two, sums_ref, weights, forms_ref, spread_ref, state_ref, out_ref, n2_ref, dy_ref, scale_ref):
    spread_sums(sums_ref, spread_ref)
    unit, _ = normalize(x)
    queries = dot((unit * gain_one).astype(LOW), weights[QUERY])
    state_ref[:, 2048:2560] = queries.astype(LOW)
    for pair in range(PAIRS):
        phi0, phi1 = feature_pair(queries[:, pair_lanes(pair)], forms_ref)
        low0, low1 = phi0.astype(LOW), phi1.astype(LOW)
        state_ref[:, head_lanes(2 * pair)] = low0
        state_ref[:, head_lanes(2 * pair + 1)] = low1
        both = dot_nt(low0, spread_ref[2 * pair]) + dot_nt(low1, spread_ref[2 * pair + 1])
        reciprocal = 1.0 / both[:, 128:]
        state_ref[:, pair_lanes(pair, 2560)] = (both[:, :128] * reciprocal).astype(LOW)
        state_ref[:, pair_lanes(pair, 3072)] = reciprocal.astype(LOW)
    mid = x + dot(state_ref[:, 2560:3072], weights[OUT])
    unit, scale = normalize(mid)
    n2_ref[...] = (unit * gain_two).astype(LOW)
    scale_ref[...] = jnp.broadcast_to(scale, scale_ref.shape)
    out_ref[...] = mid
    lanes = mask.shape[1]
    for at in range(0, D, lanes):
        dy_ref[:, at : at + lanes] = (upstream[:, at : at + lanes] * mask).astype(LOW)


def ffn_phase(first, n2, dy, w_up, w_down, out_ref, dn2_ref, up_grad_ref, down_grad_ref):
    hidden = dot(n2, w_up)
    cumulative = 0.5 * (1.0 + lax.erf(hidden * (1.0 / math.sqrt(2.0))))
    density = jnp.exp2(hidden * hidden * (-0.5 * LOG2E)) * (1.0 / math.sqrt(2.0 * math.pi))
    act = (hidden * cumulative).astype(LOW)
    du = (dot_nt(dy, w_down) * (cumulative + hidden * density)).astype(LOW)
    out_ref[...] += dot(act, w_down)
    down_grad_ref[...] += dot_tn(act, dy)
    dn2 = dot_nt(du, w_up)
    if first:
        dn2_ref[...] = dn2
    else:
        dn2_ref[...] += dn2
    up_grad_ref[...] += dot_tn(n2, du)


def attention_grad_phase(dy, dn2, n2, scale, gain, sums_ref, weights, back_ref, state_ref, spread_ref, gain_grad_ref, w_out_grad_ref, da_ref, dq_ref, grad_sums_ref):
    spread_sums(sums_ref, spread_ref)
    unit = n2.astype(F32) * (1.0 / gain)
    gain_grad_ref[...] += jnp.sum(dn2 * unit, axis=0, keepdims=True)
    da = (dy.astype(F32) + norm_grad(dn2, unit, scale, gain)).astype(LOW)
    da_ref[...] = da
    w_out_grad_ref[...] += dot_tn(state_ref[:, 2560:3072], da)
    datt = dot_nt(da, weights[OUT])
    for pair in range(PAIRS):
        dnumer = datt[:, pair_lanes(pair)] * state_ref[:, pair_lanes(pair, 3072)].astype(F32)
        weighted = -dnumer * state_ref[:, pair_lanes(pair, 2560)].astype(F32)
        left = jnp.concatenate([dnumer.astype(LOW), weighted.astype(LOW)], axis=1)
        left_t = left.T
        parts = []
        for half in range(2):
            head, own = 2 * pair + half, half * 64
            pq = state_ref[:, head_lanes(head)]
            dden = jnp.sum(left_t[128 + own : 192 + own].astype(F32), axis=0, keepdims=True)
            rows = jnp.concatenate(
                [left_t[own : own + 64], jnp.broadcast_to(dden, (16, dden.shape[1])).astype(LOW)], axis=0
            )
            got = dot(rows, pq)
            put_sums(grad_sums_ref, head, got[:64], got[64:65])
            parts.append((dot(left, spread_ref[head]) * pq.astype(F32)).astype(LOW))
        grads = dot(parts[0], back_ref[:256]) + dot(parts[1], back_ref[256:])
        q = state_ref[:, pair_lanes(pair, 2048)].astype(F32)
        dq_ref[:, pair_lanes(pair)] = (grads[:, :128] - grads[:, 128:] * q * 0.125).astype(LOW)


def keys_grad_phase(sums_ref, back_ref, state_ref, spread_ref, dq_ref, dk_ref, dv_ref, att_grad_ref):
    spread_grads(sums_ref, spread_ref)
    ones = jnp.ones((dk_ref.shape[0], 128), LOW)
    for pair in range(PAIRS):
        left = jnp.concatenate([state_ref[:, pair_lanes(pair, 2560)], ones], axis=1)
        parts = []
        dv = None
        for half in range(2):
            head = 2 * pair + half
            pk = state_ref[:, head_lanes(head)]
            parts.append((dot(left, spread_ref[head]) * pk.astype(F32)).astype(LOW))
            piece = dot_nt(pk, spread_ref[head, :128])
            dv = piece if dv is None else dv + piece
        dv_ref[:, pair_lanes(pair)] = dv.astype(LOW)
        grads = dot(parts[0], back_ref[:256]) + dot(parts[1], back_ref[256:])
        k = state_ref[:, pair_lanes(pair, 2048)].astype(F32)
        dk_ref[:, pair_lanes(pair)] = (grads[:, :128] - grads[:, 128:] * k * 0.125).astype(LOW)
    normed = state_ref[:, 3072:3584]
    att_grad_ref[KEY] += dot_tn(normed, dk_ref[...])
    att_grad_ref[VALUE] += dot_tn(normed, dv_ref[...])
    att_grad_ref[QUERY] += dot_tn(normed, dq_ref[...])


def input_grad_phase(x, da, dq, dk, dv, gain, weights, gain_grad_ref, input_grad_ref):
    dn1 = dot_nt(dq, weights[QUERY]) + dot_nt(dk, weights[KEY]) + dot_nt(dv, weights[VALUE])
    unit, scale = normalize(x)
    gain_grad_ref[...] += jnp.sum(dn1 * unit, axis=0, keepdims=True)
    input_grad_ref[...] = da.astype(F32) + norm_grad(dn1, unit, scale, gain)


class Place:
    def __init__(self, n_dp, n_seq):
        self.n_dp, self.n_seq, self.n_z = n_dp, n_seq, n_dp // 2
        self.dp, self.seq = lax.axis_index("dp"), lax.axis_index("seq")
        self.z, self.core = self.dp // 2, lax.rem(self.dp, 2)

    def up_z(self, step):
        return lax.rem(self.z + step, self.n_z)

    def up_seq(self, step):
        return lax.rem(self.seq + step, self.n_seq)

    def down_z(self, step):
        return lax.rem(self.z + (self.n_z - step), self.n_z)

    def owner(self, z):
        return z * 2 + self.core

    def other_core(self):
        return (self.z * 2 + 1 - self.core, self.seq)

    def meet(self):
        barrier = pltpu.get_barrier_semaphore()
        for step in range(1, self.n_dp):
            other = lax.rem(self.dp + step, self.n_dp)
            pl.semaphore_signal(barrier, inc=1, device_id=(other, self.seq), device_id_type=MESH)
        for step in range(1, self.n_seq):
            pl.semaphore_signal(barrier, inc=1, device_id=(self.dp, self.up_seq(step)), device_id_type=MESH)
        pl.semaphore_wait(barrier, self.n_dp - 1 + self.n_seq - 1)


def remote(source, target, sems, at, device):
    return pltpu.make_async_remote_copy(
        src_ref=source, dst_ref=target, send_sem=sems[0].at[at], recv_sem=sems[1].at[at],
        device_id=device, device_id_type=MESH,
    )


def semaphores(*shape):
    return [pltpu.SemaphoreType.DMA(shape), pltpu.SemaphoreType.DMA(shape)]


class Gather:
    def __init__(self, place, weights, first, count, index, sems):
        self.place, self.weights, self.first, self.count, self.index = place, weights, first, count, index
        self.own = D // place.n_dp
        self.across = min(place.n_seq, D // 128)
        self.units = count // (place.n_seq // self.across)
        self.z_sems, self.plane_sems, self.core_sems = sems

    def rows(self, owner):
        return pl.ds(pl.multiple_of(owner * self.own, self.own), self.own)

    def piece(self, owner, part):
        columns = D // self.across
        first = self.first + (part // self.across) * self.units
        left = pl.multiple_of(lax.rem(part, self.across) * columns, 128)
        return self.weights.at[pl.ds(first, self.units), self.rows(owner), pl.ds(left, columns)]

    def shard(self, owner):
        return self.weights.at[pl.ds(self.first, self.count), self.rows(owner)]

    def z_copy(self, step):
        place = self.place
        piece = self.piece(place.dp, place.seq)
        return remote(piece, piece, self.z_sems, (self.index, step - 1), (place.owner(place.up_z(step)), place.seq))

    def plane_copy(self, step, to):
        place = self.place
        piece = self.piece(place.owner(place.down_z(step)), place.seq)
        return remote(piece, piece, self.plane_sems, (self.index, step - 1, to - 1), (place.dp, place.up_seq(to)))

    def core_copy(self, step):
        shard = self.shard(self.place.owner(self.place.down_z(step)))
        return remote(shard, shard, self.core_sems, (self.index, step), self.place.other_core())

    def start(self):
        for step in range(1, self.place.n_z):
            self.z_copy(step).start()
        self.core_copy(0).start()

    def to_plane(self):
        for step in range(1, self.place.n_z):
            self.z_copy(step).wait_recv()
            for to in range(1, self.place.n_seq):
                self.plane_copy(step, to).start()

    def to_core(self):
        for step in range(1, self.place.n_z):
            for to in range(1, self.place.n_seq):
                self.plane_copy(step, to).wait_recv()
            self.core_copy(step).start()

    def finish(self):
        for step in range(self.place.n_z):
            self.core_copy(step).wait_recv()

    def drain(self):
        for step in range(1, self.place.n_z):
            self.z_copy(step).wait_send()
            for to in range(1, self.place.n_seq):
                self.plane_copy(step, to).wait_send()
        for step in range(self.place.n_z):
            self.core_copy(step).wait_send()


class Sums:
    def __init__(self, place, local, arrived, full, add_sems, full_sems):
        self.place, self.local, self.arrived, self.full = place, local, arrived, full
        self.add_sems, self.full_sems = add_sems, full_sems

    def add_copy(self, slot, index, to):
        other = self.place.up_seq(to)
        return remote(
            self.local.at[slot, other], self.arrived.at[index, to - 1], self.add_sems, (index, to - 1),
            (self.place.dp, other),
        )

    def full_copy(self, index, to):
        place = self.place
        mine = self.full.at[index, place.seq]
        return remote(mine, mine, self.full_sems, (index, to - 1), (place.dp, place.up_seq(to)))

    def start(self, slot, index):
        for to in range(1, self.place.n_seq):
            self.add_copy(slot, index, to).start()

    def add(self, slot, index):
        place = self.place
        total = self.local[slot, place.seq].astype(F32)
        for to in range(1, place.n_seq):
            self.add_copy(slot, index, to).wait_recv()
            total = total + self.arrived[index, to - 1].astype(F32)
        self.full[index, place.seq] = total.astype(LOW)
        for to in range(1, place.n_seq):
            self.full_copy(index, to).start()
        for to in range(1, place.n_seq):
            self.add_copy(slot, index, to).wait_send()

    def finish(self, index):
        for to in range(1, self.place.n_seq):
            self.full_copy(index, to).wait_recv()

    def drain(self, index):
        for to in range(1, self.place.n_seq):
            self.full_copy(index, to).wait_send()


OUT_SLOTS = 4


class Scatter:
    def __init__(self, place, index, refs, kept=None):
        self.place, self.index, self.slot, self.kept = place, index, index % OUT_SLOTS, kept
        self.out, self.mine, self.arrived, self.plane, self.column, self.final = refs[:6]
        self.core_sems, self.plane_sems, self.z_sems, self.full_sems = refs[6:8], refs[8:10], refs[10:12], refs[12:14]
        self.own = D // place.n_dp
        self.across = min(place.n_seq, D // 128)
        self.lanes = D // self.across

    @staticmethod
    def shapes(n_dp, n_seq, items, held):
        own, n_z = D // n_dp, n_dp // 2
        part = (own, D // min(n_seq, D // 128))
        return [
            pltpu.VMEM((OUT_SLOTS, n_seq, n_z) + part, LOW), pltpu.VMEM((held, n_seq, n_z) + part, LOW),
            pltpu.VMEM((items, n_seq, n_z) + part, LOW), pltpu.VMEM((items, n_seq - 1, n_z) + part, LOW),
            pltpu.VMEM((items, 2 * n_z - 1) + part, LOW), pltpu.VMEM((items, n_seq) + part, LOW),
            *semaphores(items), *semaphores(items, n_seq - 1), *semaphores(items, n_z - 1), *semaphores(items, n_seq - 1),
        ]

    def block(self, grads, owner, lane_part):
        rows = pl.ds(pl.multiple_of(owner * self.own, self.own), self.own)
        return grads[rows, lane_part * self.lanes : lane_part * self.lanes + self.lanes]

    def core_copy(self):
        return remote(
            self.out.at[self.slot], self.arrived.at[self.index], self.core_sems, self.index, self.place.other_core()
        )

    def plane_copy(self, to):
        other = self.place.up_seq(to)
        return remote(
            self.arrived.at[self.index, other], self.plane.at[self.index, to - 1], self.plane_sems,
            (self.index, to - 1), (self.place.dp, other),
        )

    def z_copy(self, step):
        place = self.place
        other = place.up_z(step)
        return remote(
            self.column.at[self.index, other], self.column.at[self.index, place.n_z + step - 1], self.z_sems,
            (self.index, step - 1), (place.owner(other), place.seq),
        )

    def full_copy(self, to):
        place = self.place
        mine = self.final.at[self.index, place.seq]
        return remote(mine, mine, self.full_sems, (self.index, to - 1), (place.dp, place.up_seq(to)))

    def put(self, unit, grads):
        place = self.place
        for lane_part in range(self.across):
            part = unit * self.across + lane_part
            for z in range(place.n_z):
                self.out[self.slot, part, z] = self.block(grads, z * 2 + 1 - place.core, lane_part).astype(LOW)
                if self.kept is None:
                    self.mine[self.index, part, z] = self.block(grads, place.owner(z), lane_part).astype(LOW)

    def start(self):
        self.core_copy().start()

    def to_plane(self):
        place = self.place
        self.core_copy().wait_recv()
        for part in range(place.n_seq):
            for z in range(place.n_z):
                if self.kept is None:
                    mine = self.mine[self.index, part, z].astype(F32)
                else:
                    mine = self.block(self.kept[part // self.across], place.owner(z), part % self.across)
                self.arrived[self.index, part, z] = (mine + self.arrived[self.index, part, z].astype(F32)).astype(LOW)
        for to in range(1, place.n_seq):
            self.plane_copy(to).start()

    def to_z(self):
        place = self.place
        for to in range(1, place.n_seq):
            self.plane_copy(to).wait_recv()
        for z in range(place.n_z):
            total = self.arrived[self.index, place.seq, z].astype(F32)
            for to in range(1, place.n_seq):
                total = total + self.plane[self.index, to - 1, z].astype(F32)
            self.column[self.index, z] = total.astype(LOW)
        for step in range(1, place.n_z):
            self.z_copy(step).start()

    def to_copies(self):
        place = self.place
        total = self.column[self.index, place.z].astype(F32)
        for step in range(1, place.n_z):
            self.z_copy(step).wait_recv()
            total = total + self.column[self.index, place.n_z + step - 1].astype(F32)
        self.final[self.index, place.seq] = total.astype(LOW)
        for to in range(1, place.n_seq):
            self.full_copy(to).start()

    def finish(self):
        for to in range(1, self.place.n_seq):
            self.full_copy(to).wait_recv()

    def result(self, unit):
        parts = [self.final[self.index, unit * self.across + at] for at in range(self.across)]
        return jnp.concatenate(parts, axis=1).astype(F32)

    def drain(self, core=True):
        place = self.place
        if core:
            self.core_copy().wait_send()
        for to in range(1, place.n_seq):
            self.plane_copy(to).wait_send()
            self.full_copy(to).wait_send()
        for step in range(1, place.n_z):
            self.z_copy(step).wait_send()


STATE = 2048 + 3 * D


def layer_kernel(
    sizes, x_hbm, cot_hbm, mask_ref, gains_own, wq, wk, wv, wo, wu, wd, forms_ref, back_ref,
    out_hbm, grad_hbm, gain_grads_ref, att_ref, up_ref, down_ref, state_hbm,
    weights, gain_buf, gains, att_grad, up_grad, down_grad, gain_sums, gain_mail,
    local, arrived, full, state, spread, n2_buf, dy_buf, da_buf, dq_buf, out_buf, pool, scale_buf,
    x_sems, cot_sems, write_sems, read_sems, out_sems, grad_sems, *rest,
):
    n_dp, n_seq = sizes
    count = x_hbm.shape[0]
    own = D // n_dp
    place = Place(n_dp, n_seq)
    group = max(1, n_seq // (D // 128))
    gather_sems = (rest[0:2], rest[2:4], rest[4:6])
    gain_sems, mail_sems = rest[6:8], rest[8:10]
    sums_refs = (place, local, arrived, full, rest[10:12], rest[12:14])
    scatter_refs = rest[14:]

    my_rows = pl.ds(pl.multiple_of(place.dp * own, own), own)

    def x_copy(step):
        slot = lax.rem(step, 2)
        return pltpu.make_async_copy(x_hbm.at[lax.rem(step, count)], pool.at[slot], x_sems.at[slot])

    def cot_copy(index):
        slot = lax.rem(index, 2)
        return pltpu.make_async_copy(cot_hbm.at[index], pool.at[2 + slot], cot_sems.at[slot])

    def write_copy(step):
        slot = lax.rem(step, 2)
        return pltpu.make_async_copy(state.at[slot], state_hbm.at[step], write_sems.at[slot])

    def read_copy(event):
        slot = lax.rem(event, 2)
        return pltpu.make_async_copy(
            state_hbm.at[lax.rem(count + event, 2 * count)], state.at[slot], read_sems.at[slot]
        )

    def out_copy(index):
        return pltpu.make_async_copy(out_buf.at[index], out_hbm.at[index], out_sems.at[index])

    def grad_copy(index):
        slot = lax.rem(index, 2)
        return pltpu.make_async_copy(pool.at[2 + slot], grad_hbm.at[index], grad_sems.at[slot])

    x_copy(0).start()
    cot_copy(0).start()
    for unit, ref in ((KEY, wk), (VALUE, wv), (QUERY, wq), (OUT, wo)):
        weights[unit, my_rows] = ref[...].astype(LOW)
    for chunk in range(CHUNKS):
        columns = [wu[:, (r * CHUNKS + chunk) * own : (r * CHUNKS + chunk + 1) * own] for r in range(n_dp)]
        weights[UP + chunk, my_rows] = jnp.concatenate(columns, axis=1).astype(LOW)
        weights[DOWN + chunk, my_rows] = wd[chunk * own : chunk * own + own].astype(LOW)
    gain_buf[my_rows] = gains_own[...]
    place.meet()

    runs = [(KEY, 2), (QUERY, 2), (UP, 4), (DOWN, 4)] if group == 1 else [(KEY, 4), (UP, 4), (DOWN, 4)]
    gathers = [Gather(place, weights, first, units, at, gather_sems) for at, (first, units) in enumerate(runs)]

    def gain_copy(step):
        mine = gain_buf.at[my_rows]
        other = lax.rem(place.dp + step, n_dp)
        return remote(mine, mine, gain_sems, step - 1, (other, place.seq))

    for step in range(1, n_dp):
        gain_copy(step).start()
    for item in gathers:
        item.start()
    gathers[0].to_plane()
    gathers[0].to_core()
    att_grad[...] = jnp.zeros_like(att_grad)
    gain_sums[...] = jnp.zeros_like(gain_sums)
    for step in range(1, n_dp):
        gain_copy(step).wait_recv()
    gains[...] = gain_buf[...].astype(F32).T[:8]
    gathers[0].finish()
    for item in gathers[1:]:
        item.to_plane()
    att_gathers, up_gather, down_gather = gathers[1:-2], gathers[-2], gathers[-1]

    sums = Sums(*sums_refs)

    def keys_step(index, carry):
        slot = lax.rem(index, 2)
        x_copy(index + 1).start()

        @pl.when(index >= 2)
        def _():
            write_copy(index - 2).wait()

        x_copy(index).wait()
        keys_phase(pool[slot], gains[0:1], weights, forms_ref, state.at[slot], local.at[slot])
        sums.start(slot, index)
        write_copy(index).start()

        @pl.when(index > 0)
        def _():
            sums.add(1 - slot, index - 1)

        return carry

    lax.fori_loop(0, count, keys_step, 0)
    for item in att_gathers:
        item.to_core()
    for item in att_gathers:
        item.finish()

    def front_step(index, carry):
        step = count + index
        slot = lax.rem(step, 2)

        @pl.when(index + 1 < count)
        def _():
            x_copy(step + 1).start()
            cot_copy(index + 1).start()

        write_copy(step - 2).wait()
        x_copy(step).wait()
        cot_copy(index).wait()
        sums.finish(index)
        mask = jnp.broadcast_to(mask_ref[pl.ds(index, 1)].astype(F32), (128, mask_ref.shape[1])).T
        front_phase(
            pool[slot], pool[2 + lax.rem(index, 2)], mask, gains[0:1], gains[1:2], full.at[index], weights, forms_ref,
            spread, state.at[slot], out_buf.at[index], n2_buf.at[index], dy_buf.at[index], scale_buf.at[index],
        )
        write_copy(step).start()

        @pl.when(index == 0)
        def _():
            sums.add((count - 1) % 2, count - 1)

        @pl.when(index == 1)
        def _():
            up_gather.to_core()

        @pl.when(index == 2)
        def _():
            down_gather.to_core()

        return carry

    lax.fori_loop(0, count, front_step, 0)
    up_gather.finish()
    down_gather.finish()
    for step in (2 * count - 2, 2 * count - 1):
        write_copy(step).wait()
    read_copy(0).start()
    read_copy(1).start()

    n_ffn = 2 * CHUNKS // group
    ffn_items = [Scatter(place, at, scatter_refs) for at in range(n_ffn)]
    if group == 1:
        items = ffn_items + [
            Scatter(place, n_ffn + at, scatter_refs, [att_grad.at[unit]])
            for at, unit in enumerate((OUT, KEY, VALUE, QUERY))
        ]
        early, late = [(items[n_ffn], [OUT])], [(items[n_ffn + 1 + at], [unit]) for at, unit in enumerate((KEY, VALUE, QUERY))]
    else:
        whole = Scatter(place, n_ffn, scatter_refs, [att_grad.at[unit] for unit in range(4)])
        items = ffn_items + [whole]
        early, late = [], [(whole, [KEY, VALUE, QUERY, OUT])]

    def put(item, unit, grads):
        if unit == 0 and item.index >= OUT_SLOTS:
            items[item.index - OUT_SLOTS].core_copy().wait_send()
        item.put(unit, grads)

    def whole_at(chunk):
        if chunk < 0 or chunk >= CHUNKS or (chunk + 1) % group:
            return []
        at = (chunk + 1) // group - 1
        return ffn_items[2 * at : 2 * at + 2]

    for chunk in range(CHUNKS):
        up_grad[...] = jnp.zeros_like(up_grad)
        down_grad[...] = jnp.zeros_like(down_grad)

        def ffn_step(index, carry, chunk=chunk):
            ffn_phase(
                chunk == 0, n2_buf[index], dy_buf[index], weights[UP + chunk], weights[DOWN + chunk], out_buf.at[index],
                pool.at[index], up_grad, down_grad,
            )
            if chunk == CHUNKS - 1:
                out_copy(index).start()

            @pl.when(index == 0)
            def _():
                for item in whole_at(chunk - 1):
                    item.to_plane()

            @pl.when(index == 1)
            def _():
                for item in whole_at(chunk - 2):
                    item.to_copies()

            @pl.when(index == count - 1)
            def _():
                for item in whole_at(chunk - 1):
                    item.to_z()

            return carry

        lax.fori_loop(0, count, ffn_step, 0)
        pair = ffn_items[2 * (chunk // group) : 2 * (chunk // group) + 2]
        put(pair[0], chunk % group, up_grad)
        put(pair[1], chunk % group, down_grad)
        for item in whole_at(chunk):
            item.start()

    grad_sums = Sums(place, local, arrived.at[pl.ds(count, count)], full.at[pl.ds(count, count)], rest[10:12], rest[12:14])
    grad_sums.add_sems = [ref.at[pl.ds(count, count)] for ref in rest[10:12]]
    grad_sums.full_sems = [ref.at[pl.ds(count, count)] for ref in rest[12:14]]

    def attention_step(index, carry):
        slot = lax.rem(index, 2)
        read_copy(index).wait()
        attention_grad_phase(
            dy_buf[index], pool[index], n2_buf[index], scale_buf[index][:, :1], gains[1:2], full.at[index], weights,
            back_ref, state.at[slot], spread, gain_sums.at[1:2], att_grad.at[OUT], da_buf.at[index],
            dq_buf.at[index], local.at[slot],
        )
        grad_sums.start(slot, index)
        read_copy(index + 2).start()

        @pl.when(index > 0)
        def _():
            grad_sums.add(1 - slot, index - 1)

        @pl.when(index == 0)
        def _():
            for item in whole_at(CHUNKS - 1):
                item.to_plane()
            for item in whole_at(CHUNKS - 2):
                item.to_copies()

        @pl.when(index == 2)
        def _():
            for item in whole_at(CHUNKS - 1):
                item.to_z()

        @pl.when(index == count - 1)
        def _():
            for item in whole_at(CHUNKS - 1):
                item.to_copies()

        return carry

    lax.fori_loop(0, count, attention_step, 0)
    for item, units in early:
        for at, unit in enumerate(units):
            put(item, at, att_grad.at[unit])
        item.start()
    x_copy(0).start()

    dk_buf, dv_buf = n2_buf, dy_buf

    def keys_grad_step(index, carry):
        event = count + index
        slot = lax.rem(event, 2)
        read_copy(event).wait()
        grad_sums.finish(index)
        keys_grad_phase(
            full.at[count + index], back_ref, state.at[slot], spread, dq_buf.at[index], dk_buf.at[index],
            dv_buf.at[index], att_grad,
        )

        @pl.when(index + 2 < count)
        def _():
            read_copy(event + 2).start()

        @pl.when(index == 0)
        def _():
            grad_sums.add((count - 1) % 2, count - 1)
            for item, _ in early:
                item.to_plane()

        @pl.when(index == 2)
        def _():
            for item, _ in early:
                item.to_z()

        return carry

    lax.fori_loop(0, count, keys_grad_step, 0)
    for item, units in late:
        for at, unit in enumerate(units):
            put(item, at, att_grad.at[unit])
        item.start()

    def input_grad_step(index, carry):
        slot = lax.rem(index, 2)

        @pl.when(index + 1 < count)
        def _():
            x_copy(index + 1).start()

        x_copy(index).wait()

        @pl.when(index >= 2)
        def _():
            grad_copy(index - 2).wait()

        input_grad_phase(
            pool[slot], da_buf[index], dq_buf[index], dk_buf[index], dv_buf[index], gains[0:1], weights,
            gain_sums.at[0:1], pool.at[2 + slot],
        )
        grad_copy(index).start()

        @pl.when(index == 0)
        def _():
            for item, _ in late:
                item.to_plane()
            for item, _ in early:
                item.to_copies()

        return carry

    lax.fori_loop(0, count, input_grad_step, 0)

    def mail_plane(step):
        mine = gain_mail.at[place.seq]
        return remote(mine, mine, mail_sems, step - 1, (place.dp, place.up_seq(step)))

    def mail_dp(step):
        mine = gain_mail.at[n_seq + place.dp]
        other = lax.rem(place.dp + step, n_dp)
        return remote(mine, mine, mail_sems, n_seq - 2 + step, (other, place.seq))

    gain_mail[place.seq] = gain_sums[...]
    for step in range(1, n_seq):
        mail_plane(step).start()
    for item, _ in late:
        item.to_z()
    for step in range(1, n_seq):
        mail_plane(step).wait_recv()
    total = gain_mail[0]
    for at in range(1, n_seq):
        total = total + gain_mail[at]
    gain_mail[n_seq + place.dp] = total
    for step in range(1, n_dp):
        mail_dp(step).start()
    for item, _ in late:
        item.to_copies()

    def ffn_results(at):
        return [ffn_items[2 * (chunk // group) + at].result(chunk % group) for chunk in range(CHUNKS)]

    for item in ffn_items:
        item.finish()
    up_rows = ffn_results(0)
    for r in range(n_dp):
        columns = [rows[:, r * own : r * own + own] for rows in up_rows]
        up_ref[:, r * CHUNKS * own : (r + 1) * CHUNKS * own] = jnp.concatenate(columns, axis=1)
    for chunk, rows in enumerate(ffn_results(1)):
        down_ref[chunk * own : chunk * own + own] = rows
    for step in range(1, n_dp):
        mail_dp(step).wait_recv()
    total = gain_mail[n_seq]
    for at in range(1, n_dp):
        total = total + gain_mail[n_seq + at]
    gain_grads_ref[...] = total
    for item, units in early + late:
        item.finish()
        for at, unit in enumerate(units):
            att_ref[unit] = item.result(at)

    for item in items:
        item.drain(core=item.index + OUT_SLOTS >= len(items))
    for step in range(1, n_seq):
        mail_plane(step).wait_send()
    for step in range(1, n_dp):
        mail_dp(step).wait_send()
        gain_copy(step).wait_send()
    for item in gathers:
        item.drain()
    for index in range(count):
        sums.drain(index)
        grad_sums.drain(index)
        out_copy(index).wait()
    for index in (count - 2, count - 1):
        grad_copy(index).wait()


def on_device(sizes, inputs, cotangent, masked, proj_seed, gain_attn, w_query, w_key, w_value, w_out, gain_ffn, w_up, w_down):
    n_dp, n_seq = sizes
    count, length = inputs.shape[0], inputs.shape[1]
    own, own_ff = D // n_dp, FF // n_dp
    group = max(1, n_seq // (D // 128))
    n_gathers = 4 if group == 1 else 3
    n_ffn = 2 * CHUNKS // group
    n_items = n_ffn + 4 // group
    part_rows = HEADS * HEAD_DIM // n_seq + 16
    forms, back = feature_forms(proj_seed[0])
    gains = jnp.pad(jnp.stack([gain_attn, gain_ffn], axis=1).astype(LOW), ((0, 0), (0, 126)))
    sd = jax.ShapeDtypeStruct
    vmem = pl.BlockSpec(memory_space=pltpu.VMEM)
    anywhere = pl.BlockSpec(memory_space=pl.ANY)
    outputs, input_grad, gain_grads, att, up, down, _ = pl.pallas_call(
        functools.partial(layer_kernel, sizes),
        in_specs=[anywhere, anywhere] + [vmem] * 10,
        out_specs=[anywhere, anywhere] + [vmem] * 4 + [anywhere],
        out_shape=[
            sd((count, length, D), F32), sd((count, length, D), F32), sd((8, D), F32), sd((4, own, D), F32),
            sd((own, FF), F32), sd((own_ff, D), F32), sd((2 * count, length, STATE), LOW),
        ],
        scratch_shapes=[
            pltpu.VMEM((UNITS, D, D), LOW), pltpu.VMEM((D, 128), LOW), pltpu.VMEM((8, D), F32),
            pltpu.VMEM((4, D, D), F32), pltpu.VMEM((D, D), F32), pltpu.VMEM((D, D), F32),
            pltpu.VMEM((8, D), F32), pltpu.VMEM((n_seq + n_dp, 8, D), F32),
            pltpu.VMEM((2, n_seq, part_rows, 256), LOW), pltpu.VMEM((2 * count, n_seq - 1, part_rows, 256), LOW),
            pltpu.VMEM((2 * count, n_seq, part_rows, 256), LOW),
            pltpu.VMEM((2, length, STATE), LOW), pltpu.VMEM((HEADS, 256, 256), LOW),
            pltpu.VMEM((count, length, D), LOW), pltpu.VMEM((count, length, D), LOW),
            pltpu.VMEM((count, length, D), LOW), pltpu.VMEM((count, length, D), LOW),
            pltpu.VMEM((count, length, D), F32), pltpu.VMEM((max(count, 4), length, D), F32),
            pltpu.VMEM((count, length, 128), F32),
            *[pltpu.SemaphoreType.DMA((2,)) for _ in range(4)],
            pltpu.SemaphoreType.DMA((count,)), pltpu.SemaphoreType.DMA((2,)),
            *semaphores(n_gathers, n_dp // 2 - 1), *semaphores(n_gathers, n_dp // 2 - 1, n_seq - 1),
            *semaphores(n_gathers, n_dp // 2),
            *semaphores(n_dp - 1), *semaphores(n_seq + n_dp - 2),
            *semaphores(2 * count, n_seq - 1), *semaphores(2 * count, n_seq - 1),
            *Scatter.shapes(n_dp, n_seq, n_items, n_ffn),
        ],
        compiler_params=pltpu.CompilerParams(
            vmem_limit_bytes=63 * 2**20, collective_id=0, has_side_effects=True
        ),
        name="layer",
    )(inputs, cotangent, masked, gains, w_query, w_key, w_value, w_out, w_up, w_down, forms, back)
    gain_grads = lax.dynamic_slice(gain_grads, (0, lax.axis_index("dp") * own), (2, own))
    return (
        outputs, input_grad, gain_grads[0], att[QUERY], att[KEY], att[VALUE], att[OUT], gain_grads[1], up, down,
    )


def solution(mesh):
    in_specs = (
        P("dp", "seq", None),
        P("dp", "seq", None),
        P("dp", "seq"),
        P(),
        P("dp"),
        P("dp", None),
        P("dp", None),
        P("dp", None),
        P("dp", None),
        P("dp"),
        P("dp", None),
        P("dp", None),
    )
    out_specs = (
        P("dp", "seq", None),
        P("dp", "seq", None),
        P("dp"),
        P("dp", None),
        P("dp", None),
        P("dp", None),
        P("dp", None),
        P("dp"),
        P("dp", None),
        P("dp", None),
    )
    sizes = (mesh.shape["dp"], mesh.shape["seq"])
    return jax.shard_map(functools.partial(on_device, sizes), mesh=mesh, in_specs=in_specs, out_specs=out_specs, check_vma=False)
```

time: 746 us -> 200 us (0.27); the launches traced: 737 us -> 200 us
  matrix products: 296 us -> 0 us
  blocking collectives: 200 us -> 0 us
  Pallas kernels: 0 us -> 183 us
  waiting for transfers between devices: 134 us -> 0 us
  local copies, waits for them, and re-layouts: 49.2 us -> 12.4 us
  other arithmetic: 36.3 us -> 3.35 us
  between operations: 19.6 us -> 1.35 us
    dot_general x120 -> x0, matrix products: 296 us -> none  [the longest x104 212 us: contract(): return jnp.einsum(form, left, right, preferred_element_type=jnp.float32)]
    pallas_call x0 -> x1, Pallas kernels: none -> 183 us  [on_device(): pl.pallas_call(functools.partial(layer_kernel, sizes), in_specs=[anywhere...]
    psum x3 -> x0, blocking collectives: 103 us -> none  [the longest x1 79.1 us: micro_step(): summary, totals = lax.psum((local_summary, local_totals), 'seq')]
    reduce_scatter x6 -> x0, waiting for transfers between devices: 103 us -> none  [the longest x1 37.3 us: on_device(): lax.psum_scatter(running[7].astype(jnp.bfloat16), 'dp', scatter_dimension...]
    all_gather x4 -> x0, blocking collectives: 63.5 us -> none  [the longest x1 17.1 us: on_device(): lax.all_gather(low_query, 'dp', axis=0, tiled=True)]
    unnamed x485 -> x10, local copies, waits for them, and re-layouts: 43.3 us -> 8.43 us
    unnamed x2 -> x0, blocking collectives: 33.5 us -> none
    psum x2 -> x0, waiting for transfers between devices: 31.3 us -> none  [the longest x1 16.1 us: on_device(): lax.psum(summed_rows[1].astype(jnp.bfloat16), 'seq').astype(jnp.float32)]
  transfers between devices with their start and end apart: 10 -> 0, of which waited for: 5 -> 0; matrix products, arithmetic and copies ran while one was open for 37% -> 0% of each run, Pallas kernels for 0% -> 0%
where the time goes in v3:
time: 200 us
  Pallas kernels  183 us (92%)
  local copies, waits for them, and re-layouts  12.4 us (6%)
  other arithmetic  3.35 us (2%)
    pallas_call x1, Pallas kernels, on_device(): pl.pallas_call(functools.partial(layer_kernel, sizes), in_specs=[anywhere...  183 us
    unnamed x10, local copies, waits for them, and re-layouts  8.43 us

profile of v3, /device:TPU:0, one launch (start us, length us, event | category | flops | bytes accessed | tf_op | source)
XLA Modules:
  0.0 199.6 jit_solution(13632466820888345646)
XLA Ops:
  1.3 0.3 subtract_convert_fusion
  1.7 0.7 pad_maximum_fusion.forms_ref
  2.4 0.7 fusion.21
  3.1 0.9 maximum_maximum_fusion.back_ref
  4.0 0.7 convert_bitcast_fusion
  4.7 0.1 copy.25
  4.8 0.6 pad.4.gains_own
  5.4 182.6 %layer.1 = (f32[4,512,512]{2,1,0:T(8,128)}, f32[4,512,512]{2,1,0:T(8,128)}, f32[8,512]{1,0:T(8,128)}, f32[4,64,512]{2,1,0:T(8,128)}, f32[64,2048]{1,0:T(8,128)},...) custom-call(f32[4,512,512]{2,1,0:T(8,128)} %x_hbm.1, f32[4,512,512]{2,1,0:T(8,128)} %cot_hbm.1, s32[4,512]{1,0:T(4,128)} %mask_ref.1, ...), custom_call_target="tpu_custom_call" | custom-call | tf_op jit(solution)/shard_map/layer/pallas_call | solution.py:937
  188.0 0.8 constant_dynamic-slice_fusion
  188.8 0.5 slice_bitcast_fusion.4
  189.3 1.9 slice_bitcast_fusion
  191.2 0.0 copy-start
  191.2 4.8 %copy.32 = f32[4,512,512]{2,1,0:T(8,128)} copy(f32[4,512,512]{2,1,0:T(8,128)} %get-tuple-element.44) | data formatting | bytes 8388608
  196.0 0.0 copy-done
  196.0 0.0 copy-start.2
  196.0 0.0 copy-start.1
  196.0 2.0 %copy.33 = f32[4,512,512]{2,1,0:T(8,128)} copy(f32[4,512,512]{2,1,0:T(8,128)S(1)} %copy-done) | data formatting | bytes 8388608
  198.0 0.0 copy-done.2
  198.0 0.8 copy.34
  198.8 0.0 copy-done.1
  198.8 0.8 copy.35
  (6 shorter events, 0.1 us)
Async XLA Ops:
  191.2 4.8 %copy-start = (f32[4,512,512]{2,1,0:T(8,128)S(1)}, f32[4,512,512]{2,1,0:T(8,128)}, u32[]{:S(2)}) copy-start(f32[4,512,512]{2,1,0:T(8,128)} %get-tuple-element.45) | copy-start | bytes 12582916
  196.0 2.0 %copy-start.2 = (f32[64,2048]{1,0:T(8,128)S(1)}, f32[64,2048]{1,0:T(8,128)}, u32[]{:S(2)}) copy-start(f32[64,2048]{1,0:T(8,128)} %get-tuple-element.52) | copy-start | bytes 1572868
  196.0 2.8 %copy-start.1 = (f32[256,512]{1,0:T(8,128)S(1)}, f32[256,512]{1,0:T(8,128)}, u32[]{:S(2)}) copy-start(f32[256,512]{1,0:T(8,128)} %get-tuple-element.53) | copy-start | bytes 1572868

commit v4 on v3

--- a/solution.py
+++ b/solution.py
@@ -15,7 +15,7 @@
 FEATURES = 256
 FF = 2048
 CHUNKS = 4
-KEY, VALUE, QUERY, OUT, UP, DOWN, UNITS = 0, 1, 2, 3, 4, 8, 12
+KEY, VALUE, QUERY, OUT, UP, DOWN, UNITS = 0, 1, 2, 3, 4, 5, 12
 
 epsilon = 1e-05
 LOG2E = math.log2(math.e)
@@ -43,7 +43,7 @@
     return radius * jnp.cos(2.0 * math.pi * turn)
 
 
-def feature_forms(seed):
+def feature_forms(seed, forms_ref, back_ref):
     col = lax.broadcasted_iota(jnp.int32, (HEAD_DIM, FEATURES), 1)
     row = lax.broadcasted_iota(jnp.int32, (HEAD_DIM, FEATURES), 0)
     dirs_t = direction_entries(col * HEAD_DIM + row, seed) * HEAD_DIM ** (-0.25)
@@ -51,15 +51,13 @@
     high = scaled.astype(LOW)
     rest = (scaled - high.astype(F32)).astype(LOW)
     minus = jnp.full((HEAD_DIM, FEATURES), -1.0, LOW)
-    forms = jnp.stack(
-        [jnp.concatenate([high, high, rest, minus], axis=0), jnp.concatenate([high, high, minus, rest], axis=0)]
-    )
-    back = dirs_t.T.astype(LOW)
-    one, zero = jnp.ones_like(back), jnp.zeros_like(back)
-    back = jnp.concatenate(
-        [jnp.concatenate([back, zero, one, zero], axis=1), jnp.concatenate([zero, back, zero, one], axis=1)], axis=0
-    )
-    return forms, back
+    for half, pieces in enumerate(((high, high, rest, minus), (high, high, minus, rest))):
+        for at, piece in enumerate(pieces):
+            forms_ref[half, at * HEAD_DIM : at * HEAD_DIM + HEAD_DIM] = piece
+    one, zero = jnp.ones((FEATURES, HEAD_DIM), F32), jnp.zeros((FEATURES, HEAD_DIM), F32)
+    back = dirs_t.T
+    back_ref[:FEATURES] = jnp.concatenate([back, zero, one, zero], axis=1).astype(LOW)
+    back_ref[FEATURES:] = jnp.concatenate([zero, back, zero, one], axis=1).astype(LOW)
 
 
 def dot(left, right):
@@ -170,16 +168,21 @@
             put_sums(sums_ref, head, got[:64], got[64:65])
 
 
-def front_phase(x, upstream, mask, gain_one, gain_two, sums_ref, weights, forms_ref, spread_ref, state_ref, out_ref, n2_ref, dy_ref, scale_ref):
-    spread_sums(sums_ref, spread_ref)
+def front_phase(x, upstream, mask, gain_one, gain_two, sums_arrive, sums_ref, weights, forms_ref, spread_ref, state_ref, out_ref, n2_ref, dy_ref, scale_ref):
     unit, _ = normalize(x)
     queries = dot((unit * gain_one).astype(LOW), weights[QUERY])
     state_ref[:, 2048:2560] = queries.astype(LOW)
     for pair in range(PAIRS):
         phi0, phi1 = feature_pair(queries[:, pair_lanes(pair)], forms_ref)
-        low0, low1 = phi0.astype(LOW), phi1.astype(LOW)
-        state_ref[:, head_lanes(2 * pair)] = low0
-        state_ref[:, head_lanes(2 * pair + 1)] = low1
+        state_ref[:, head_lanes(2 * pair)] = phi0.astype(LOW)
+        state_ref[:, head_lanes(2 * pair + 1)] = phi1.astype(LOW)
+    lanes = mask.shape[1]
+    for at in range(0, D, lanes):
+        dy_ref[:, at : at + lanes] = (upstream[:, at : at + lanes] * mask).astype(LOW)
+    sums_arrive()
+    spread_sums(sums_ref, spread_ref)
+    for pair in range(PAIRS):
+        low0, low1 = state_ref[:, head_lanes(2 * pair)], state_ref[:, head_lanes(2 * pair + 1)]
         both = dot_nt(low0, spread_ref[2 * pair]) + dot_nt(low1, spread_ref[2 * pair + 1])
         reciprocal = 1.0 / both[:, 128:]
         state_ref[:, pair_lanes(pair, 2560)] = (both[:, :128] * reciprocal).astype(LOW)
@@ -189,18 +192,18 @@
     n2_ref[...] = (unit * gain_two).astype(LOW)
     scale_ref[...] = jnp.broadcast_to(scale, scale_ref.shape)
     out_ref[...] = mid
-    lanes = mask.shape[1]
-    for at in range(0, D, lanes):
-        dy_ref[:, at : at + lanes] = (upstream[:, at : at + lanes] * mask).astype(LOW)
-
-
-def ffn_phase(first, n2, dy, w_up, w_down, out_ref, dn2_ref, up_grad_ref, down_grad_ref):
+
+
+def ffn_phase(first, n2, dy, w_up, w_down, out_ref, low_out_ref, dn2_ref, up_grad_ref, down_grad_ref):
     hidden = dot(n2, w_up)
     cumulative = 0.5 * (1.0 + lax.erf(hidden * (1.0 / math.sqrt(2.0))))
     density = jnp.exp2(hidden * hidden * (-0.5 * LOG2E)) * (1.0 / math.sqrt(2.0 * math.pi))
     act = (hidden * cumulative).astype(LOW)
     du = (dot_nt(dy, w_down) * (cumulative + hidden * density)).astype(LOW)
-    out_ref[...] += dot(act, w_down)
+    if low_out_ref is None:
+        out_ref[...] += dot(act, w_down)
+    else:
+        low_out_ref[...] = (out_ref[...] + dot(act, w_down)).astype(LOW)
     down_grad_ref[...] += dot_tn(act, dy)
     dn2 = dot_nt(du, w_up)
     if first:
@@ -262,11 +265,11 @@
     att_grad_ref[QUERY] += dot_tn(normed, dq_ref[...])
 
 
-def input_grad_phase(x, da, dq, dk, dv, gain, weights, gain_grad_ref, input_grad_ref):
+def input_grad_phase(x, da_ref, dq, dk, dv, gain, weights, gain_grad_ref):
     dn1 = dot_nt(dq, weights[QUERY]) + dot_nt(dk, weights[KEY]) + dot_nt(dv, weights[VALUE])
     unit, scale = normalize(x)
     gain_grad_ref[...] += jnp.sum(dn1 * unit, axis=0, keepdims=True)
-    input_grad_ref[...] = da.astype(F32) + norm_grad(dn1, unit, scale, gain)
+    da_ref[...] = (da_ref[...].astype(F32) + norm_grad(dn1, unit, scale, gain)).astype(LOW)
 
 
 class Place:
@@ -290,14 +293,16 @@
     def other_core(self):
         return (self.z * 2 + 1 - self.core, self.seq)
 
-    def meet(self):
+    def arrive(self):
         barrier = pltpu.get_barrier_semaphore()
         for step in range(1, self.n_dp):
             other = lax.rem(self.dp + step, self.n_dp)
             pl.semaphore_signal(barrier, inc=1, device_id=(other, self.seq), device_id_type=MESH)
         for step in range(1, self.n_seq):
             pl.semaphore_signal(barrier, inc=1, device_id=(self.dp, self.up_seq(step)), device_id_type=MESH)
-        pl.semaphore_wait(barrier, self.n_dp - 1 + self.n_seq - 1)
+
+    def meet(self):
+        pl.semaphore_wait(pltpu.get_barrier_semaphore(), self.n_dp - 1 + self.n_seq - 1)
 
 
 def remote(source, target, sems, at, device):
@@ -312,8 +317,9 @@
 
 
 class Gather:
-    def __init__(self, place, weights, first, count, index, sems):
+    def __init__(self, place, weights, first, count, index, sems, line=False):
         self.place, self.weights, self.first, self.count, self.index = place, weights, first, count, index
+        self.line = line
         self.own = D // place.n_dp
         self.across = min(place.n_seq, D // 128)
         self.units = count // (place.n_seq // self.across)
@@ -333,7 +339,7 @@
 
     def z_copy(self, step):
         place = self.place
-        piece = self.piece(place.dp, place.seq)
+        piece = self.shard(place.dp) if self.line else self.piece(place.dp, place.seq)
         return remote(piece, piece, self.z_sems, (self.index, step - 1), (place.owner(place.up_z(step)), place.seq))
 
     def plane_copy(self, step, to):
@@ -358,8 +364,11 @@
 
     def to_core(self):
         for step in range(1, self.place.n_z):
-            for to in range(1, self.place.n_seq):
-                self.plane_copy(step, to).wait_recv()
+            if self.line:
+                self.z_copy(step).wait_recv()
+            else:
+                for to in range(1, self.place.n_seq):
+                    self.plane_copy(step, to).wait_recv()
             self.core_copy(step).start()
 
     def finish(self):
@@ -369,8 +378,9 @@
     def drain(self):
         for step in range(1, self.place.n_z):
             self.z_copy(step).wait_send()
-            for to in range(1, self.place.n_seq):
-                self.plane_copy(step, to).wait_send()
+            if not self.line:
+                for to in range(1, self.place.n_seq):
+                    self.plane_copy(step, to).wait_send()
         for step in range(self.place.n_z):
             self.core_copy(step).wait_send()
 
@@ -421,13 +431,15 @@
 
 
 class Scatter:
-    def __init__(self, place, index, refs, kept=None):
+    def __init__(self, place, index, refs, kept=None, z_first=False):
         self.place, self.index, self.slot, self.kept = place, index, index % OUT_SLOTS, kept
-        self.out, self.mine, self.arrived, self.plane, self.column, self.final = refs[:6]
+        self.z_first = z_first
+        self.out, self.mine, self.arrived, self.first, self.second, self.final = refs[:6]
         self.core_sems, self.plane_sems, self.z_sems, self.full_sems = refs[6:8], refs[8:10], refs[10:12], refs[12:14]
         self.own = D // place.n_dp
         self.across = min(place.n_seq, D // 128)
         self.lanes = D // self.across
+        self.n_first, self.n_second = (place.n_z, place.n_seq) if z_first else (place.n_seq, place.n_z)
 
     @staticmethod
     def shapes(n_dp, n_seq, items, held):
@@ -435,8 +447,9 @@
         part = (own, D // min(n_seq, D // 128))
         return [
             pltpu.VMEM((OUT_SLOTS, n_seq, n_z) + part, LOW), pltpu.VMEM((held, n_seq, n_z) + part, LOW),
-            pltpu.VMEM((items, n_seq, n_z) + part, LOW), pltpu.VMEM((items, n_seq - 1, n_z) + part, LOW),
-            pltpu.VMEM((items, 2 * n_z - 1) + part, LOW), pltpu.VMEM((items, n_seq) + part, LOW),
+            pltpu.VMEM((items, n_seq, n_z) + part, LOW),
+            pltpu.VMEM((items, max((n_seq - 1) * n_z, (n_z - 1) * n_seq)) + part, LOW),
+            pltpu.VMEM((items, 2 * max(n_z, n_seq) - 1) + part, LOW), pltpu.VMEM((items, n_seq) + part, LOW),
             *semaphores(items), *semaphores(items, n_seq - 1), *semaphores(items, n_z - 1), *semaphores(items, n_seq - 1),
         ]
 
@@ -449,19 +462,27 @@
             self.out.at[self.slot], self.arrived.at[self.index], self.core_sems, self.index, self.place.other_core()
         )
 
-    def plane_copy(self, to):
-        other = self.place.up_seq(to)
-        return remote(
-            self.arrived.at[self.index, other], self.plane.at[self.index, to - 1], self.plane_sems,
-            (self.index, to - 1), (self.place.dp, other),
-        )
-
-    def z_copy(self, step):
-        place = self.place
-        other = place.up_z(step)
-        return remote(
-            self.column.at[self.index, other], self.column.at[self.index, place.n_z + step - 1], self.z_sems,
-            (self.index, step - 1), (place.owner(other), place.seq),
+    def axis_copy(self, along_z, step, source, target):
+        place = self.place
+        if along_z:
+            return remote(
+                source, target, self.z_sems, (self.index, step - 1), (place.owner(place.up_z(step)), place.seq)
+            )
+        return remote(source, target, self.plane_sems, (self.index, step - 1), (place.dp, place.up_seq(step)))
+
+    def first_copy(self, step):
+        place = self.place
+        arrived = self.arrived.at[self.index]
+        source = arrived.at[:, place.up_z(step)] if self.z_first else arrived.at[place.up_seq(step)]
+        target = self.first.at[self.index, pl.ds((step - 1) * self.n_second, self.n_second)]
+        return self.axis_copy(self.z_first, step, source, target)
+
+    def second_copy(self, step):
+        place = self.place
+        other = place.up_seq(step) if self.z_first else place.up_z(step)
+        return self.axis_copy(
+            not self.z_first, step, self.second.at[self.index, other],
+            self.second.at[self.index, self.n_second + step - 1],
         )
 
     def full_copy(self, to):
@@ -481,7 +502,7 @@
     def start(self):
         self.core_copy().start()
 
-    def to_plane(self):
+    def to_first(self):
         place = self.place
         self.core_copy().wait_recv()
         for part in range(place.n_seq):
@@ -491,27 +512,28 @@
                 else:
                     mine = self.block(self.kept[part // self.across], place.owner(z), part % self.across)
                 self.arrived[self.index, part, z] = (mine + self.arrived[self.index, part, z].astype(F32)).astype(LOW)
-        for to in range(1, place.n_seq):
-            self.plane_copy(to).start()
-
-    def to_z(self):
-        place = self.place
-        for to in range(1, place.n_seq):
-            self.plane_copy(to).wait_recv()
-        for z in range(place.n_z):
-            total = self.arrived[self.index, place.seq, z].astype(F32)
-            for to in range(1, place.n_seq):
-                total = total + self.plane[self.index, to - 1, z].astype(F32)
-            self.column[self.index, z] = total.astype(LOW)
-        for step in range(1, place.n_z):
-            self.z_copy(step).start()
+        for step in range(1, self.n_first):
+            self.first_copy(step).start()
+
+    def to_second(self):
+        place = self.place
+        for step in range(1, self.n_first):
+            self.first_copy(step).wait_recv()
+        for at in range(self.n_second):
+            total = self.arrived[self.index, at, place.z] if self.z_first else self.arrived[self.index, place.seq, at]
+            total = total.astype(F32)
+            for step in range(1, self.n_first):
+                total = total + self.first[self.index, (step - 1) * self.n_second + at].astype(F32)
+            self.second[self.index, at] = total.astype(LOW)
+        for step in range(1, self.n_second):
+            self.second_copy(step).start()
 
     def to_copies(self):
         place = self.place
-        total = self.column[self.index, place.z].astype(F32)
-        for step in range(1, place.n_z):
-            self.z_copy(step).wait_recv()
-            total = total + self.column[self.index, place.n_z + step - 1].astype(F32)
+        total = self.second[self.index, place.seq if self.z_first else place.z].astype(F32)
+        for step in range(1, self.n_second):
+            self.second_copy(step).wait_recv()
+            total = total + self.second[self.index, self.n_second + step - 1].astype(F32)
         self.final[self.index, place.seq] = total.astype(LOW)
         for to in range(1, place.n_seq):
             self.full_copy(to).start()
@@ -522,28 +544,28 @@
 
     def result(self, unit):
         parts = [self.final[self.index, unit * self.across + at] for at in range(self.across)]
-        return jnp.concatenate(parts, axis=1).astype(F32)
+        return jnp.concatenate(parts, axis=1)
 
     def drain(self, core=True):
-        place = self.place
         if core:
             self.core_copy().wait_send()
-        for to in range(1, place.n_seq):
-            self.plane_copy(to).wait_send()
+        for step in range(1, self.n_first):
+            self.first_copy(step).wait_send()
+        for step in range(1, self.n_second):
+            self.second_copy(step).wait_send()
+        for to in range(1, self.place.n_seq):
             self.full_copy(to).wait_send()
-        for step in range(1, place.n_z):
-            self.z_copy(step).wait_send()
 
 
 STATE = 2048 + 3 * D
 
 
 def layer_kernel(
-    sizes, x_hbm, cot_hbm, mask_ref, gains_own, wq, wk, wv, wo, wu, wd, forms_ref, back_ref,
-    out_hbm, grad_hbm, gain_grads_ref, att_ref, up_ref, down_ref, state_hbm,
+    sizes, x_hbm, cot_hbm, mask_ref, gains_own, wq, wk, wv, wo, wu, wd, seed_ref,
+    out_hbm, grad_hbm, gain_grads_ref, dwk, dwv, dwq, dwo, up_ref, down_ref, state_hbm,
     weights, gain_buf, gains, att_grad, up_grad, down_grad, gain_sums, gain_mail,
     local, arrived, full, state, spread, n2_buf, dy_buf, da_buf, dq_buf, out_buf, pool, scale_buf,
-    x_sems, cot_sems, write_sems, read_sems, out_sems, grad_sems, *rest,
+    forms_ref, back_ref, x_sems, cot_sems, write_sems, read_sems, out_sems, grad_sems, *rest,
 ):
     n_dp, n_seq = sizes
     count = x_hbm.shape[0]
@@ -576,25 +598,30 @@
         )
 
     def out_copy(index):
-        return pltpu.make_async_copy(out_buf.at[index], out_hbm.at[index], out_sems.at[index])
+        return pltpu.make_async_copy(da_buf.at[index], out_hbm.at[index], out_sems.at[index])
 
     def grad_copy(index):
-        slot = lax.rem(index, 2)
-        return pltpu.make_async_copy(pool.at[2 + slot], grad_hbm.at[index], grad_sems.at[slot])
-
+        return pltpu.make_async_copy(da_buf.at[index], grad_hbm.at[index], grad_sems.at[index])
+
+    place.arrive()
     x_copy(0).start()
     cot_copy(0).start()
     for unit, ref in ((KEY, wk), (VALUE, wv), (QUERY, wq), (OUT, wo)):
         weights[unit, my_rows] = ref[...].astype(LOW)
     for chunk in range(CHUNKS):
         columns = [wu[:, (r * CHUNKS + chunk) * own : (r * CHUNKS + chunk + 1) * own] for r in range(n_dp)]
-        weights[UP + chunk, my_rows] = jnp.concatenate(columns, axis=1).astype(LOW)
-        weights[DOWN + chunk, my_rows] = wd[chunk * own : chunk * own + own].astype(LOW)
+        weights[UP + 2 * chunk, my_rows] = jnp.concatenate(columns, axis=1).astype(LOW)
+        weights[DOWN + 2 * chunk, my_rows] = wd[chunk * own : chunk * own + own].astype(LOW)
     gain_buf[my_rows] = gains_own[...]
     place.meet()
 
-    runs = [(KEY, 2), (QUERY, 2), (UP, 4), (DOWN, 4)] if group == 1 else [(KEY, 4), (UP, 4), (DOWN, 4)]
-    gathers = [Gather(place, weights, first, units, at, gather_sems) for at, (first, units) in enumerate(runs)]
+    runs = [(KEY, 2), (QUERY, 2)] if group == 1 else [(KEY, 4)]
+    gathers = [Gather(place, weights, first, units, at, gather_sems, line=at > 0) for at, (first, units) in enumerate(runs)]
+    keys_gathers, att_gathers = gathers[:1], gathers[1:]
+    ffn_gathers = [
+        Gather(place, weights, UP + 2 * chunk, 2, len(runs) + chunk, gather_sems, line=True) for chunk in range(CHUNKS)
+    ]
+    gathers = gathers + ffn_gathers
 
     def gain_copy(step):
         mine = gain_buf.at[my_rows]
@@ -603,19 +630,22 @@
 
     for step in range(1, n_dp):
         gain_copy(step).start()
-    for item in gathers:
+    for item in keys_gathers:
         item.start()
+    feature_forms(seed_ref[0], forms_ref, back_ref)
     gathers[0].to_plane()
-    gathers[0].to_core()
     att_grad[...] = jnp.zeros_like(att_grad)
     gain_sums[...] = jnp.zeros_like(gain_sums)
+    for item in keys_gathers[1:]:
+        item.to_core()
+    for item in att_gathers + ffn_gathers[:1]:
+        item.start()
+    gathers[0].to_core()
     for step in range(1, n_dp):
         gain_copy(step).wait_recv()
     gains[...] = gain_buf[...].astype(F32).T[:8]
-    gathers[0].finish()
-    for item in gathers[1:]:
-        item.to_plane()
-    att_gathers, up_gather, down_gather = gathers[1:-2], gathers[-2], gathers[-1]
+    for item in keys_gathers:
+        item.finish()
 
     sums = Sums(*sums_refs)
 
@@ -636,11 +666,15 @@
         def _():
             sums.add(1 - slot, index - 1)
 
+        @pl.when(index == 2)
+        def _():
+            for item in att_gathers:
+                item.to_core()
+            ffn_gathers[1].start()
+
         return carry
 
     lax.fori_loop(0, count, keys_step, 0)
-    for item in att_gathers:
-        item.to_core()
     for item in att_gathers:
         item.finish()
 
@@ -656,41 +690,44 @@
         write_copy(step - 2).wait()
         x_copy(step).wait()
         cot_copy(index).wait()
-        sums.finish(index)
+
+        def sums_arrive():
+            @pl.when(index == 0)
+            def _():
+                sums.add((count - 1) % 2, count - 1)
+
+            sums.finish(index)
+
         mask = jnp.broadcast_to(mask_ref[pl.ds(index, 1)].astype(F32), (128, mask_ref.shape[1])).T
         front_phase(
-            pool[slot], pool[2 + lax.rem(index, 2)], mask, gains[0:1], gains[1:2], full.at[index], weights, forms_ref,
+            pool[slot], pool[2 + lax.rem(index, 2)], mask, gains[0:1], gains[1:2], sums_arrive, full.at[index], weights, forms_ref,
             spread, state.at[slot], out_buf.at[index], n2_buf.at[index], dy_buf.at[index], scale_buf.at[index],
         )
         write_copy(step).start()
 
-        @pl.when(index == 0)
-        def _():
-            sums.add((count - 1) % 2, count - 1)
-
         @pl.when(index == 1)
         def _():
-            up_gather.to_core()
-
-        @pl.when(index == 2)
-        def _():
-            down_gather.to_core()
+            ffn_gathers[0].to_core()
+            ffn_gathers[2].start()
+
+        @pl.when(index == count - 1)
+        def _():
+            ffn_gathers[1].to_core()
+            ffn_gathers[3].start()
 
         return carry
 
     lax.fori_loop(0, count, front_step, 0)
-    up_gather.finish()
-    down_gather.finish()
     for step in (2 * count - 2, 2 * count - 1):
         write_copy(step).wait()
     read_copy(0).start()
     read_copy(1).start()
 
     n_ffn = 2 * CHUNKS // group
-    ffn_items = [Scatter(place, at, scatter_refs) for at in range(n_ffn)]
+    ffn_items = [Scatter(place, at, scatter_refs, z_first=at >= n_ffn - 2) for at in range(n_ffn)]
     if group == 1:
         items = ffn_items + [
-            Scatter(place, n_ffn + at, scatter_refs, [att_grad.at[unit]])
+            Scatter(place, n_ffn + at, scatter_refs, [att_grad.at[unit]], z_first=at < 2)
             for at, unit in enumerate((OUT, KEY, VALUE, QUERY))
         ]
         early, late = [(items[n_ffn], [OUT])], [(items[n_ffn + 1 + at], [unit]) for at, unit in enumerate((KEY, VALUE, QUERY))]
@@ -711,13 +748,14 @@
         return ffn_items[2 * at : 2 * at + 2]
 
     for chunk in range(CHUNKS):
+        ffn_gathers[chunk].finish()
         up_grad[...] = jnp.zeros_like(up_grad)
         down_grad[...] = jnp.zeros_like(down_grad)
 
         def ffn_step(index, carry, chunk=chunk):
             ffn_phase(
-                chunk == 0, n2_buf[index], dy_buf[index], weights[UP + chunk], weights[DOWN + chunk], out_buf.at[index],
-                pool.at[index], up_grad, down_grad,
+                chunk == 0, n2_buf[index], dy_buf[index], weights[UP + 2 * chunk], weights[DOWN + 2 * chunk],
+                out_buf.at[index], da_buf.at[index] if chunk == CHUNKS - 1 else None, pool.at[index], up_grad, down_grad,
             )
             if chunk == CHUNKS - 1:
                 out_copy(index).start()
@@ -725,17 +763,16 @@
             @pl.when(index == 0)
             def _():
                 for item in whole_at(chunk - 1):
-                    item.to_plane()
-
-            @pl.when(index == 1)
+                    item.to_first()
+                for item in whole_at(chunk - 2):
+                    item.to_second()
+
+            @pl.when(index == count - 1)
             def _():
                 for item in whole_at(chunk - 2):
                     item.to_copies()
-
-            @pl.when(index == count - 1)
-            def _():
-                for item in whole_at(chunk - 1):
-                    item.to_z()
+                if chunk < 2:
+                    ffn_gathers[chunk + 2].to_core()
 
             return carry
 
@@ -753,6 +790,7 @@
     def attention_step(index, carry):
         slot = lax.rem(index, 2)
         read_copy(index).wait()
+        out_copy(index).wait()
         attention_grad_phase(
             dy_buf[index], pool[index], n2_buf[index], scale_buf[index][:, :1], gains[1:2], full.at[index], weights,
             back_ref, state.at[slot], spread, gain_sums.at[1:2], att_grad.at[OUT], da_buf.at[index],
@@ -768,19 +806,19 @@
         @pl.when(index == 0)
         def _():
             for item in whole_at(CHUNKS - 1):
-                item.to_plane()
+                item.to_first()
+
+        @pl.when(index == 1)
+        def _():
+            for item in whole_at(CHUNKS - 2):
+                item.to_second()
+
+        @pl.when(index == count - 1)
+        def _():
             for item in whole_at(CHUNKS - 2):
                 item.to_copies()
-
-        @pl.when(index == 2)
-        def _():
             for item in whole_at(CHUNKS - 1):
-                item.to_z()
-
-        @pl.when(index == count - 1)
-        def _():
-            for item in whole_at(CHUNKS - 1):
-                item.to_copies()
+                item.to_second()
 
         return carry
 
@@ -811,12 +849,17 @@
         def _():
             grad_sums.add((count - 1) % 2, count - 1)
             for item, _ in early:
-                item.to_plane()
+                item.to_first()
 
         @pl.when(index == 2)
         def _():
+            for item in whole_at(CHUNKS - 1):
+                item.to_copies()
+
+        @pl.when(index == count - 1)
+        def _():
             for item, _ in early:
-                item.to_z()
+                item.to_second()
 
         return carry
 
@@ -835,22 +878,22 @@
 
         x_copy(index).wait()
 
-        @pl.when(index >= 2)
-        def _():
-            grad_copy(index - 2).wait()
-
         input_grad_phase(
-            pool[slot], da_buf[index], dq_buf[index], dk_buf[index], dv_buf[index], gains[0:1], weights,
-            gain_sums.at[0:1], pool.at[2 + slot],
+            pool[slot], da_buf.at[index], dq_buf[index], dk_buf[index], dv_buf[index], gains[0:1], weights,
+            gain_sums.at[0:1],
         )
         grad_copy(index).start()
 
         @pl.when(index == 0)
         def _():
             for item, _ in late:
-                item.to_plane()
+                item.to_first()
+
+        @pl.when(index == 1)
+        def _():
             for item, _ in early:
                 item.to_copies()
+
 
         return carry
 
@@ -869,7 +912,9 @@
     for step in range(1, n_seq):
         mail_plane(step).start()
     for item, _ in late:
-        item.to_z()
+        item.to_second()
+    for item, _ in late:
+        item.to_copies()
     for step in range(1, n_seq):
         mail_plane(step).wait_recv()
     total = gain_mail[0]
@@ -878,8 +923,6 @@
     gain_mail[n_seq + place.dp] = total
     for step in range(1, n_dp):
         mail_dp(step).start()
-    for item, _ in late:
-        item.to_copies()
 
     def ffn_results(at):
         return [ffn_items[2 * (chunk // group) + at].result(chunk % group) for chunk in range(CHUNKS)]
@@ -897,11 +940,14 @@
     total = gain_mail[n_seq]
     for at in range(1, n_dp):
         total = total + gain_mail[n_seq + at]
-    gain_grads_ref[...] = total
+    own_gains = jnp.zeros((8, own), F32)
+    for r in range(n_dp):
+        own_gains = jnp.where(place.dp == r, total[:, r * own : r * own + own], own_gains)
+    gain_grads_ref[...] = own_gains
     for item, units in early + late:
         item.finish()
         for at, unit in enumerate(units):
-            att_ref[unit] = item.result(at)
+            (dwk, dwv, dwq, dwo)[unit][...] = item.result(at)
 
     for item in items:
         item.drain(core=item.index + OUT_SLOTS >= len(items))
@@ -915,8 +961,6 @@
     for index in range(count):
         sums.drain(index)
         grad_sums.drain(index)
-        out_copy(index).wait()
-    for index in (count - 2, count - 1):
         grad_copy(index).wait()
 
 
@@ -925,22 +969,21 @@
     count, length = inputs.shape[0], inputs.shape[1]
     own, own_ff = D // n_dp, FF // n_dp
     group = max(1, n_seq // (D // 128))
-    n_gathers = 4 if group == 1 else 3
+    n_gathers = CHUNKS + (2 if group == 1 else 1)
     n_ffn = 2 * CHUNKS // group
     n_items = n_ffn + 4 // group
     part_rows = HEADS * HEAD_DIM // n_seq + 16
-    forms, back = feature_forms(proj_seed[0])
     gains = jnp.pad(jnp.stack([gain_attn, gain_ffn], axis=1).astype(LOW), ((0, 0), (0, 126)))
     sd = jax.ShapeDtypeStruct
     vmem = pl.BlockSpec(memory_space=pltpu.VMEM)
     anywhere = pl.BlockSpec(memory_space=pl.ANY)
-    outputs, input_grad, gain_grads, att, up, down, _ = pl.pallas_call(
+    outputs, input_grad, gain_grads, dwk, dwv, dwq, dwo, up, down, _ = pl.pallas_call(
         functools.partial(layer_kernel, sizes),
-        in_specs=[anywhere, anywhere] + [vmem] * 10,
-        out_specs=[anywhere, anywhere] + [vmem] * 4 + [anywhere],
+        in_specs=[anywhere, anywhere] + [vmem] * 8 + [pl.BlockSpec(memory_space=pltpu.SMEM)],
+        out_specs=[anywhere, anywhere] + [vmem] * 7 + [anywhere],
         out_shape=[
-            sd((count, length, D), F32), sd((count, length, D), F32), sd((8, D), F32), sd((4, own, D), F32),
-            sd((own, FF), F32), sd((own_ff, D), F32), sd((2 * count, length, STATE), LOW),
+            sd((count, length, D), LOW), sd((count, length, D), LOW), sd((8, own), F32), *[sd((own, D), LOW)] * 4,
+            sd((own, FF), LOW), sd((own_ff, D), LOW), sd((2 * count, length, STATE), LOW),
         ],
         scratch_shapes=[
             pltpu.VMEM((UNITS, D, D), LOW), pltpu.VMEM((D, 128), LOW), pltpu.VMEM((8, D), F32),
@@ -953,8 +996,9 @@
             pltpu.VMEM((count, length, D), LOW), pltpu.VMEM((count, length, D), LOW),
             pltpu.VMEM((count, length, D), F32), pltpu.VMEM((max(count, 4), length, D), F32),
             pltpu.VMEM((count, length, 128), F32),
+            pltpu.VMEM((2, 256, 256), LOW), pltpu.VMEM((512, 256), LOW),
             *[pltpu.SemaphoreType.DMA((2,)) for _ in range(4)],
-            pltpu.SemaphoreType.DMA((count,)), pltpu.SemaphoreType.DMA((2,)),
+            pltpu.SemaphoreType.DMA((count,)), pltpu.SemaphoreType.DMA((count,)),
             *semaphores(n_gathers, n_dp // 2 - 1), *semaphores(n_gathers, n_dp // 2 - 1, n_seq - 1),
             *semaphores(n_gathers, n_dp // 2),
             *semaphores(n_dp - 1), *semaphores(n_seq + n_dp - 2),
@@ -965,10 +1009,38 @@
             vmem_limit_bytes=63 * 2**20, collective_id=0, has_side_effects=True
         ),
         name="layer",
-    )(inputs, cotangent, masked, gains, w_query, w_key, w_value, w_out, w_up, w_down, forms, back)
-    gain_grads = lax.dynamic_slice(gain_grads, (0, lax.axis_index("dp") * own), (2, own))
+    )(inputs, cotangent, masked, gains, w_query, w_key, w_value, w_out, w_up, w_down, proj_seed)
+    grains = 2
+    block = pl.BlockSpec((None, length // grains, D), lambda i: (i // grains, lax.rem(i, grains), 0))
+    small = [(own, D)] * 4 + [(own, FF), (own_ff, D)]
+
+    def fixed(shape):
+        return pl.BlockSpec(shape, lambda i: (0, 0))
+
+    def widen(out_ref, grad_ref, gains_ref, *refs):
+        wide_out, wide_grad, gain_one, gain_two = refs[len(small) : len(small) + 4]
+        wide_out[...] = out_ref[...].astype(F32)
+        wide_grad[...] = grad_ref[...].astype(F32)
+
+        @pl.when(pl.program_id(0) == 0)
+        def _():
+            gain_one[...] = gains_ref[0:1]
+            gain_two[...] = gains_ref[1:2]
+            for low_ref, wide_ref in zip(refs[: len(small)], refs[len(small) + 4 :]):
+                wide_ref[...] = low_ref[...].astype(F32)
+
+    outputs, input_grad, gain_one, gain_two, dwk, dwv, dwq, dwo, up, down = pl.pallas_call(
+        widen,
+        grid=(count * grains,),
+        in_specs=[block, block, fixed((8, own))] + [fixed(shape) for shape in small],
+        out_specs=[block, block, fixed((1, own)), fixed((1, own))] + [fixed(shape) for shape in small],
+        out_shape=[sd((count, length, D), F32), sd((count, length, D), F32), sd((1, own), F32), sd((1, own), F32)]
+        + [sd(shape, F32) for shape in small],
+        compiler_params=pltpu.CompilerParams(vmem_limit_bytes=63 * 2**20),
+        name="widen",
+    )(outputs, input_grad, gain_grads, dwk, dwv, dwq, dwo, up, down)
     return (
-        outputs, input_grad, gain_grads[0], att[QUERY], att[KEY], att[VALUE], att[OUT], gain_grads[1], up, down,
+        outputs, input_grad, gain_one.reshape(own), dwq, dwk, dwv, dwo, gain_two.reshape(own), up, down,
     )
 
 

time: 200 us -> 164 us (0.82)
  Pallas kernels: 183 us -> 161 us
  local copies, waits for them, and re-layouts: 12.4 us -> 0.73 us
  other arithmetic: 3.35 us -> 0.69 us
    pallas_call x1, Pallas kernels: 183 us -> 153 us  [on_device(): pl.pallas_call(functools.partial(layer_kernel, sizes), in_specs=[anywhere...]
    unnamed x10 -> x0, local copies, waits for them, and re-layouts: 8.43 us -> none
    pallas_call x0 -> x1, Pallas kernels: none -> 8.19 us  [on_device(): pl.pallas_call(widen, grid=(count * grains,), in_specs=[block, block, fix...]
    squeeze x2 -> x0, local copies, waits for them, and re-layouts: 2.41 us -> none  [the longest x1 1.89 us: on_device(): att[OUT]]
where the time goes in v4:
time: 164 us
  Pallas kernels  161 us (98%)
    pallas_call x1, Pallas kernels, on_device(): pl.pallas_call(functools.partial(layer_kernel, sizes), in_specs=[anywhere...  153 us
    pallas_call x1, Pallas kernels, on_device(): pl.pallas_call(widen, grid=(count * grains,), in_specs=[block, block, fix...  8.19 us

profile of v4, /device:TPU:0, one launch (start us, length us, event | category | flops | bytes accessed | tf_op | source)
XLA Modules:
  0.0 164.1 jit_solution(15720712060409750472)
XLA Ops:
  1.3 0.7 convert_bitcast_fusion
  2.0 0.1 copy.24
  2.1 0.6 pad.4.gains_own
  2.7 153.0 %layer.1 = (bf16[4,512,512]{2,1,0:T(8,128)(2,1)}, bf16[4,512,512]{2,1,0:T(8,128)(2,1)}, f32[8,64]{1,0:T(8,128)}, bf16[64,512]{1,0:T(8,128)(2,1)}, bf16[64,512]{1...) custom-call(f32[4,512,512]{2,1,0:T(8,128)} %x_hbm.1, ...), custom_call_target="tpu_custom_call" | custom-call | tf_op jit(solution)/shard_map/layer/pallas_call | solution.py:980
  155.7 8.2 %widen.1 = (f32[4,512,512]{2,1,0:T(8,128)}, f32[4,512,512]{2,1,0:T(8,128)}, f32[1,64]{1,0:T(1,128)}, f32[1,64]{1,0:T(1,128)}, f32[64,512]{1,0:T(8,128)}, /*index...) custom-call(bf16[4,512,512]{2,1,0:T(8,128)(2,1)} %get-tuple-element.29.out_r, ...), custom_call_target="tpu_custom_call" | custom-call | tf_op jit(solution)/shard_map/widen/pallas_call | solution.py:1032
  (1 shorter events, 0.0 us)

commit v5 on v4

--- a/solution.py
+++ b/solution.py
@@ -85,6 +85,10 @@
     return scale * (scaled_grad - first - unit_rows * second)
 
 
+def unit_of(weights, unit):
+    return weights[unit].reshape(D, D)
+
+
 def pair_lanes(pair, base=0):
     return slice(base + pair * 128, base + pair * 128 + 128)
 
@@ -151,9 +155,9 @@
     unit, _ = normalize(x)
     normed = (unit * gain).astype(LOW)
     state_ref[:, 3072:3584] = normed
-    values = dot(normed, weights[VALUE]).astype(LOW)
+    values = dot(normed, unit_of(weights, VALUE)).astype(LOW)
     state_ref[:, 2560:3072] = values
-    keys = dot(normed, weights[KEY])
+    keys = dot(normed, unit_of(weights, KEY))
     state_ref[:, 2048:2560] = keys.astype(LOW)
     ones = jnp.ones((16, x.shape[0]), LOW)
     for pair in range(PAIRS):
@@ -170,7 +174,7 @@
 
 def front_phase(x, upstream, mask, gain_one, gain_two, sums_arrive, sums_ref, weights, forms_ref, spread_ref, state_ref, out_ref, n2_ref, dy_ref, scale_ref):
     unit, _ = normalize(x)
-    queries = dot((unit * gain_one).astype(LOW), weights[QUERY])
+    queries = dot((unit * gain_one).astype(LOW), unit_of(weights, QUERY))
     state_ref[:, 2048:2560] = queries.astype(LOW)
     for pair in range(PAIRS):
         phi0, phi1 = feature_pair(queries[:, pair_lanes(pair)], forms_ref)
@@ -187,7 +191,7 @@
         reciprocal = 1.0 / both[:, 128:]
         state_ref[:, pair_lanes(pair, 2560)] = (both[:, :128] * reciprocal).astype(LOW)
         state_ref[:, pair_lanes(pair, 3072)] = reciprocal.astype(LOW)
-    mid = x + dot(state_ref[:, 2560:3072], weights[OUT])
+    mid = x + dot(state_ref[:, 2560:3072], unit_of(weights, OUT))
     unit, scale = normalize(mid)
     n2_ref[...] = (unit * gain_two).astype(LOW)
     scale_ref[...] = jnp.broadcast_to(scale, scale_ref.shape)
@@ -220,7 +224,7 @@
     da = (dy.astype(F32) + norm_grad(dn2, unit, scale, gain)).astype(LOW)
     da_ref[...] = da
     w_out_grad_ref[...] += dot_tn(state_ref[:, 2560:3072], da)
-    datt = dot_nt(da, weights[OUT])
+    datt = dot_nt(da, unit_of(weights, OUT))
     for pair in range(PAIRS):
         dnumer = datt[:, pair_lanes(pair)] * state_ref[:, pair_lanes(pair, 3072)].astype(F32)
         weighted = -dnumer * state_ref[:, pair_lanes(pair, 2560)].astype(F32)
@@ -266,7 +270,7 @@
 
 
 def input_grad_phase(x, da_ref, dq, dk, dv, gain, weights, gain_grad_ref):
-    dn1 = dot_nt(dq, weights[QUERY]) + dot_nt(dk, weights[KEY]) + dot_nt(dv, weights[VALUE])
+    dn1 = dot_nt(dq, unit_of(weights, QUERY)) + dot_nt(dk, unit_of(weights, KEY)) + dot_nt(dv, unit_of(weights, VALUE))
     unit, scale = normalize(x)
     gain_grad_ref[...] += jnp.sum(dn1 * unit, axis=0, keepdims=True)
     da_ref[...] = (da_ref[...].astype(F32) + norm_grad(dn1, unit, scale, gain)).astype(LOW)
@@ -325,36 +329,32 @@
         self.units = count // (place.n_seq // self.across)
         self.z_sems, self.plane_sems, self.core_sems = sems
 
-    def rows(self, owner):
-        return pl.ds(pl.multiple_of(owner * self.own, self.own), self.own)
-
-    def piece(self, owner, part):
+    def piece(self, z, part):
         columns = D // self.across
         first = self.first + (part // self.across) * self.units
         left = pl.multiple_of(lax.rem(part, self.across) * columns, 128)
-        return self.weights.at[pl.ds(first, self.units), self.rows(owner), pl.ds(left, columns)]
-
-    def shard(self, owner):
-        return self.weights.at[pl.ds(self.first, self.count), self.rows(owner)]
+        return self.weights.at[pl.ds(first, self.units), z, self.place.core, :, pl.ds(left, columns)]
+
+    def shard(self, z):
+        return self.weights.at[pl.ds(self.first, self.count), z, self.place.core]
 
     def z_copy(self, step):
         place = self.place
-        piece = self.shard(place.dp) if self.line else self.piece(place.dp, place.seq)
+        piece = self.shard(place.z) if self.line else self.piece(place.z, place.seq)
         return remote(piece, piece, self.z_sems, (self.index, step - 1), (place.owner(place.up_z(step)), place.seq))
 
     def plane_copy(self, step, to):
         place = self.place
-        piece = self.piece(place.owner(place.down_z(step)), place.seq)
+        piece = self.piece(place.down_z(step), place.seq)
         return remote(piece, piece, self.plane_sems, (self.index, step - 1, to - 1), (place.dp, place.up_seq(to)))
 
-    def core_copy(self, step):
-        shard = self.shard(self.place.owner(self.place.down_z(step)))
-        return remote(shard, shard, self.core_sems, (self.index, step), self.place.other_core())
+    def core_copy(self):
+        shards = self.weights.at[pl.ds(self.first, self.count), :, self.place.core]
+        return remote(shards, shards, self.core_sems, self.index, self.place.other_core())
 
     def start(self):
         for step in range(1, self.place.n_z):
             self.z_copy(step).start()
-        self.core_copy(0).start()
 
     def to_plane(self):
         for step in range(1, self.place.n_z):
@@ -369,11 +369,10 @@
             else:
                 for to in range(1, self.place.n_seq):
                     self.plane_copy(step, to).wait_recv()
-            self.core_copy(step).start()
+        self.core_copy().start()
 
     def finish(self):
-        for step in range(self.place.n_z):
-            self.core_copy(step).wait_recv()
+        self.core_copy().wait_recv()
 
     def drain(self):
         for step in range(1, self.place.n_z):
@@ -381,8 +380,7 @@
             if not self.line:
                 for to in range(1, self.place.n_seq):
                     self.plane_copy(step, to).wait_send()
-        for step in range(self.place.n_z):
-            self.core_copy(step).wait_send()
+        self.core_copy().wait_send()
 
 
 class Sums:
@@ -427,30 +425,29 @@
             self.full_copy(index, to).wait_send()
 
 
-OUT_SLOTS = 4
-
-
 class Scatter:
-    def __init__(self, place, index, refs, kept=None, z_first=False):
-        self.place, self.index, self.slot, self.kept = place, index, index % OUT_SLOTS, kept
-        self.z_first = z_first
+    REFS = 14
+
+    def __init__(self, place, refs, z_first, kept=None):
+        self.place, self.z_first, self.kept = place, z_first, kept
         self.out, self.mine, self.arrived, self.first, self.second, self.final = refs[:6]
         self.core_sems, self.plane_sems, self.z_sems, self.full_sems = refs[6:8], refs[8:10], refs[10:12], refs[12:14]
         self.own = D // place.n_dp
         self.across = min(place.n_seq, D // 128)
         self.lanes = D // self.across
+        self.units = self.out.shape[2]
         self.n_first, self.n_second = (place.n_z, place.n_seq) if z_first else (place.n_seq, place.n_z)
 
     @staticmethod
-    def shapes(n_dp, n_seq, items, held):
+    def shapes(n_dp, n_seq, units, z_first, keep):
         own, n_z = D // n_dp, n_dp // 2
-        part = (own, D // min(n_seq, D // 128))
+        part = (units, own, D // min(n_seq, D // 128))
+        n_first, n_second = (n_z, n_seq) if z_first else (n_seq, n_z)
         return [
-            pltpu.VMEM((OUT_SLOTS, n_seq, n_z) + part, LOW), pltpu.VMEM((held, n_seq, n_z) + part, LOW),
-            pltpu.VMEM((items, n_seq, n_z) + part, LOW),
-            pltpu.VMEM((items, max((n_seq - 1) * n_z, (n_z - 1) * n_seq)) + part, LOW),
-            pltpu.VMEM((items, 2 * max(n_z, n_seq) - 1) + part, LOW), pltpu.VMEM((items, n_seq) + part, LOW),
-            *semaphores(items), *semaphores(items, n_seq - 1), *semaphores(items, n_z - 1), *semaphores(items, n_seq - 1),
+            pltpu.VMEM((n_seq, n_z) + part, LOW), pltpu.VMEM((n_seq, n_z) + part if keep else (16, 128), LOW),
+            pltpu.VMEM((n_seq, n_z) + part, LOW), pltpu.VMEM(((n_first - 1) * n_second,) + part, LOW),
+            pltpu.VMEM((2 * n_second - 1,) + part, LOW), pltpu.VMEM((n_seq,) + part, LOW),
+            *semaphores(1), *semaphores(n_seq - 1), *semaphores(n_z - 1), *semaphores(n_seq - 1),
         ]
 
     def block(self, grads, owner, lane_part):
@@ -458,46 +455,38 @@
         return grads[rows, lane_part * self.lanes : lane_part * self.lanes + self.lanes]
 
     def core_copy(self):
-        return remote(
-            self.out.at[self.slot], self.arrived.at[self.index], self.core_sems, self.index, self.place.other_core()
-        )
+        return remote(self.out, self.arrived, self.core_sems, 0, self.place.other_core())
 
     def axis_copy(self, along_z, step, source, target):
         place = self.place
         if along_z:
-            return remote(
-                source, target, self.z_sems, (self.index, step - 1), (place.owner(place.up_z(step)), place.seq)
-            )
-        return remote(source, target, self.plane_sems, (self.index, step - 1), (place.dp, place.up_seq(step)))
+            return remote(source, target, self.z_sems, step - 1, (place.owner(place.up_z(step)), place.seq))
+        return remote(source, target, self.plane_sems, step - 1, (place.dp, place.up_seq(step)))
 
     def first_copy(self, step):
         place = self.place
-        arrived = self.arrived.at[self.index]
-        source = arrived.at[:, place.up_z(step)] if self.z_first else arrived.at[place.up_seq(step)]
-        target = self.first.at[self.index, pl.ds((step - 1) * self.n_second, self.n_second)]
+        source = self.arrived.at[:, place.up_z(step)] if self.z_first else self.arrived.at[place.up_seq(step)]
+        target = self.first.at[pl.ds((step - 1) * self.n_second, self.n_second)]
         return self.axis_copy(self.z_first, step, source, target)
 
     def second_copy(self, step):
         place = self.place
         other = place.up_seq(step) if self.z_first else place.up_z(step)
-        return self.axis_copy(
-            not self.z_first, step, self.second.at[self.index, other],
-            self.second.at[self.index, self.n_second + step - 1],
-        )
+        return self.axis_copy(not self.z_first, step, self.second.at[other], self.second.at[self.n_second + step - 1])
 
     def full_copy(self, to):
         place = self.place
-        mine = self.final.at[self.index, place.seq]
-        return remote(mine, mine, self.full_sems, (self.index, to - 1), (place.dp, place.up_seq(to)))
-
-    def put(self, unit, grads):
+        mine = self.final.at[place.seq]
+        return remote(mine, mine, self.full_sems, to - 1, (place.dp, place.up_seq(to)))
+
+    def put(self, unit, group, grads):
         place = self.place
         for lane_part in range(self.across):
-            part = unit * self.across + lane_part
+            part = group * self.across + lane_part
             for z in range(place.n_z):
-                self.out[self.slot, part, z] = self.block(grads, z * 2 + 1 - place.core, lane_part).astype(LOW)
+                self.out[part, z, unit] = self.block(grads, z * 2 + 1 - place.core, lane_part).astype(LOW)
                 if self.kept is None:
-                    self.mine[self.index, part, z] = self.block(grads, place.owner(z), lane_part).astype(LOW)
+                    self.mine[part, z, unit] = self.block(grads, place.owner(z), lane_part).astype(LOW)
 
     def start(self):
         self.core_copy().start()
@@ -507,11 +496,13 @@
         self.core_copy().wait_recv()
         for part in range(place.n_seq):
             for z in range(place.n_z):
-                if self.kept is None:
-                    mine = self.mine[self.index, part, z].astype(F32)
-                else:
-                    mine = self.block(self.kept[part // self.across], place.owner(z), part % self.across)
-                self.arrived[self.index, part, z] = (mine + self.arrived[self.index, part, z].astype(F32)).astype(LOW)
+                for unit in range(self.units):
+                    if self.kept is None:
+                        mine = self.mine[part, z, unit].astype(F32)
+                    else:
+                        grads = self.kept[part // self.across * self.units + unit]
+                        mine = self.block(grads, place.owner(z), part % self.across)
+                    self.arrived[part, z, unit] = (mine + self.arrived[part, z, unit].astype(F32)).astype(LOW)
         for step in range(1, self.n_first):
             self.first_copy(step).start()
 
@@ -520,21 +511,21 @@
         for step in range(1, self.n_first):
             self.first_copy(step).wait_recv()
         for at in range(self.n_second):
-            total = self.arrived[self.index, at, place.z] if self.z_first else self.arrived[self.index, place.seq, at]
+            total = self.arrived[at, place.z] if self.z_first else self.arrived[place.seq, at]
             total = total.astype(F32)
             for step in range(1, self.n_first):
-                total = total + self.first[self.index, (step - 1) * self.n_second + at].astype(F32)
-            self.second[self.index, at] = total.astype(LOW)
+                total = total + self.first[(step - 1) * self.n_second + at].astype(F32)
+            self.second[at] = total.astype(LOW)
         for step in range(1, self.n_second):
             self.second_copy(step).start()
 
     def to_copies(self):
         place = self.place
-        total = self.second[self.index, place.seq if self.z_first else place.z].astype(F32)
+        total = self.second[place.seq if self.z_first else place.z].astype(F32)
         for step in range(1, self.n_second):
             self.second_copy(step).wait_recv()
-            total = total + self.second[self.index, self.n_second + step - 1].astype(F32)
-        self.final[self.index, place.seq] = total.astype(LOW)
+            total = total + self.second[self.n_second + step - 1].astype(F32)
+        self.final[place.seq] = total.astype(LOW)
         for to in range(1, place.n_seq):
             self.full_copy(to).start()
 
@@ -542,13 +533,12 @@
         for to in range(1, self.place.n_seq):
             self.full_copy(to).wait_recv()
 
-    def result(self, unit):
-        parts = [self.final[self.index, unit * self.across + at] for at in range(self.across)]
+    def result(self, unit, group=0):
+        parts = [self.final[group * self.across + at, unit] for at in range(self.across)]
         return jnp.concatenate(parts, axis=1)
 
-    def drain(self, core=True):
-        if core:
-            self.core_copy().wait_send()
+    def drain(self):
+        self.core_copy().wait_send()
         for step in range(1, self.n_first):
             self.first_copy(step).wait_send()
         for step in range(1, self.n_second):
@@ -557,6 +547,25 @@
             self.full_copy(to).wait_send()
 
 
+UP_HALF, DOWN_HALF = 0, 1
+
+
+def scatter_plan(group):
+    def chunk(at):
+        return [(UP_HALF, at), (DOWN_HALF, at)]
+
+    if group == 1:
+        return [
+            (chunk(0) + chunk(1), False),
+            (chunk(2), True),
+            ([(UP_HALF, 3), ("att", OUT)], False),
+            ([(DOWN_HALF, 3)], True),
+            ([("att", KEY)], True),
+            ([("att", VALUE), ("att", QUERY)], False),
+        ]
+    return [([(UP_HALF, None), (DOWN_HALF, None)], False), ([("att", None)], False)]
+
+
 STATE = 2048 + 3 * D
 
 
@@ -564,7 +573,7 @@
     sizes, x_hbm, cot_hbm, mask_ref, gains_own, wq, wk, wv, wo, wu, wd, seed_ref,
     out_hbm, grad_hbm, gain_grads_ref, dwk, dwv, dwq, dwo, up_ref, down_ref, state_hbm,
     weights, gain_buf, gains, att_grad, up_grad, down_grad, gain_sums, gain_mail,
-    local, arrived, full, state, spread, n2_buf, dy_buf, da_buf, dq_buf, out_buf, pool, scale_buf,
+    local, arrived, full, state, spread, n2_buf, dy_buf, da_buf, dq_buf, out_buf, out_low, pool, scale_buf,
     forms_ref, back_ref, x_sems, cot_sems, write_sems, read_sems, out_sems, grad_sems, *rest,
 ):
     n_dp, n_seq = sizes
@@ -581,11 +590,14 @@
 
     def x_copy(step):
         slot = lax.rem(step, 2)
-        return pltpu.make_async_copy(x_hbm.at[lax.rem(step, count)], pool.at[slot], x_sems.at[slot])
+        return pltpu.make_async_copy(x_hbm.at[lax.rem(step, count)], att_grad.at[QUERY + slot], x_sems.at[slot])
+
+    def x_again(index):
+        slot = lax.rem(index, 2)
+        return pltpu.make_async_copy(x_hbm.at[index], pool.at[slot], x_sems.at[slot])
 
     def cot_copy(index):
-        slot = lax.rem(index, 2)
-        return pltpu.make_async_copy(cot_hbm.at[index], pool.at[2 + slot], cot_sems.at[slot])
+        return pltpu.make_async_copy(cot_hbm.at[index], out_buf.at[index], cot_sems.at[index])
 
     def write_copy(step):
         slot = lax.rem(step, 2)
@@ -598,25 +610,26 @@
         )
 
     def out_copy(index):
-        return pltpu.make_async_copy(da_buf.at[index], out_hbm.at[index], out_sems.at[index])
+        return pltpu.make_async_copy(out_low, out_hbm.at[index], out_sems.at[index])
 
     def grad_copy(index):
         return pltpu.make_async_copy(da_buf.at[index], grad_hbm.at[index], grad_sems.at[index])
 
     place.arrive()
     x_copy(0).start()
-    cot_copy(0).start()
+    for index in range(count):
+        cot_copy(index).start()
     for unit, ref in ((KEY, wk), (VALUE, wv), (QUERY, wq), (OUT, wo)):
-        weights[unit, my_rows] = ref[...].astype(LOW)
+        weights[unit, place.z, place.core] = ref[...].astype(LOW)
     for chunk in range(CHUNKS):
         columns = [wu[:, (r * CHUNKS + chunk) * own : (r * CHUNKS + chunk + 1) * own] for r in range(n_dp)]
-        weights[UP + 2 * chunk, my_rows] = jnp.concatenate(columns, axis=1).astype(LOW)
-        weights[DOWN + 2 * chunk, my_rows] = wd[chunk * own : chunk * own + own].astype(LOW)
+        weights[UP + 2 * chunk, place.z, place.core] = jnp.concatenate(columns, axis=1).astype(LOW)
+        weights[DOWN + 2 * chunk, place.z, place.core] = wd[chunk * own : chunk * own + own].astype(LOW)
     gain_buf[my_rows] = gains_own[...]
     place.meet()
 
     runs = [(KEY, 2), (QUERY, 2)] if group == 1 else [(KEY, 4)]
-    gathers = [Gather(place, weights, first, units, at, gather_sems, line=at > 0) for at, (first, units) in enumerate(runs)]
+    gathers = [Gather(place, weights, first, units, at, gather_sems, line=False) for at, (first, units) in enumerate(runs)]
     keys_gathers, att_gathers = gathers[:1], gathers[1:]
     ffn_gathers = [
         Gather(place, weights, UP + 2 * chunk, 2, len(runs) + chunk, gather_sems, line=True) for chunk in range(CHUNKS)
@@ -634,7 +647,6 @@
         item.start()
     feature_forms(seed_ref[0], forms_ref, back_ref)
     gathers[0].to_plane()
-    att_grad[...] = jnp.zeros_like(att_grad)
     gain_sums[...] = jnp.zeros_like(gain_sums)
     for item in keys_gathers[1:]:
         item.to_core()
@@ -646,6 +658,8 @@
     gains[...] = gain_buf[...].astype(F32).T[:8]
     for item in keys_gathers:
         item.finish()
+    for item in att_gathers:
+        item.to_plane()
 
     sums = Sums(*sums_refs)
 
@@ -658,7 +672,7 @@
             write_copy(index - 2).wait()
 
         x_copy(index).wait()
-        keys_phase(pool[slot], gains[0:1], weights, forms_ref, state.at[slot], local.at[slot])
+        keys_phase(att_grad[QUERY + slot], gains[0:1], weights, forms_ref, state.at[slot], local.at[slot])
         sums.start(slot, index)
         write_copy(index).start()
 
@@ -666,11 +680,19 @@
         def _():
             sums.add(1 - slot, index - 1)
 
+        @pl.when(index == 0)
+        def _():
+            ffn_gathers[1].start()
+
         @pl.when(index == 2)
         def _():
             for item in att_gathers:
                 item.to_core()
-            ffn_gathers[1].start()
+
+        @pl.when(index == count - 1)
+        def _():
+            ffn_gathers[0].to_core()
+            ffn_gathers[2].start()
 
         return carry
 
@@ -678,6 +700,49 @@
     for item in att_gathers:
         item.finish()
 
+    plan = scatter_plan(group)
+    items, of_unit = [], {}
+    for at, (units, z_first) in enumerate(plan):
+        kept = None
+        if all(kind == "att" for kind, _ in units):
+            kept = [att_grad.at[index] for _, index in units] if group == 1 else [att_grad.at[index] for index in range(4)]
+        item = Scatter(place, scatter_refs[at * Scatter.REFS : (at + 1) * Scatter.REFS], z_first, kept)
+        items.append(item)
+        for position, unit in enumerate(units):
+            of_unit[unit] = (item, position)
+
+    def put(kind, index, grads):
+        if group == 1:
+            item, position = of_unit[kind, index]
+            item.put(position, 0, grads)
+        else:
+            item, position = of_unit[kind, None]
+            item.put(position, index, grads)
+
+    def result(kind, index):
+        if group == 1:
+            item, position = of_unit[kind, index]
+            return item.result(position)
+        item, position = of_unit[kind, None]
+        return item.result(position, index)
+
+    def chunk_grads(chunk):
+        return (att_grad.at[KEY], att_grad.at[VALUE]) if chunk == 1 else (up_grad, down_grad)
+
+    def open_chunk(chunk):
+        for ref in chunk_grads(chunk):
+            ref[...] = jnp.zeros(ref.shape, F32)
+
+    def ffn_step(chunk, index):
+        ffn_phase(
+            chunk == 0, n2_buf[index], dy_buf[index], unit_of(weights, UP + 2 * chunk), unit_of(weights, DOWN + 2 * chunk),
+            out_buf.at[index], out_low if chunk == CHUNKS - 1 else None, pool.at[index], *chunk_grads(chunk),
+        )
+
+    def close_chunk(chunk):
+        for kind, grads in zip((UP_HALF, DOWN_HALF), chunk_grads(chunk)):
+            put(kind, chunk, grads)
+
     def front_step(index, carry):
         step = count + index
         slot = lax.rem(step, 2)
@@ -685,7 +750,6 @@
         @pl.when(index + 1 < count)
         def _():
             x_copy(step + 1).start()
-            cot_copy(index + 1).start()
 
         write_copy(step - 2).wait()
         x_copy(step).wait()
@@ -700,88 +764,75 @@
 
         mask = jnp.broadcast_to(mask_ref[pl.ds(index, 1)].astype(F32), (128, mask_ref.shape[1])).T
         front_phase(
-            pool[slot], pool[2 + lax.rem(index, 2)], mask, gains[0:1], gains[1:2], sums_arrive, full.at[index], weights, forms_ref,
-            spread, state.at[slot], out_buf.at[index], n2_buf.at[index], dy_buf.at[index], scale_buf.at[index],
+            att_grad[QUERY + slot], out_buf[index], mask, gains[0:1], gains[1:2], sums_arrive, full.at[index], weights,
+            forms_ref, spread, state.at[slot], out_buf.at[index], n2_buf.at[index], dy_buf.at[index],
+            scale_buf.at[index],
         )
         write_copy(step).start()
 
+        @pl.when(index == 0)
+        def _():
+            ffn_gathers[0].finish()
+
+        ffn_step(0, index)
+
         @pl.when(index == 1)
-        def _():
-            ffn_gathers[0].to_core()
-            ffn_gathers[2].start()
-
-        @pl.when(index == count - 1)
         def _():
             ffn_gathers[1].to_core()
             ffn_gathers[3].start()
 
         return carry
 
+    open_chunk(0)
+    open_chunk(1)
     lax.fori_loop(0, count, front_step, 0)
     for step in (2 * count - 2, 2 * count - 1):
         write_copy(step).wait()
     read_copy(0).start()
     read_copy(1).start()
-
-    n_ffn = 2 * CHUNKS // group
-    ffn_items = [Scatter(place, at, scatter_refs, z_first=at >= n_ffn - 2) for at in range(n_ffn)]
-    if group == 1:
-        items = ffn_items + [
-            Scatter(place, n_ffn + at, scatter_refs, [att_grad.at[unit]], z_first=at < 2)
-            for at, unit in enumerate((OUT, KEY, VALUE, QUERY))
-        ]
-        early, late = [(items[n_ffn], [OUT])], [(items[n_ffn + 1 + at], [unit]) for at, unit in enumerate((KEY, VALUE, QUERY))]
-    else:
-        whole = Scatter(place, n_ffn, scatter_refs, [att_grad.at[unit] for unit in range(4)])
-        items = ffn_items + [whole]
-        early, late = [], [(whole, [KEY, VALUE, QUERY, OUT])]
-
-    def put(item, unit, grads):
-        if unit == 0 and item.index >= OUT_SLOTS:
-            items[item.index - OUT_SLOTS].core_copy().wait_send()
-        item.put(unit, grads)
-
-    def whole_at(chunk):
-        if chunk < 0 or chunk >= CHUNKS or (chunk + 1) % group:
-            return []
-        at = (chunk + 1) // group - 1
-        return ffn_items[2 * at : 2 * at + 2]
-
-    for chunk in range(CHUNKS):
-        ffn_gathers[chunk].finish()
-        up_grad[...] = jnp.zeros_like(up_grad)
-        down_grad[...] = jnp.zeros_like(down_grad)
-
-        def ffn_step(index, carry, chunk=chunk):
-            ffn_phase(
-                chunk == 0, n2_buf[index], dy_buf[index], weights[UP + 2 * chunk], weights[DOWN + 2 * chunk],
-                out_buf.at[index], da_buf.at[index] if chunk == CHUNKS - 1 else None, pool.at[index], up_grad, down_grad,
-            )
-            if chunk == CHUNKS - 1:
-                out_copy(index).start()
-
-            @pl.when(index == 0)
-            def _():
-                for item in whole_at(chunk - 1):
-                    item.to_first()
-                for item in whole_at(chunk - 2):
-                    item.to_second()
-
-            @pl.when(index == count - 1)
-            def _():
-                for item in whole_at(chunk - 2):
-                    item.to_copies()
-                if chunk < 2:
-                    ffn_gathers[chunk + 2].to_core()
-
-            return carry
-
-        lax.fori_loop(0, count, ffn_step, 0)
-        pair = ffn_items[2 * (chunk // group) : 2 * (chunk // group) + 2]
-        put(pair[0], chunk % group, up_grad)
-        put(pair[1], chunk % group, down_grad)
-        for item in whole_at(chunk):
-            item.start()
+    ffn_gathers[1].finish()
+
+    def second_step(index, carry):
+        ffn_step(1, index)
+
+        @pl.when(index == 1)
+        def _():
+            ffn_gathers[2].to_core()
+
+        return carry
+
+    lax.fori_loop(0, count, second_step, 0)
+    close_chunk(0)
+    close_chunk(1)
+    first_items, third_items, last_items, late_items = (
+        (items[0:1], items[1:2], items[2:4], items[4:6]) if group == 1 else ([], [], items[:1], items[1:])
+    )
+    for item in first_items:
+        item.start()
+    att_grad[...] = jnp.zeros_like(att_grad)
+    ffn_gathers[2].finish()
+    open_chunk(2)
+
+    def third_step(index, carry):
+        ffn_step(2, index)
+
+        @pl.when(index == 1)
+        def _():
+            for item in first_items:
+                item.to_first()
+
+        @pl.when(index == 2)
+        def _():
+            ffn_gathers[3].to_core()
+
+        return carry
+
+    lax.fori_loop(0, count, third_step, 0)
+    close_chunk(2)
+    for item in third_items:
+        item.start()
+    ffn_gathers[3].finish()
+    open_chunk(3)
 
     grad_sums = Sums(place, local, arrived.at[pl.ds(count, count)], full.at[pl.ds(count, count)], rest[10:12], rest[12:14])
     grad_sums.add_sems = [ref.at[pl.ds(count, count)] for ref in rest[10:12]]
@@ -789,8 +840,14 @@
 
     def attention_step(index, carry):
         slot = lax.rem(index, 2)
+
+        @pl.when(index > 0)
+        def _():
+            out_copy(index - 1).wait()
+
+        ffn_step(CHUNKS - 1, index)
+        out_copy(index).start()
         read_copy(index).wait()
-        out_copy(index).wait()
         attention_grad_phase(
             dy_buf[index], pool[index], n2_buf[index], scale_buf[index][:, :1], gains[1:2], full.at[index], weights,
             back_ref, state.at[slot], spread, gain_sums.at[1:2], att_grad.at[OUT], da_buf.at[index],
@@ -805,29 +862,28 @@
 
         @pl.when(index == 0)
         def _():
-            for item in whole_at(CHUNKS - 1):
+            for item in third_items:
                 item.to_first()
 
-        @pl.when(index == 1)
-        def _():
-            for item in whole_at(CHUNKS - 2):
+        @pl.when(index == 2)
+        def _():
+            for item in first_items:
                 item.to_second()
 
         @pl.when(index == count - 1)
         def _():
-            for item in whole_at(CHUNKS - 2):
-                item.to_copies()
-            for item in whole_at(CHUNKS - 1):
+            for item in third_items:
                 item.to_second()
 
         return carry
 
     lax.fori_loop(0, count, attention_step, 0)
-    for item, units in early:
-        for at, unit in enumerate(units):
-            put(item, at, att_grad.at[unit])
+    close_chunk(CHUNKS - 1)
+    if group == 1:
+        put("att", OUT, att_grad.at[OUT])
+    for item in last_items:
         item.start()
-    x_copy(0).start()
+    x_again(0).start()
 
     dk_buf, dv_buf = n2_buf, dy_buf
 
@@ -848,25 +904,25 @@
         @pl.when(index == 0)
         def _():
             grad_sums.add((count - 1) % 2, count - 1)
-            for item, _ in early:
+            for item in first_items:
+                item.to_copies()
+
+        @pl.when(index == 1)
+        def _():
+            for item in last_items:
                 item.to_first()
 
         @pl.when(index == 2)
         def _():
-            for item in whole_at(CHUNKS - 1):
+            for item in third_items:
                 item.to_copies()
 
-        @pl.when(index == count - 1)
-        def _():
-            for item, _ in early:
-                item.to_second()
-
         return carry
 
     lax.fori_loop(0, count, keys_grad_step, 0)
-    for item, units in late:
-        for at, unit in enumerate(units):
-            put(item, at, att_grad.at[unit])
+    for unit in (KEY, VALUE, QUERY) + (() if group == 1 else (OUT,)):
+        put("att", unit, att_grad.at[unit])
+    for item in late_items:
         item.start()
 
     def input_grad_step(index, carry):
@@ -874,10 +930,9 @@
 
         @pl.when(index + 1 < count)
         def _():
-            x_copy(index + 1).start()
-
-        x_copy(index).wait()
-
+            x_again(index + 1).start()
+
+        x_again(index).wait()
         input_grad_phase(
             pool[slot], da_buf.at[index], dq_buf[index], dk_buf[index], dv_buf[index], gains[0:1], weights,
             gain_sums.at[0:1],
@@ -886,13 +941,13 @@
 
         @pl.when(index == 0)
         def _():
-            for item, _ in late:
+            for item in late_items:
                 item.to_first()
 
-        @pl.when(index == 1)
-        def _():
-            for item, _ in early:
-                item.to_copies()
+        @pl.when(index == 2)
+        def _():
+            for item in last_items:
+                item.to_second()
 
 
         return carry
@@ -911,9 +966,9 @@
     gain_mail[place.seq] = gain_sums[...]
     for step in range(1, n_seq):
         mail_plane(step).start()
-    for item, _ in late:
+    for item in late_items:
         item.to_second()
-    for item, _ in late:
+    for item in last_items:
         item.to_copies()
     for step in range(1, n_seq):
         mail_plane(step).wait_recv()
@@ -923,18 +978,19 @@
     gain_mail[n_seq + place.dp] = total
     for step in range(1, n_dp):
         mail_dp(step).start()
-
-    def ffn_results(at):
-        return [ffn_items[2 * (chunk // group) + at].result(chunk % group) for chunk in range(CHUNKS)]
-
-    for item in ffn_items:
+    for item in late_items:
+        item.to_copies()
+
+    for item in first_items + third_items + last_items:
         item.finish()
-    up_rows = ffn_results(0)
+    up_rows = [result(UP_HALF, chunk) for chunk in range(CHUNKS)]
     for r in range(n_dp):
         columns = [rows[:, r * own : r * own + own] for rows in up_rows]
         up_ref[:, r * CHUNKS * own : (r + 1) * CHUNKS * own] = jnp.concatenate(columns, axis=1)
-    for chunk, rows in enumerate(ffn_results(1)):
-        down_ref[chunk * own : chunk * own + own] = rows
+    for chunk in range(CHUNKS):
+        down_ref[chunk * own : chunk * own + own] = result(DOWN_HALF, chunk)
+    if group == 1:
+        dwo[...] = result("att", OUT)
     for step in range(1, n_dp):
         mail_dp(step).wait_recv()
     total = gain_mail[n_seq]
@@ -944,13 +1000,13 @@
     for r in range(n_dp):
         own_gains = jnp.where(place.dp == r, total[:, r * own : r * own + own], own_gains)
     gain_grads_ref[...] = own_gains
-    for item, units in early + late:
+    for item in late_items:
         item.finish()
-        for at, unit in enumerate(units):
-            (dwk, dwv, dwq, dwo)[unit][...] = item.result(at)
+    for unit, ref in ((KEY, dwk), (VALUE, dwv), (QUERY, dwq)) + (() if group == 1 else ((OUT, dwo),)):
+        ref[...] = result("att", unit)
 
     for item in items:
-        item.drain(core=item.index + OUT_SLOTS >= len(items))
+        item.drain()
     for step in range(1, n_seq):
         mail_plane(step).wait_send()
     for step in range(1, n_dp):
@@ -962,6 +1018,7 @@
         sums.drain(index)
         grad_sums.drain(index)
         grad_copy(index).wait()
+    out_copy(count - 1).wait()
 
 
 def on_device(sizes, inputs, cotangent, masked, proj_seed, gain_attn, w_query, w_key, w_value, w_out, gain_ffn, w_up, w_down):
@@ -970,8 +1027,10 @@
     own, own_ff = D // n_dp, FF // n_dp
     group = max(1, n_seq // (D // 128))
     n_gathers = CHUNKS + (2 if group == 1 else 1)
-    n_ffn = 2 * CHUNKS // group
-    n_items = n_ffn + 4 // group
+    scatter_scratch = []
+    for units, z_first in scatter_plan(group):
+        keep = not all(kind == "att" for kind, _ in units)
+        scatter_scratch += Scatter.shapes(n_dp, n_seq, len(units), z_first, keep)
     part_rows = HEADS * HEAD_DIM // n_seq + 16
     gains = jnp.pad(jnp.stack([gain_attn, gain_ffn], axis=1).astype(LOW), ((0, 0), (0, 126)))
     sd = jax.ShapeDtypeStruct
@@ -986,7 +1045,7 @@
             sd((own, FF), LOW), sd((own_ff, D), LOW), sd((2 * count, length, STATE), LOW),
         ],
         scratch_shapes=[
-            pltpu.VMEM((UNITS, D, D), LOW), pltpu.VMEM((D, 128), LOW), pltpu.VMEM((8, D), F32),
+            pltpu.VMEM((UNITS, n_dp // 2, 2, own, D), LOW), pltpu.VMEM((D, 128), LOW), pltpu.VMEM((8, D), F32),
             pltpu.VMEM((4, D, D), F32), pltpu.VMEM((D, D), F32), pltpu.VMEM((D, D), F32),
             pltpu.VMEM((8, D), F32), pltpu.VMEM((n_seq + n_dp, 8, D), F32),
             pltpu.VMEM((2, n_seq, part_rows, 256), LOW), pltpu.VMEM((2 * count, n_seq - 1, part_rows, 256), LOW),
@@ -994,16 +1053,17 @@
             pltpu.VMEM((2, length, STATE), LOW), pltpu.VMEM((HEADS, 256, 256), LOW),
             pltpu.VMEM((count, length, D), LOW), pltpu.VMEM((count, length, D), LOW),
             pltpu.VMEM((count, length, D), LOW), pltpu.VMEM((count, length, D), LOW),
-            pltpu.VMEM((count, length, D), F32), pltpu.VMEM((max(count, 4), length, D), F32),
+            pltpu.VMEM((count, length, D), F32), pltpu.VMEM((length, D), LOW), pltpu.VMEM((count, length, D), F32),
             pltpu.VMEM((count, length, 128), F32),
             pltpu.VMEM((2, 256, 256), LOW), pltpu.VMEM((512, 256), LOW),
-            *[pltpu.SemaphoreType.DMA((2,)) for _ in range(4)],
+            pltpu.SemaphoreType.DMA((2,)), pltpu.SemaphoreType.DMA((count,)),
+            pltpu.SemaphoreType.DMA((2,)), pltpu.SemaphoreType.DMA((2,)),
             pltpu.SemaphoreType.DMA((count,)), pltpu.SemaphoreType.DMA((count,)),
             *semaphores(n_gathers, n_dp // 2 - 1), *semaphores(n_gathers, n_dp // 2 - 1, n_seq - 1),
-            *semaphores(n_gathers, n_dp // 2),
+            *semaphores(n_gathers),
             *semaphores(n_dp - 1), *semaphores(n_seq + n_dp - 2),
             *semaphores(2 * count, n_seq - 1), *semaphores(2 * count, n_seq - 1),
-            *Scatter.shapes(n_dp, n_seq, n_items, n_ffn),
+            *scatter_scratch,
         ],
         compiler_params=pltpu.CompilerParams(
             vmem_limit_bytes=63 * 2**20, collective_id=0, has_side_effects=True

time: 164 us -> 158 us (0.963)
  Pallas kernels: 161 us -> 154 us
    pallas_call x1, Pallas kernels: 153 us -> 146 us  [on_device(): pl.pallas_call(functools.partial(layer_kernel, sizes), in_specs=[anywhere...]
where the time goes in v5:
time: 158 us; the launch traced here: 157 us
  Pallas kernels  154 us (97%)
    pallas_call x1, Pallas kernels, on_device(): pl.pallas_call(functools.partial(layer_kernel, sizes), in_specs=[anywhere...  146 us
    pallas_call x1, Pallas kernels, on_device(): pl.pallas_call(widen, grid=(count * grains,), in_specs=[block, block, fix...  8.19 us

profile of v5, /device:TPU:0, one launch (start us, length us, event | category | flops | bytes accessed | tf_op | source)
XLA Modules:
  0.0 157.4 jit_solution(11878214064177186384)
XLA Ops:
  1.3 0.7 convert_bitcast_fusion
  2.0 0.1 copy.24
  2.1 0.6 pad.4.gains_own
  2.7 146.3 %layer.1 = (bf16[4,512,512]{2,1,0:T(8,128)(2,1)}, bf16[4,512,512]{2,1,0:T(8,128)(2,1)}, f32[8,64]{1,0:T(8,128)}, bf16[64,512]{1,0:T(8,128)(2,1)}, bf16[64,512]{1...) custom-call(f32[4,512,512]{2,1,0:T(8,128)} %x_hbm.1, ...), custom_call_target="tpu_custom_call" | custom-call | tf_op jit(solution)/shard_map/layer/pallas_call | solution.py:1039
  149.0 8.2 %widen.1 = (f32[4,512,512]{2,1,0:T(8,128)}, f32[4,512,512]{2,1,0:T(8,128)}, f32[1,64]{1,0:T(1,128)}, f32[1,64]{1,0:T(1,128)}, f32[64,512]{1,0:T(8,128)}, /*index...) custom-call(bf16[4,512,512]{2,1,0:T(8,128)(2,1)} %get-tuple-element.29.out_r, ...), custom_call_target="tpu_custom_call" | custom-call | tf_op jit(solution)/shard_map/widen/pallas_call | solution.py:1092
  (1 shorter events, 0.0 us)

commit v6 on v5

--- a/solution.py
+++ b/solution.py
@@ -556,7 +556,8 @@
 
     if group == 1:
         return [
-            (chunk(0) + chunk(1), False),
+            (chunk(0), False),
+            (chunk(1), False),
             (chunk(2), True),
             ([(UP_HALF, 3), ("att", OUT)], False),
             ([(DOWN_HALF, 3)], True),
@@ -792,22 +793,30 @@
     read_copy(1).start()
     ffn_gathers[1].finish()
 
+    close_chunk(0)
+    first_items, second_items, third_items, last_items, late_items = (
+        (items[:1], items[1:2], items[2:3], items[3:5], items[5:7]) if group == 1 else ([], [], [], items[:1], items[1:])
+    )
+    for item in first_items:
+        item.start()
+
     def second_step(index, carry):
         ffn_step(1, index)
 
         @pl.when(index == 1)
         def _():
+            for item in first_items:
+                item.to_first()
+
+        @pl.when(index == 1)
+        def _():
             ffn_gathers[2].to_core()
 
         return carry
 
     lax.fori_loop(0, count, second_step, 0)
-    close_chunk(0)
     close_chunk(1)
-    first_items, third_items, last_items, late_items = (
-        (items[0:1], items[1:2], items[2:4], items[4:6]) if group == 1 else ([], [], items[:1], items[1:])
-    )
-    for item in first_items:
+    for item in second_items:
         item.start()
     att_grad[...] = jnp.zeros_like(att_grad)
     ffn_gathers[2].finish()
@@ -818,8 +827,10 @@
 
         @pl.when(index == 1)
         def _():
+            for item in second_items:
+                item.to_first()
             for item in first_items:
-                item.to_first()
+                item.to_second()
 
         @pl.when(index == 2)
         def _():
@@ -865,9 +876,14 @@
             for item in third_items:
                 item.to_first()
 
+        @pl.when(index == 1)
+        def _():
+            for item in first_items:
+                item.to_copies()
+
         @pl.when(index == 2)
         def _():
-            for item in first_items:
+            for item in second_items:
                 item.to_second()
 
         @pl.when(index == count - 1)
@@ -904,7 +920,7 @@
         @pl.when(index == 0)
         def _():
             grad_sums.add((count - 1) % 2, count - 1)
-            for item in first_items:
+            for item in second_items:
                 item.to_copies()
 
         @pl.when(index == 1)
@@ -981,7 +997,7 @@
     for item in late_items:
         item.to_copies()
 
-    for item in first_items + third_items + last_items:
+    for item in first_items + second_items + third_items + last_items:
         item.finish()
     up_rows = [result(UP_HALF, chunk) for chunk in range(CHUNKS)]
     for r in range(n_dp):

time: 158 us -> 157 us (level)
  no operation moved by 1% of the time
where the time goes in v6:
time: 157 us
  Pallas kernels  154 us (98%)
    pallas_call x1, Pallas kernels, on_device(): pl.pallas_call(functools.partial(layer_kernel, sizes), in_specs=[anywhere...  145 us
    pallas_call x1, Pallas kernels, on_device(): pl.pallas_call(widen, grid=(count * grains,), in_specs=[block, block, fix...  8.19 us

profile of v6, /device:TPU:0, one launch (start us, length us, event | category | flops | bytes accessed | tf_op | source)
XLA Modules:
  0.0 156.5 jit_solution(5367024674095629482)
XLA Ops:
  1.3 0.7 convert_bitcast_fusion
  2.0 0.1 copy.24
  2.1 0.6 pad.4.gains_own
  2.7 145.5 %layer.1 = (bf16[4,512,512]{2,1,0:T(8,128)(2,1)}, bf16[4,512,512]{2,1,0:T(8,128)(2,1)}, f32[8,64]{1,0:T(8,128)}, bf16[64,512]{1,0:T(8,128)(2,1)}, bf16[64,512]{1...) custom-call(f32[4,512,512]{2,1,0:T(8,128)} %x_hbm.1, ...), custom_call_target="tpu_custom_call" | custom-call | tf_op jit(solution)/shard_map/layer/pallas_call | solution.py:1055
  148.2 8.2 %widen.1 = (f32[4,512,512]{2,1,0:T(8,128)}, f32[4,512,512]{2,1,0:T(8,128)}, f32[1,64]{1,0:T(1,128)}, f32[1,64]{1,0:T(1,128)}, f32[64,512]{1,0:T(8,128)}, /*index...) custom-call(bf16[4,512,512]{2,1,0:T(8,128)(2,1)} %get-tuple-element.29.out_r, ...), custom_call_target="tpu_custom_call" | custom-call | tf_op jit(solution)/shard_map/widen/pallas_call | solution.py:1108
  (1 shorter events, 0.0 us)
